TPU v7x, 32 devices: a whole 2x2x4 slice. The times are simulated.
32 devices in a mesh: grp: 2 (over y), dp: 8 (over z, x), space: 2 (over core).
Axes of the slice: x: 2, y: 2, z: 4, core: 2. Of those that a mesh axis runs over, the one named last changes fastest.
Arguments:
- inputs: bfloat16 [16, 32, 64, 512], P(('grp', 'dp'), 'space'), parts along dimension 0, may hold values from -6 to 6
- cotangent: bfloat16 [16, 32, 64, 512], P(('grp', 'dp'), 'space'), parts along dimension 0, may hold values from -6 to 6
- spectral_weight: float32 [4, 128, 9, 64, 128], P(('grp', 'space'), 'dp'), parts along dimension 0, may hold values from -0.5 to 0.5
- first_moment: float32 [4, 128, 9, 64, 128], P(('grp', 'space'), 'dp'), parts along dimension 0, may hold values from -18 to 18
- second_moment: float32 [4, 128, 9, 64, 128], P(('grp', 'space'), 'dp'), parts along dimension 0, may hold values from 1 to 100
- pointwise_weight: float32 [128, 64], P('grp'), parts along dimension 0, may hold values from -0.75 to 0.75
Outputs:
- grad_input: bfloat16 [16, 32, 64, 512], P(('grp', 'dp'), 'space'), parts along dimension 0
- new_weight: float32 [4, 128, 9, 64, 128], P(('grp', 'space'), 'dp'), parts along dimension 0
- new_first: float32 [4, 128, 9, 64, 128], P(('grp', 'space'), 'dp'), parts along dimension 0
- new_second: float32 [4, 128, 9, 64, 128], P(('grp', 'space'), 'dp'), parts along dimension 0
There are 2 independent parts, one for each index of `grp`. A program takes and returns all parts, laid end to end along the dimension named above; each array names one. Nothing has to cross between parts.
All inputs are finite; a program needn't handle non-finite values.
Results may differ from a plain program's by a relative error of at most 0.001.
Values sent between devices are 32-bit elements; how exact they have to be, the bound alone decides.
No kernel may reach another device: no remote copies, remote signals or barrier semaphores. Data moves between devices by JAX's collectives and lax.ppermute only.
A program may use at most 128 MiB of HBM per device.

v0:
```python
import math

import jax
import jax.numpy as jnp
import ml_dtypes
import numpy as np
from jax import lax
from jax.experimental import pallas as pl
from jax.experimental.pallas import tpu as pltpu
from jax.sharding import PartitionSpec as P

MX = 16
MY = 16
MZ = 9
GX = 32
GY = 16
GZ = 32
HALF = MX // 2 + 1
CBLOCK = 16

beta_first = 0.9
beta_second = 0.999
learn_rate = 0.001
adam_epsilon = 1e-08
first_correct = 1.0 - math.exp(1000.0 * math.log(0.9))
second_correct = 1.0 - math.exp(1000.0 * math.log(0.999))

f32 = jnp.float32
bf16 = jnp.bfloat16


def split_np(table):
    high = table.astype(np.float32).astype(ml_dtypes.bfloat16)
    low = (table - high.astype(np.float64)).astype(np.float32).astype(ml_dtypes.bfloat16)
    return high, low


def yz_tables(groups, scaled):
    per_group = MY // groups
    y_frequency = np.concatenate([np.arange(MY // 2), np.arange(GY - MY // 2, GY)]).reshape(groups, per_group)
    y_place = np.repeat(np.arange(GY), GZ)
    z_place = np.tile(np.arange(GZ), GY)
    turns = y_frequency[:, :, None, None] * y_place / GY + np.arange(MZ)[None, None, :, None] * z_place / GZ
    angle = 2.0 * np.pi * (turns % 1.0)
    table = np.stack([np.cos(angle), -np.sin(angle)], axis=1)
    if scaled:
        table = table * (np.where(np.arange(MZ) == 0, 1.0, 2.0) / (GX * GY * GZ))[:, None]
    table = table.reshape(groups, 2 * per_group * MZ, GY * GZ)
    return np.concatenate(split_np(table), axis=1)


def x_tables(groups):
    width = GX // groups
    place = np.arange(GX).reshape(groups, 1, width)
    angle = 2.0 * np.pi * (np.arange(HALF)[None, :, None] * place % GX) / GX
    table = np.stack([np.cos(angle), -np.sin(angle)], axis=2).reshape(groups, 2 * HALF, width)
    wide = np.einsum("gkx,cd->gkcxd", table, np.eye(CBLOCK)).reshape(groups, 2 * HALF * CBLOCK, width * CBLOCK)
    high, low = split_np(wide)
    forward = np.concatenate([high, low, high], axis=2)
    flip = lambda t: np.swapaxes(t, 1, 2)
    inverse = np.concatenate([flip(high), flip(low), flip(high)], axis=2)
    return forward, np.ascontiguousarray(inverse)


def dot(a, b):
    return lax.dot_general(a, b, (((1,), (0,)), ((), ())), preferred_element_type=f32)


def dot_nt(a, b):
    return lax.dot_general(a, b, (((1,), (1,)), ((), ())), preferred_element_type=f32)


def dot_tn(a, b):
    return lax.dot_general(a, b, (((0,), (0,)), ((), ())), preferred_element_type=f32)


def split(value):
    high = value.astype(bf16)
    return high, (value - high.astype(f32)).astype(bf16)


def lane_sign(shape, first):
    lane = lax.broadcasted_iota(jnp.int32, shape, len(shape) - 1)
    return jnp.where(lane < shape[-1] // 2, first, -first).astype(f32)


def swap(value):
    return pltpu.roll(value, value.shape[-1] // 2, value.ndim - 1)


def to_spectra(channels, fields, x_table, own, other, own_out, other_out, u_high, u_low):
    cells = x_table.shape[1] // 3
    for block in range(channels // CBLOCK):
        pieces = fields(block)
        stacked = pieces[0] if len(pieces) == 1 else jnp.concatenate(pieces, axis=0)
        result = dot(x_table[:, : cells * len(pieces)], stacked)
        high, low = split(result)
        rows = pl.ds(block * CBLOCK, CBLOCK)
        shape = (2 * HALF, CBLOCK, high.shape[-1])
        u_high[:, rows, :] = high.reshape(shape)
        u_low[:, rows, :] = low.reshape(shape)
    table = jnp.concatenate([own[...], other[...]], axis=0)
    part = own.shape[0] // 2
    count = part // 2
    brief = jnp.concatenate([own[:part, :], other[:part, :]], axis=0)
    width = 2 * channels
    sign = lane_sign((count, width), -1.0)
    for first in range(0, HALF, 2):
        several = min(2, HALF - first)
        at = pl.ds(2 * first, 2 * several)
        high = u_high[at].reshape(several * width, u_high.shape[-1])
        low = u_low[at].reshape(several * width, u_low.shape[-1])
        wide = dot_nt(table, high)
        small = dot_nt(brief, low)
        for which, out in enumerate((own_out, other_out)):
            base = 2 * part * which
            total = (wide[base : base + part] + wide[base + part : base + 2 * part]) + small[
                part * which : part * (which + 1)
            ]
            for step in range(several):
                kx = first + step
                real = total[:count, step * width : (step + 1) * width]
                imag = swap(total[count:, step * width : (step + 1) * width])
                if kx < MX // 2:
                    out[kx] = real + imag * sign
                if kx > 0:
                    out[MX - kx] = imag - real * sign


def from_spectra(channels, own_in, other_in, x_table, own, other, u_high, u_low, t_high, t_low):
    part = own.shape[0] // 2
    count = part // 2
    width = 2 * channels
    sign = lane_sign((count, width), -1.0)
    for kx in range(HALF):
        pieces = []
        for source in (own_in, other_in):
            if kx == 0:
                ahead = source[0]
                real, imag = ahead, ahead * sign
            elif kx == MX // 2:
                behind = source[MX - kx]
                real, imag = -behind * sign, behind
            else:
                ahead, behind = source[kx], source[MX - kx]
                real, imag = ahead - behind * sign, ahead * sign + behind
            pieces += [real, swap(imag)]
        turned = jnp.concatenate(pieces, axis=0).T
        high, low = split(turned)
        t_high[pl.ds(kx * width, width), :] = high
        t_low[pl.ds(kx * width, width), :] = low
    table_high = jnp.concatenate([own[:part, :], other[:part, :]], axis=0)
    table_low = jnp.concatenate([own[part:, :], other[part:, :]], axis=0)
    several = 3 if HALF % 3 == 0 else 1
    for first in range(0, HALF, several):
        at = pl.ds(first * width, several * width)
        high, low = t_high[at, :], t_low[at, :]
        value = dot(high, table_high) + dot(low, table_high) + dot(high, table_low)
        value_high, value_low = split(value)
        shape = (2 * several, channels, value.shape[-1])
        u_high[pl.ds(2 * first, 2 * several)] = value_high.reshape(shape)
        u_low[pl.ds(2 * first, 2 * several)] = value_low.reshape(shape)

    def block(index):
        rows = pl.ds(index * CBLOCK, CBLOCK)
        shape = (2 * HALF * CBLOCK, u_high.shape[-1])
        high = u_high[:, rows, :].reshape(shape)
        low = u_low[:, rows, :].reshape(shape)
        return dot(x_table[...], jnp.concatenate([high, high, low], axis=0))

    return block


def first_kernel(place, field, x_table, own, other, own_out, other_out, u_high, u_low):
    width, channels, cells = field.shape

    def fields(block):
        piece = field[:, pl.ds(block * CBLOCK, CBLOCK), :].reshape(width * CBLOCK, cells)
        return [piece, piece]

    to_spectra(channels, fields, x_table, own, other, own_out, other_out, u_high, u_low)


def middle_kernel(
    place, own_in, other_in, field, cotangent, pointwise, x_inverse, x_forward, own, other,
    own_out, other_out, slope_high, slope_low, u_high, u_low, t_high, t_low, pre,
):
    width, channels, cells = field.shape
    block = from_spectra(channels, own_in, other_in, x_inverse, own, other, u_high, u_low, t_high, t_low)
    for index in range(channels // CBLOCK):
        pre[:, pl.ds(index * CBLOCK, CBLOCK), :] = block(index).reshape(width, CBLOCK, cells)
    root = math.sqrt(2.0 / math.pi)
    mixer = jnp.concatenate(split(pointwise[...].T), axis=0)

    @pl.loop(0, width)
    def _(x):
        local = dot(mixer, field[x])
        value = pre[x] + (local[:channels] + local[channels:])
        square = value * value
        tanh = jnp.tanh(root * value * (1.0 + 0.044715 * square))
        slope = 0.5 * (1.0 + tanh) + (0.5 * root) * value * (1.0 - tanh * tanh) * (1.0 + 3.0 * 0.044715 * square)
        slope = slope * cotangent[x].astype(f32)
        high, low = split(slope)
        slope_high[x] = high
        slope_low[x] = low

    def fields(index):
        rows = pl.ds(index * CBLOCK, CBLOCK)
        shape = (width * CBLOCK, cells)
        high = slope_high[:, rows, :].reshape(shape)
        return [high, high, slope_low[:, rows, :].reshape(shape)]

    to_spectra(channels, fields, x_forward, own, other, own_out, other_out, u_high, u_low)


def last_kernel(place, own_in, other_in, local, x_inverse, own, other, out, u_high, u_low, t_high, t_low):
    width, channels, cells = out.shape
    block = from_spectra(channels, own_in, other_in, x_inverse, own, other, u_high, u_low, t_high, t_low)
    for index in range(channels // CBLOCK):
        rows = pl.ds(index * CBLOCK, CBLOCK)
        value = block(index).reshape(width, CBLOCK, cells) + local[:, rows, :]
        out[:, rows, :] = value.astype(bf16)


def local_kernel(high_in, low_in, pointwise, out):
    channels = pointwise.shape[0]
    high, low = split(pointwise[...])
    wide = dot(jnp.concatenate([high, low], axis=0), high_in[0])
    out[0] = (wide[:channels] + wide[channels:]) + dot(high, low_in[0])


def pairs_of(count):
    return [list(range(first, min(first + 2, count))) for first in range(0, count, 2)]


def spread_rows(rows, lower):
    if len(rows) == 1:
        half = rows[0].shape[-1] // 2
        return jnp.concatenate([rows[0][:, :half], rows[0][:, half:]], axis=0)
    zero = jnp.zeros_like(rows[0])
    one, two = rows
    return jnp.concatenate(
        [
            jnp.where(lower, one, zero),
            jnp.where(lower, swap(one), zero),
            jnp.where(lower, zero, swap(two)),
            jnp.where(lower, zero, two),
        ],
        axis=0,
    )


def lower_half(shape):
    return lax.broadcasted_iota(jnp.int32, shape, 1) < shape[1] // 2


def mix_kernel(spectra, weight, out):
    samples, modes, width = spectra.shape
    lower = lower_half((samples, width))
    sign = lane_sign((samples, width), -1.0)
    for group in pairs_of(modes):
        rows = spread_rows([spectra[:, mode, :] for mode in group], lower)
        high, low = split(rows)
        block = weight[group[0] : group[0] + len(group)].reshape(-1, width)
        block_high, block_low = split(block)
        wide = dot(jnp.concatenate([high, low], axis=0), block_high)
        total = wide[: rows.shape[0]] + wide[rows.shape[0] :] + dot(high, block_low)
        for step, mode in enumerate(group):
            base = 2 * samples * step
            real, imag = total[base : base + samples], total[base + samples : base + 2 * samples]
            out[:, mode, :] = real + swap(imag) * sign


def adjoint_kernel(spectra, weight, out):
    samples, modes, width = spectra.shape
    lower = lower_half((samples, width))
    sign = lane_sign((samples, width), 1.0)
    for group in pairs_of(modes):
        rows = []
        for mode in group:
            row = spectra[:, mode, :]
            rows += [row, swap(row) * sign]
        rows = jnp.concatenate(rows, axis=0)
        high, low = split(rows)
        block = weight[group[0] : group[0] + len(group)].reshape(-1, width)
        block_high, block_low = split(block)
        wide = dot_nt(jnp.concatenate([high, low], axis=0), block_high)
        total = wide[: rows.shape[0]] + wide[rows.shape[0] :] + dot_nt(high, block_low)
        if len(group) == 1:
            total = jnp.concatenate([total, total], axis=1)
        for step, mode in enumerate(group):
            base = 2 * samples * step
            real, imag = total[base : base + samples], total[base + samples : base + 2 * samples]
            if len(group) == 1:
                out[:, mode, :] = jnp.where(lower, real, imag)
            elif step == 0:
                out[:, mode, :] = jnp.where(lower, real, swap(imag))
            else:
                out[:, mode, :] = jnp.where(lower, swap(real), imag)


def adam_kernel(spectra, slopes, weight, first, second, weight_out, first_out, second_out):
    samples, modes, width = spectra.shape
    lower = lower_half((samples, width))
    sign = lane_sign((samples, width), 1.0)
    for group in pairs_of(modes):
        left = spread_rows([spectra[:, mode, :] for mode in group], lower)
        right = []
        for mode in group:
            row = slopes[:, mode, :]
            right += [row, swap(row) * sign]
        right = jnp.concatenate(right, axis=0)
        left_high, left_low = split(left)
        right_high, right_low = split(right)
        gradient = dot_tn(
            jnp.concatenate([left_high, left_low, left_high], axis=0),
            jnp.concatenate([right_high, right_high, right_low], axis=0),
        )
        at = pl.ds(group[0], len(group))
        shape = (len(group),) + weight.shape[1:]
        gradient = gradient.reshape(shape)
        new_first = beta_first * first[at] + (1.0 - beta_first) * gradient
        new_second = beta_second * second[at] + (1.0 - beta_second) * gradient * gradient
        bottom = jnp.sqrt(new_second * (1.0 / second_correct)) + adam_epsilon
        first_out[at] = new_first
        second_out[at] = new_second
        weight_out[at] = weight[at] - (learn_rate / first_correct) * new_first / bottom


def body(inputs, cotangent, spectral_weight, first_moment, second_moment, pointwise_weight):
    groups = lax.axis_size("space")
    owners = lax.axis_size("dp")
    assert groups == 2 and inputs.shape[0] == 1
    per_group = MY // groups
    _, width, channels, cells = inputs.shape
    lanes = 2 * channels
    count = per_group * MZ
    pairs = spectral_weight.shape[1]
    modes = pairs * MZ
    place = lax.axis_index("space").astype(jnp.int32).reshape(1)

    plain_table = jnp.asarray(yz_tables(groups, False))
    scaled_table = jnp.asarray(yz_tables(groups, True))
    x_forward, x_inverse = map(jnp.asarray, x_tables(groups))

    def mine(array):
        return pl.BlockSpec((None,) + array.shape[1:], lambda i, s: (s[0], 0, 0))

    def others(array):
        return pl.BlockSpec((None,) + array.shape[1:], lambda i, s: (1 - s[0], 0, 0))

    def entire(shape):
        return pl.BlockSpec(shape, lambda i, s: (0,) * len(shape))

    sample = pl.BlockSpec((None, width, channels, cells), lambda i, s: (0, 0, 0, 0))
    spectrum_shape = (MX, count, lanes)
    spectrum = jax.ShapeDtypeStruct(spectrum_shape, f32)
    field_shape = (width, channels, cells)
    u_scratch = [pltpu.VMEM((2 * HALF, channels, cells), bf16)] * 2
    t_scratch = [pltpu.VMEM((HALF * lanes, 2 * groups * count), bf16)] * 2
    params = pltpu.CompilerParams(vmem_limit_bytes=36 * 1024 * 1024)

    def other_core(value):
        return lax.ppermute(value, "space", [(0, 1), (1, 0)])

    def exchange(value):
        return lax.all_to_all(value, "dp", split_axis=0, concat_axis=0, tiled=True)

    own, sent = pl.pallas_call(
        first_kernel,
        out_shape=[spectrum, spectrum],
        grid_spec=pltpu.PrefetchScalarGridSpec(
            num_scalar_prefetch=1,
            grid=(1,),
            in_specs=[sample, mine(x_forward), mine(plain_table), others(plain_table)],
            out_specs=[entire(spectrum_shape)] * 2,
            scratch_shapes=u_scratch,
        ),
        compiler_params=params,
        name="first",
    )(place, inputs, x_forward, plain_table, plain_table)
    owned = exchange((own + other_core(sent)).reshape(owners, modes, lanes))

    block = 16 if modes % 16 == 0 else modes
    grid = (modes // block,)
    spectra_spec = pl.BlockSpec((owners, block, lanes), lambda i: (0, i, 0))
    weight_shape = (modes, channels, lanes)
    weight_spec = pl.BlockSpec((block, channels, lanes), lambda i: (i, 0, 0))
    weight = spectral_weight.reshape(weight_shape)
    mode_params = pltpu.CompilerParams(vmem_limit_bytes=24 * 1024 * 1024)

    def mixing(kernel, value, name):
        return pl.pallas_call(
            kernel,
            out_shape=jax.ShapeDtypeStruct((owners, modes, lanes), f32),
            grid=grid,
            in_specs=[spectra_spec, weight_spec],
            out_specs=spectra_spec,
            compiler_params=mode_params,
            name=name,
        )(value, weight)

    mixture = exchange(mixing(mix_kernel, owned, "mix")).reshape(spectrum_shape)

    field = jax.ShapeDtypeStruct(field_shape, bf16)
    own, sent, slope_high, slope_low = pl.pallas_call(
        middle_kernel,
        out_shape=[spectrum, spectrum, field, field],
        grid_spec=pltpu.PrefetchScalarGridSpec(
            num_scalar_prefetch=1,
            grid=(1,),
            in_specs=[
                entire(spectrum_shape), entire(spectrum_shape), sample, sample, entire(pointwise_weight.shape),
                mine(x_inverse), mine(x_forward), mine(scaled_table), others(scaled_table),
            ],
            out_specs=[entire(spectrum_shape)] * 2 + [entire(field_shape)] * 2,
            scratch_shapes=u_scratch + t_scratch + [pltpu.VMEM(field_shape, f32)],
        ),
        compiler_params=params,
        name="middle",
    )(place, mixture, other_core(mixture), inputs, cotangent, pointwise_weight, x_inverse, x_forward, scaled_table, scaled_table)
    slopes = exchange((own + other_core(sent)).reshape(owners, modes, lanes))

    plane = pl.BlockSpec((1, channels, cells), lambda i: (i, 0, 0))
    local = pl.pallas_call(
        local_kernel,
        out_shape=jax.ShapeDtypeStruct(field_shape, f32),
        grid=(width,),
        in_specs=[plane, plane, pl.BlockSpec(pointwise_weight.shape, lambda i: (0, 0))],
        out_specs=plane,
        cost_estimate=pl.CostEstimate(flops=4 * 10**9, bytes_accessed=4 * 10**6, transcendentals=0),
        name="local",
    )(slope_high, slope_low, pointwise_weight)

    back = exchange(mixing(adjoint_kernel, slopes, "adjoint")).reshape(spectrum_shape)

    whole = jax.ShapeDtypeStruct(weight_shape, f32)
    new_weight, new_first, new_second = pl.pallas_call(
        adam_kernel,
        out_shape=[whole] * 3,
        grid=grid,
        in_specs=[spectra_spec, spectra_spec] + [weight_spec] * 3,
        out_specs=[weight_spec] * 3,
        compiler_params=mode_params,
        cost_estimate=pl.CostEstimate(flops=10**10, bytes_accessed=3 * 10**7, transcendentals=10**6),
        name="adam",
    )(owned, slopes, weight, first_moment.reshape(weight_shape), second_moment.reshape(weight_shape))

    out_field = pl.pallas_call(
        last_kernel,
        out_shape=jax.ShapeDtypeStruct(inputs.shape, bf16),
        grid_spec=pltpu.PrefetchScalarGridSpec(
            num_scalar_prefetch=1,
            grid=(1,),
            in_specs=[
                entire(spectrum_shape), entire(spectrum_shape), entire(field_shape),
                mine(x_inverse), mine(plain_table), others(plain_table),
            ],
            out_specs=sample,
            scratch_shapes=u_scratch + t_scratch,
        ),
        compiler_params=params,
        name="last",
    )(place, back, other_core(back), local, x_inverse, plain_table, plain_table)
    shape = spectral_weight.shape
    return (out_field, new_weight.reshape(shape), new_first.reshape(shape), new_second.reshape(shape))


def solution(mesh):
    return jax.shard_map(
        body,
        mesh=mesh,
        in_specs=(
            P(("grp", "dp"), "space", None, None),
            P(("grp", "dp"), "space", None, None),
            P(("grp", "space"), "dp", None, None, None),
            P(("grp", "space"), "dp", None, None, None),
            P(("grp", "space"), "dp", None, None, None),
            P("grp", None),
        ),
        out_specs=(
            P(("grp", "dp"), "space", None, None),
            P(("grp", "space"), "dp", None, None, None),
            P(("grp", "space"), "dp", None, None, None),
            P(("grp", "space"), "dp", None, None, None),
        ),
        check_vma=False,
    )
```

profile of v0, /device:TPU:0, one launch (start us, length us, event | category | flops | bytes accessed | tf_op | source)
XLA Modules:
  0.0 135.8 jit_solution(18078751433614825269)
XLA Ops:
  0.6 0.0 copy-start
  0.6 0.0 copy-start.2
  0.7 1.2 copy-done.2
  1.9 0.0 copy-start.4
  1.9 1.5 %copy-done.4 = bf16[1,16,64,512]{3,2,1,0:T(8,128)(2,1)S(1)} copy-done((bf16[1,16,64,512]{3,2,1,0:T(8,128)(2,1)S(1)}, bf16[1,16,64,512]{3,2,1,0:T(8,128)(2,1)}, u32[]{:S(2)}) %copy-start.4) | copy-done | bytes 1048600
  3.4 0.0 copy-start.6
  3.4 1.2 copy-done.6
  4.5 2.3 %first.1 = (f32[16,72,128]{2,1,0:T(8,128)S(1)}, f32[16,72,128]{2,1,0:T(8,128)S(1)}) custom-call(s32[1]{0:T(128)} %bitcast.place, bf16[1,16,64,512]{3,2,1,0:T(8,128)(2,1)S(1)} %copy-done.4, bf16[2,288,768]{2,1,0:T(8,128)(2,1)S(1)} %copy-done.6, bf16[2,288,512]{2,1,0:T(8,128)(2,1)S(1)} %copy-done.2, bf16[2,288,512]{2,1,0:T(8,128)(2,1)S(1)} %copy-done.2), custom_call_target="tpu_custom_call" | custom-call | tf_op jit(solution)/shard_map/first/pallas_call | solution.py:369
  6.8 0.5 collective-permute-start
  7.4 1.6 %collective-permute-done = f32[16,72,128]{2,1,0:T(8,128)S(1)} collective-permute-done((f32[16,72,128]{2,1,0:T(8,128)S(1)}, f32[16,72,128]{2,1,0:T(8,128)S(1)}, u32[]{:S(2)}, u32[]{:S(2)}) %collective-permute-start) | collective-permute-done | bytes 589856 | tf_op jit(solution)/shard_map/ppermute | solution.py:364
  9.0 0.0 copy-start.5
  9.0 0.0 copy-start.7
  9.0 0.0 copy-start.9
  9.0 0.0 copy-start.10
  9.0 0.1 add.6
  9.1 23.9 %all_to_all.20.spectra = f32[8,144,128]{2,1,0:T(8,128)S(1)} all-to-all(f32[8,144,128]{2,1,0:T(8,128)S(1)} %bitcast.20), channel_id=1, replica_groups=mesh['grp'=2,'dp'=8,'space'=2] {'dp'}, dimensions={0} | all-to-all | bytes 1179648 | tf_op jit(solution)/shard_map/all_to_all | solution.py:367
  33.0 0.0 copy-done
  33.0 3.8 %mix.1 = f32[8,144,128]{2,1,0:T(8,128)S(1)} custom-call(f32[8,144,128]{2,1,0:T(8,128)S(1)} %all_to_all.20.spectra, f32[144,64,128]{2,1,0:T(8,128)S(1)} %bitcast.11), custom_call_target="tpu_custom_call" | custom-call | tf_op jit(solution)/shard_map/mix/pallas_call | solution.py:393
  36.8 19.3 %all_to_all.21 = f32[8,144,128]{2,1,0:T(8,128)S(1)} all-to-all(f32[8,144,128]{2,1,0:T(8,128)S(1)} %mix.1), channel_id=1, replica_groups=mesh['grp'=2,'dp'=8,'space'=2] {'dp'}, dimensions={0} | all-to-all | bytes 1179648 | tf_op jit(solution)/shard_map/all_to_all | solution.py:367
  56.1 0.0 collective-permute-start.1
  56.1 2.0 %collective-permute-done.1.other_in = f32[16,72,128]{2,1,0:T(8,128)S(1)} collective-permute-done((f32[16,72,128]{2,1,0:T(8,128)S(1)}, f32[16,72,128]{2,1,0:T(8,128)S(1)}, u32[]{:S(2)}, u32[]{:S(2)}) %collective-permute-start.1) | collective-permute-done | bytes 589856 | tf_op jit(solution)/shard_map/ppermute | solution.py:364
  58.1 0.0 copy-done.5
  58.1 0.0 copy-done.7
  58.1 0.0 copy-done.9
  58.1 0.0 copy-done.10
  58.1 10.2 %middle.1 = (f32[16,72,128]{2,1,0:T(8,128)S(1)}, f32[16,72,128]{2,1,0:T(8,128)S(1)}, bf16[16,64,512]{2,1,0:T(8,128)(2,1)S(1)}, bf16[16,64,512]{2,1,0:T(8,128)(2,1)S(1)}) custom-call(s32[1]{0:T(128)} %bitcast.place, f32[16,72,128]{2,1,0:T(8,128)S(1)} %bitcast.17, f32[16,72,128]{2,1,0:T(8,128)S(1)} %collective-permute-done.1.other_in, ...), custom_call_target="tpu_custom_call" | custom-call | tf_op jit(solution)/shard_map/middle/pallas_call | solution.py:406
  68.3 0.0 copy-start.14
  68.3 1.0 copy-done.14
  69.3 0.0 copy-start.13
  69.3 0.1 collective-permute-start.2
  69.4 1.9 %collective-permute-done.2 = f32[16,72,128]{2,1,0:T(8,128)S(1)} collective-permute-done((f32[16,72,128]{2,1,0:T(8,128)S(1)}, f32[16,72,128]{2,1,0:T(8,128)S(1)}, u32[]{:S(2)}, u32[]{:S(2)}) %collective-permute-start.2) | collective-permute-done | bytes 589856 | tf_op jit(solution)/shard_map/ppermute | solution.py:364
  71.3 0.1 add.7
  71.4 0.0 copy-done.13
  71.4 19.6 %all_to_all.22.spectra.slopes = f32[8,144,128]{2,1,0:T(8,128)S(1)} all-to-all(f32[8,144,128]{2,1,0:T(8,128)S(1)} %bitcast.21), channel_id=1, replica_groups=mesh['grp'=2,'dp'=8,'space'=2] {'dp'}, dimensions={0} | all-to-all | bytes 1179648 | tf_op jit(solution)/shard_map/all_to_all | solution.py:367
  91.0 5.8 %adjoint.1 = f32[8,144,128]{2,1,0:T(8,128)} custom-call(f32[8,144,128]{2,1,0:T(8,128)S(1)} %all_to_all.22.spectra.slopes, f32[144,64,128]{2,1,0:T(8,128)S(1)} %bitcast.12), custom_call_target="tpu_custom_call" | custom-call | tf_op jit(solution)/shard_map/adjoint/pallas_call | solution.py:393
  96.8 3.5 %all-to-all-start.3 = ((f32[8,144,128]{2,1,0:T(8,128)}), f32[8,144,128]{2,1,0:T(8,128)S(1)}, u32[]{:S(2)}, u32[]{:S(2)}) async-start(f32[8,144,128]{2,1,0:T(8,128)} %adjoint.1), calls=%async_computation.3 | async-start | bytes 1179648 | tf_op jit(solution)/shard_map/all_to_all | solution.py:367
  100.3 10.3 %local.1 = f32[16,64,512]{2,1,0:T(8,128)} custom-call(bf16[16,64,512]{2,1,0:T(8,128)(2,1)} %copy-done.13, bf16[16,64,512]{2,1,0:T(8,128)(2,1)} %copy-done.14, f32[64,64]{1,0:T(8,128)} %pointwise.3), custom_call_target="tpu_custom_call" | custom-call | flops 4000000000 | bytes 4000000 | tf_op jit(solution)/shard_map/local/pallas_call | solution.py:425
  110.6 5.0 %all-to-all-done.3 = f32[8,144,128]{2,1,0:T(8,128)S(1)} async-done(((f32[8,144,128]{2,1,0:T(8,128)}), f32[8,144,128]{2,1,0:T(8,128)S(1)}, u32[]{:S(2)}, u32[]{:S(2)}) %all-to-all-start.3) | async-done | bytes 589856 | tf_op jit(solution)/shard_map/all_to_all | solution.py:367
  115.6 0.0 collective-permute-start.3
  115.6 0.0 copy-start.1
  115.6 2.3 %copy-done.1 = f32[1,16,9,64,128]{4,3,2,1,0:T(8,128)S(1)} copy-done((f32[1,16,9,64,128]{4,3,2,1,0:T(8,128)S(1)}, f32[1,16,9,64,128]{4,3,2,1,0:T(8,128)}, u32[]{:S(2)}) %copy-start.1) | copy-done | bytes 4718616
  118.0 2.3 %copy-done.11 = f32[1,16,9,64,128]{4,3,2,1,0:T(8,128)S(1)} copy-done((f32[1,16,9,64,128]{4,3,2,1,0:T(8,128)S(1)}, f32[1,16,9,64,128]{4,3,2,1,0:T(8,128)}, u32[]{:S(2)}) %copy-start.11) | copy-done | bytes 4718616
  120.3 2.3 %copy-done.12 = f32[1,16,9,64,128]{4,3,2,1,0:T(8,128)S(1)} copy-done((f32[1,16,9,64,128]{4,3,2,1,0:T(8,128)S(1)}, f32[1,16,9,64,128]{4,3,2,1,0:T(8,128)}, u32[]{:S(2)}) %copy-start.12) | copy-done | bytes 4718616
  122.6 8.7 %adam.1 = (f32[144,64,128]{2,1,0:T(8,128)}, f32[144,64,128]{2,1,0:T(8,128)}, f32[144,64,128]{2,1,0:T(8,128)}) custom-call(f32[8,144,128]{2,1,0:T(8,128)S(1)} %all_to_all.20.spectra, f32[8,144,128]{2,1,0:T(8,128)S(1)} %all_to_all.22.spectra.slopes, f32[144,64,128]{2,1,0:T(8,128)S(1)} %bitcast.13, f32[144,64,128]{2,1,0:T(8,128)S(1)} %bitcast.18, ...), custom_call_target="tpu_custom_call" | custom-call | flops 10000000000 | bytes 30000000 | tf_op jit(solution)/shard_map/adam/pallas_call | solution.py:438
  131.4 0.0 collective-permute-done.3.other_in
  131.4 0.0 copy-done.3
  131.4 0.0 copy-done.8
  131.4 4.4 %last.1 = bf16[1,16,64,512]{3,2,1,0:T(8,128)(2,1)} custom-call(s32[1]{0:T(128)} %bitcast.place, f32[16,72,128]{2,1,0:T(8,128)S(1)} %bitcast.15, f32[16,72,128]{2,1,0:T(8,128)S(1)} %collective-permute-done.3.other_in, f32[16,64,512]{2,1,0:T(8,128)S(1)} %copy-done.8, bf16[2,256,864]{2,1,0:T(8,128)(2,1)S(1)} %copy-done.5, bf16[2,288,512]{2,1,0:T(8,128)(2,1)S(1)} %copy-done.3, ...), custom_call_target="tpu_custom_call" | custom-call | tf_op jit(solution)/shard_map/last/pallas_call | solution.py:449
  (4 shorter events, 0.0 us)
Async XLA Ops:
  0.6 32.4 %copy-start = (f32[1,16,9,64,128]{4,3,2,1,0:T(8,128)S(1)}, f32[1,16,9,64,128]{4,3,2,1,0:T(8,128)}, u32[]{:S(2)}) copy-start(f32[1,16,9,64,128]{4,3,2,1,0:T(8,128)} %param.12) | copy-start | bytes 14155780
  0.6 1.2 copy-start.2
  1.9 1.5 %copy-start.4 = (bf16[1,16,64,512]{3,2,1,0:T(8,128)(2,1)S(1)}, bf16[1,16,64,512]{3,2,1,0:T(8,128)(2,1)}, u32[]{:S(2)}) copy-start(bf16[1,16,64,512]{3,2,1,0:T(8,128)(2,1)} %field.3) | copy-start | bytes 3145732
  3.4 1.2 copy-start.6
  6.8 2.2 %collective-permute-start = (f32[16,72,128]{2,1,0:T(8,128)S(1)}, f32[16,72,128]{2,1,0:T(8,128)S(1)}, u32[]{:S(2)}, u32[]{:S(2)}) collective-permute-start(f32[16,72,128]{2,1,0:T(8,128)S(1)} %get-tuple-element.14), channel_id=1, source_target_pairs={{0,1},{1,0},{2,3},{3,2},{4,5},{5,4},{6,7},{7,6},{8,9},{9,8},{10,11... | collective-permute-start | bytes 1769480 | tf_op jit(solution)/shard_map/ppermute | solution.py:364
  9.0 49.1 %copy-start.5 = (bf16[2,256,864]{2,1,0:T(8,128)(2,1)S(1)}, bf16[2,256,864]{2,1,0:T(8,128)(2,1)}, u32[]{:S(2)}) copy-start(bf16[2,256,864]{2,1,0:T(8,128)(2,1)} %constant.15.clone.x_inverse) | copy-start | bytes 2654212
  9.0 49.1 %copy-start.7 = (bf16[2,288,512]{2,1,0:T(8,128)(2,1)S(1)}, bf16[2,288,512]{2,1,0:T(8,128)(2,1)}, u32[]{:S(2)}) copy-start(bf16[2,288,512]{2,1,0:T(8,128)(2,1)} %constant.13.clone.own.other) | copy-start | bytes 1769476
  9.0 49.1 %copy-start.9 = (bf16[1,16,64,512]{3,2,1,0:T(8,128)(2,1)S(1)}, bf16[1,16,64,512]{3,2,1,0:T(8,128)(2,1)}, u32[]{:S(2)}) copy-start(bf16[1,16,64,512]{3,2,1,0:T(8,128)(2,1)} %cotangent.1) | copy-start | bytes 3145732
  9.0 49.1 %copy-start.10 = (f32[64,64]{1,0:T(8,128)S(1)}, f32[64,64]{1,0:T(8,128)}, u32[]{:S(2)}) copy-start(f32[64,64]{1,0:T(8,128)} %pointwise.3) | copy-start | bytes 49156
  56.1 2.0 %collective-permute-start.1 = (f32[16,72,128]{2,1,0:T(8,128)S(1)}, f32[16,72,128]{2,1,0:T(8,128)S(1)}, u32[]{:S(2)}, u32[]{:S(2)}) collective-permute-start(f32[16,72,128]{2,1,0:T(8,128)S(1)} %bitcast.16), channel_id=1, source_target_pairs={{0,1},{1,0},{2,3},{3,2},{4,5},{5,4},{6,7},{7,6},{8,9},{9,8},{10,11... | collective-permute-start | bytes 1769480 | tf_op jit(solution)/shard_map/ppermute | solution.py:364
  68.3 1.0 copy-start.14
  69.3 2.1 %copy-start.13 = (bf16[16,64,512]{2,1,0:T(8,128)(2,1)}, bf16[16,64,512]{2,1,0:T(8,128)(2,1)S(1)}, u32[]{:S(2)}) copy-start(bf16[16,64,512]{2,1,0:T(8,128)(2,1)S(1)} %get-tuple-element.17.high_in) | copy-start | bytes 3145732
  69.3 2.0 %collective-permute-start.2 = (f32[16,72,128]{2,1,0:T(8,128)S(1)}, f32[16,72,128]{2,1,0:T(8,128)S(1)}, u32[]{:S(2)}, u32[]{:S(2)}) collective-permute-start(f32[16,72,128]{2,1,0:T(8,128)S(1)} %get-tuple-element.16), channel_id=1, source_target_pairs={{0,1},{1,0},{2,3},{3,2},{4,5},{5,4},{6,7},{7,6},{8,9},{9,8},{10,11... | collective-permute-start | bytes 1769480 | tf_op jit(solution)/shard_map/ppermute | solution.py:364
  96.8 18.8 %all-to-all-start.3 = ((f32[8,144,128]{2,1,0:T(8,128)}), f32[8,144,128]{2,1,0:T(8,128)S(1)}, u32[]{:S(2)}, u32[]{:S(2)}) async-start(f32[8,144,128]{2,1,0:T(8,128)} %adjoint.1), calls=%async_computation.3 | async-start | bytes 1179648 | tf_op jit(solution)/shard_map/all_to_all | solution.py:367
  115.6 15.8 %collective-permute-start.3 = (f32[16,72,128]{2,1,0:T(8,128)S(1)}, f32[16,72,128]{2,1,0:T(8,128)S(1)}, u32[]{:S(2)}, u32[]{:S(2)}) collective-permute-start(f32[16,72,128]{2,1,0:T(8,128)S(1)} %bitcast.14), channel_id=1, source_target_pairs={{0,1},{1,0},{2,3},{3,2},{4,5},{5,4},{6,7},{7,6},{8,9},{9,8},{10,11... | collective-permute-start | bytes 1769480 | tf_op jit(solution)/shard_map/ppermute | solution.py:364
  115.6 2.3 %copy-start.1 = (f32[1,16,9,64,128]{4,3,2,1,0:T(8,128)S(1)}, f32[1,16,9,64,128]{4,3,2,1,0:T(8,128)}, u32[]{:S(2)}) copy-start(f32[1,16,9,64,128]{4,3,2,1,0:T(8,128)} %param.12) | copy-start | bytes 14155780
  118.0 2.3 %copy-start.11 = (f32[1,16,9,64,128]{4,3,2,1,0:T(8,128)S(1)}, f32[1,16,9,64,128]{4,3,2,1,0:T(8,128)}, u32[]{:S(2)}) copy-start(f32[1,16,9,64,128]{4,3,2,1,0:T(8,128)} %param.13) | copy-start | bytes 14155780
  120.3 2.3 %copy-start.12 = (f32[1,16,9,64,128]{4,3,2,1,0:T(8,128)S(1)}, f32[1,16,9,64,128]{4,3,2,1,0:T(8,128)}, u32[]{:S(2)}) copy-start(f32[1,16,9,64,128]{4,3,2,1,0:T(8,128)} %param.14) | copy-start | bytes 14155780
  122.6 8.7 %copy-start.3 = (bf16[2,288,512]{2,1,0:T(8,128)(2,1)S(1)}, bf16[2,288,512]{2,1,0:T(8,128)(2,1)}, u32[]{:S(2)}) copy-start(bf16[2,288,512]{2,1,0:T(8,128)(2,1)} %constant.12.clone.own.other) | copy-start | bytes 1769476
  122.6 8.7 %copy-start.8 = (f32[16,64,512]{2,1,0:T(8,128)S(1)}, f32[16,64,512]{2,1,0:T(8,128)}, u32[]{:S(2)}) copy-start(f32[16,64,512]{2,1,0:T(8,128)} %local.1) | copy-start | bytes 6291460
where the time goes:
time: 137 us; the launch traced here: 136 us
  blocking collectives  62.8 us (46%)
  Pallas kernels  45.6 us (33%)
  local copies, waits for them, and re-layouts  11.9 us (9%)
  waiting for transfers between devices  10.5 us (8%)
  starting transfers between devices  4.2 us (3%)
    all_to_all x3, blocking collectives, exchange(): return lax.all_to_all(value, 'dp', split_axis=0, concat_axis=0, tiled=True)  62.8 us
    unnamed x30, local copies, waits for them, and re-layouts  11.9 us
    pallas_call x1, Pallas kernels, body(): pl.pallas_call(local_kernel, out_shape=jax.ShapeDtypeStruct(field_shape,...  10.3 us
    pallas_call x1, Pallas kernels, body(): pl.pallas_call(middle_kernel, out_shape=[spectrum, spectrum, field, field...  10.2 us
    pallas_call x2, Pallas kernels, mixing(): pl.pallas_call(kernel, out_shape=jax.ShapeDtypeStruct((owners, modes, lan...  9.63 us
    pallas_call x1, Pallas kernels, body(): pl.pallas_call(adam_kernel, out_shape=[whole] * 3, grid=grid, in_specs=[s...  8.73 us
    ppermute x4, waiting for transfers between devices, other_core(): return lax.ppermute(value, 'space', [(0, 1), (1, 0)])  5.51 us
    all_to_all x1, waiting for transfers between devices, exchange(): return lax.all_to_all(value, 'dp', split_axis=0, concat_axis=0, tiled=True)  4.98 us
  transfers between devices with their start and end apart: 5, of which 4 were waited for; matrix products, arithmetic and copies ran while one was open for 0% of the time, Pallas kernels for 14%

commit v1 on v0

--- a/solution.py
+++ b/solution.py
@@ -1,3 +1,4 @@
+import functools
 import math
 
 import jax
@@ -17,6 +18,9 @@
 GZ = 32
 HALF = MX // 2 + 1
 CBLOCK = 16
+ORDER = (0, 1, 2, 3, 4, 5, 6, 7)
+BACK_ORDER = (4, 5, 6, 7, 3, 2, 1, 0)
+LAST_ORDER = (1, 2, 4, 5, 6, 7, 3, 0)
 
 beta_first = 0.9
 beta_second = 0.999
@@ -88,10 +92,10 @@
     return pltpu.roll(value, value.shape[-1] // 2, value.ndim - 1)
 
 
-def to_spectra(channels, fields, x_table, own, other, own_out, other_out, u_high, u_low):
-    cells = x_table.shape[1] // 3
+def to_spectra(channels, fields, x_table, own, other, own_out, other_out, u_high, u_low, ready=None):
     for block in range(channels // CBLOCK):
         pieces = fields(block)
+        cells = pieces[0].shape[0]
         stacked = pieces[0] if len(pieces) == 1 else jnp.concatenate(pieces, axis=0)
         result = dot(x_table[:, : cells * len(pieces)], stacked)
         high, low = split(result)
@@ -99,6 +103,8 @@
         shape = (2 * HALF, CBLOCK, high.shape[-1])
         u_high[:, rows, :] = high.reshape(shape)
         u_low[:, rows, :] = low.reshape(shape)
+    if ready is not None:
+        ready()
     table = jnp.concatenate([own[...], other[...]], axis=0)
     part = own.shape[0] // 2
     count = part // 2
@@ -125,6 +131,18 @@
                     out[kx] = real + imag * sign
                 if kx > 0:
                     out[MX - kx] = imag - real * sign
+
+
+def gather(place, order, sources, target):
+    for step, source in zip(order, sources):
+        block = source.shape[0]
+        target[pl.ds((place[1] ^ step) * block, block)] = source[...]
+
+
+def scatter(place, order, source, target):
+    block = target.shape[1]
+    for index, step in enumerate(order):
+        target[index] = source[pl.ds((place[1] ^ step) * block, block)]
 
 
 def from_spectra(channels, own_in, other_in, x_table, own, other, u_high, u_low, t_high, t_low):
@@ -171,20 +189,44 @@
     return block
 
 
-def first_kernel(place, field, x_table, own, other, own_out, other_out, u_high, u_low):
-    width, channels, cells = field.shape
+def first_kernel(
+    order, field_in, x_in, table_in, own_part, other_part, field, x_table, own, other, sems, u_high, u_low, own_out, other_out
+):
+    blocks, width, _, cells = field.shape
+    space = lax.axis_index("space")
+    place = (space, lax.axis_index("dp") if len(order) > 1 else 0)
+    copies = [pltpu.make_async_copy(x_in.at[space], x_table, sems.at[0])]
+    for block in range(blocks):
+        piece = field_in.at[0, :, pl.ds(block * CBLOCK, CBLOCK), :]
+        copies.append(pltpu.make_async_copy(piece, field.at[block], sems.at[1 + block]))
+    copies.append(pltpu.make_async_copy(table_in.at[space], own, sems.at[1 + blocks]))
+    copies.append(pltpu.make_async_copy(table_in.at[1 - space], other, sems.at[2 + blocks]))
+    for copy in copies:
+        copy.start()
+    copies[0].wait()
 
     def fields(block):
-        piece = field[:, pl.ds(block * CBLOCK, CBLOCK), :].reshape(width * CBLOCK, cells)
+        copies[1 + block].wait()
+        piece = field[block].reshape(width * CBLOCK, cells)
         return [piece, piece]
 
-    to_spectra(channels, fields, x_table, own, other, own_out, other_out, u_high, u_low)
-
-
-def middle_kernel(
-    place, own_in, other_in, field, cotangent, pointwise, x_inverse, x_forward, own, other,
-    own_out, other_out, slope_high, slope_low, u_high, u_low, t_high, t_low, pre,
-):
+    def ready():
+        copies[1 + blocks].wait()
+        copies[2 + blocks].wait()
+
+    channels = blocks * CBLOCK
+    to_spectra(channels, fields, x_table, own, other, own_out, other_out, u_high, u_low, ready)
+    scatter(place, order, other_out, other_part)
+    scatter(place, order, own_out, own_part)
+
+
+def middle_kernel(back_order, order, place, *refs):
+    number = len(back_order)
+    own_blocks, other_blocks = refs[:number], refs[number : 2 * number]
+    field, cotangent, pointwise, x_inverse, x_forward, own, other, *refs = refs[2 * number :]
+    own_part, other_part, slope_high, slope_low, u_high, u_low, t_high, t_low, own_in, other_in, pre = refs
+    gather(place, back_order, own_blocks, own_in)
+    gather(place, back_order, other_blocks, other_in)
     width, channels, cells = field.shape
     block = from_spectra(channels, own_in, other_in, x_inverse, own, other, u_high, u_low, t_high, t_low)
     for index in range(channels // CBLOCK):
@@ -210,10 +252,17 @@
         high = slope_high[:, rows, :].reshape(shape)
         return [high, high, slope_low[:, rows, :].reshape(shape)]
 
-    to_spectra(channels, fields, x_forward, own, other, own_out, other_out, u_high, u_low)
-
-
-def last_kernel(place, own_in, other_in, local, x_inverse, own, other, out, u_high, u_low, t_high, t_low):
+    to_spectra(channels, fields, x_forward, own, other, own_in, other_in, u_high, u_low)
+    scatter(place, order, other_in, other_part)
+    scatter(place, order, own_in, own_part)
+
+
+def last_kernel(order, place, *refs):
+    number = len(order)
+    own_blocks, other_blocks = refs[:number], refs[number : 2 * number]
+    local, x_inverse, own, other, out, u_high, u_low, t_high, t_low, own_in, other_in = refs[2 * number :]
+    gather(place, order, own_blocks, own_in)
+    gather(place, order, other_blocks, other_in)
     width, channels, cells = out.shape
     block = from_spectra(channels, own_in, other_in, x_inverse, own, other, u_high, u_low, t_high, t_low)
     for index in range(channels // CBLOCK):
@@ -222,11 +271,15 @@
         out[:, rows, :] = value.astype(bf16)
 
 
-def local_kernel(high_in, low_in, pointwise, out):
+def local_gradient(high_in, low_in, pointwise, out):
     channels = pointwise.shape[0]
     high, low = split(pointwise[...])
-    wide = dot(jnp.concatenate([high, low], axis=0), high_in[0])
-    out[0] = (wide[:channels] + wide[channels:]) + dot(high, low_in[0])
+    both = jnp.concatenate([high, low], axis=0)
+
+    @pl.loop(0, out.shape[0])
+    def _(x):
+        wide = dot(both, high_in[x])
+        out[x] = (wide[:channels] + wide[channels:]) + dot(high, low_in[x])
 
 
 def pairs_of(count):
@@ -254,52 +307,116 @@
     return lax.broadcasted_iota(jnp.int32, shape, 1) < shape[1] // 2
 
 
-def mix_kernel(spectra, weight, out):
-    samples, modes, width = spectra.shape
+def mode_chunk(modes):
+    return 16 if modes % 16 == 0 else modes
+
+
+def stack(refs, target):
+    base = 0
+    for ref in refs:
+        target[pl.ds(base, ref.shape[0])] = ref[...]
+        base += ref.shape[0]
+
+
+def unstack(source, refs):
+    base = 0
+    for ref in refs:
+        ref[...] = source[pl.ds(base, ref.shape[0])]
+        base += ref.shape[0]
+
+
+def split_kernel(weight, high, low):
+    high[...], low[...] = split(weight[...])
+
+
+def local_split_kernel(slope_high, slope_low, pointwise, weight, local, high, low):
+    local_gradient(slope_high, slope_low, pointwise, local)
+    modes = weight.shape[0]
+    chunk = mode_chunk(modes)
+
+    @pl.loop(0, modes // chunk)
+    def _(index):
+        at = pl.ds(index * chunk, chunk)
+        high[at], low[at] = split(weight[at])
+
+
+def hold_kernel(*refs):
+    number = len(refs) // 2
+    for source, target in zip(refs[:number], refs[number:]):
+        target[...] = source[...]
+
+
+def mode_kernel(one_chunk, number, *refs):
+    sources, weights, refs = refs[:number], refs[number : number + 2], refs[number + 2 :]
+    spectra, out = refs[-2:]
+    stack(sources, spectra)
+    modes = spectra.shape[1]
+    chunk = mode_chunk(modes)
+
+    @pl.loop(0, modes // chunk)
+    def _(index):
+        start = index * chunk
+        rows = [spectra[:, start + mode, :] for mode in range(chunk)]
+
+        def weight(first, count):
+            values = [part[pl.ds(start + first, count)] for part in weights]
+            return [value.reshape(-1, value.shape[-1]) for value in values]
+
+        for mode, value in enumerate(one_chunk(rows, weight)):
+            out[:, start + mode, :] = value
+
+    unstack(out, refs[:number])
+
+
+def mix_chunk(rows_of, weight):
+    samples, width = rows_of[0].shape
     lower = lower_half((samples, width))
     sign = lane_sign((samples, width), -1.0)
-    for group in pairs_of(modes):
-        rows = spread_rows([spectra[:, mode, :] for mode in group], lower)
+    results = []
+    for group in pairs_of(len(rows_of)):
+        rows = spread_rows([rows_of[mode] for mode in group], lower)
         high, low = split(rows)
-        block = weight[group[0] : group[0] + len(group)].reshape(-1, width)
-        block_high, block_low = split(block)
+        block_high, block_low = weight(group[0], len(group))
         wide = dot(jnp.concatenate([high, low], axis=0), block_high)
         total = wide[: rows.shape[0]] + wide[rows.shape[0] :] + dot(high, block_low)
         for step, mode in enumerate(group):
             base = 2 * samples * step
             real, imag = total[base : base + samples], total[base + samples : base + 2 * samples]
-            out[:, mode, :] = real + swap(imag) * sign
-
-
-def adjoint_kernel(spectra, weight, out):
-    samples, modes, width = spectra.shape
+            results.append(real + swap(imag) * sign)
+    return results
+
+
+def adjoint_chunk(rows_of, weight):
+    samples, width = rows_of[0].shape
     lower = lower_half((samples, width))
     sign = lane_sign((samples, width), 1.0)
-    for group in pairs_of(modes):
+    results = []
+    for group in pairs_of(len(rows_of)):
         rows = []
         for mode in group:
-            row = spectra[:, mode, :]
-            rows += [row, swap(row) * sign]
+            rows += [rows_of[mode], swap(rows_of[mode]) * sign]
         rows = jnp.concatenate(rows, axis=0)
         high, low = split(rows)
-        block = weight[group[0] : group[0] + len(group)].reshape(-1, width)
-        block_high, block_low = split(block)
+        block_high, block_low = weight(group[0], len(group))
         wide = dot_nt(jnp.concatenate([high, low], axis=0), block_high)
         total = wide[: rows.shape[0]] + wide[rows.shape[0] :] + dot_nt(high, block_low)
-        if len(group) == 1:
-            total = jnp.concatenate([total, total], axis=1)
-        for step, mode in enumerate(group):
+        for step in range(len(group)):
             base = 2 * samples * step
             real, imag = total[base : base + samples], total[base + samples : base + 2 * samples]
             if len(group) == 1:
-                out[:, mode, :] = jnp.where(lower, real, imag)
+                results.append(jnp.concatenate([real, imag], axis=1))
             elif step == 0:
-                out[:, mode, :] = jnp.where(lower, real, swap(imag))
+                results.append(jnp.where(lower, real, swap(imag)))
             else:
-                out[:, mode, :] = jnp.where(lower, swap(real), imag)
-
-
-def adam_kernel(spectra, slopes, weight, first, second, weight_out, first_out, second_out):
+                results.append(jnp.where(lower, swap(real), imag))
+    return results
+
+
+def adam_kernel(number, *refs):
+    spectra_parts, slope_parts, refs = refs[:number], refs[number : 2 * number], refs[2 * number :]
+    weight, first, second, weight_out, first_out, second_out, spectra, slopes = refs
+    stack(spectra_parts, spectra)
+    stack(slope_parts, slopes)
     samples, modes, width = spectra.shape
     lower = lower_half((samples, width))
     sign = lane_sign((samples, width), 1.0)
@@ -337,11 +454,19 @@
     count = per_group * MZ
     pairs = spectral_weight.shape[1]
     modes = pairs * MZ
-    place = lax.axis_index("space").astype(jnp.int32).reshape(1)
+    paired = owners in (2, 4, 8)
+    order, back_order, last_order = (
+        [step for step in steps if step < owners] if paired else [0] for steps in (ORDER, BACK_ORDER, LAST_ORDER)
+    )
+    blocks = owners if paired else 1
+    owner = lax.axis_index("dp").astype(jnp.int32)
+    place = jnp.stack([lax.axis_index("space").astype(jnp.int32), owner if paired else jnp.int32(0)])
 
     plain_table = jnp.asarray(yz_tables(groups, False))
     scaled_table = jnp.asarray(yz_tables(groups, True))
-    x_forward, x_inverse = map(jnp.asarray, x_tables(groups))
+    x_forward, x_inverse = x_tables(groups)
+    x_brief = jnp.asarray(x_forward[:, :, : 2 * width * CBLOCK])
+    x_forward, x_inverse = jnp.asarray(x_forward), jnp.asarray(x_inverse)
 
     def mine(array):
         return pl.BlockSpec((None,) + array.shape[1:], lambda i, s: (s[0], 0, 0))
@@ -358,110 +483,157 @@
     field_shape = (width, channels, cells)
     u_scratch = [pltpu.VMEM((2 * HALF, channels, cells), bf16)] * 2
     t_scratch = [pltpu.VMEM((HALF * lanes, 2 * groups * count), bf16)] * 2
-    params = pltpu.CompilerParams(vmem_limit_bytes=36 * 1024 * 1024)
+    params = pltpu.CompilerParams(vmem_limit_bytes=20 * 1024 * 1024)
 
     def other_core(value):
         return lax.ppermute(value, "space", [(0, 1), (1, 0)])
 
-    def exchange(value):
-        return lax.all_to_all(value, "dp", split_axis=0, concat_axis=0, tiled=True)
-
+    spectrum_scratch = [pltpu.VMEM(spectrum_shape, f32)] * 2
+    part_shape = (blocks, MX // blocks, count, lanes)
+    block_specs = [entire(part_shape[1:])] * (2 * blocks)
+    part_type = jax.ShapeDtypeStruct(part_shape, f32)
+    table_scratch = pltpu.VMEM(plain_table.shape[1:], bf16)
     own, sent = pl.pallas_call(
-        first_kernel,
-        out_shape=[spectrum, spectrum],
-        grid_spec=pltpu.PrefetchScalarGridSpec(
-            num_scalar_prefetch=1,
-            grid=(1,),
-            in_specs=[sample, mine(x_forward), mine(plain_table), others(plain_table)],
-            out_specs=[entire(spectrum_shape)] * 2,
-            scratch_shapes=u_scratch,
-        ),
-        compiler_params=params,
+        functools.partial(first_kernel, order),
+        out_shape=[part_type] * 2,
+        in_specs=[pl.BlockSpec(memory_space=pltpu.HBM)] * 3,
+        scratch_shapes=[
+            pltpu.VMEM((channels // CBLOCK, width, CBLOCK, cells), bf16),
+            pltpu.VMEM(x_brief.shape[1:], bf16),
+            table_scratch,
+            table_scratch,
+            pltpu.SemaphoreType.DMA((channels // CBLOCK + 3,)),
+        ]
+        + u_scratch
+        + spectrum_scratch,
+        compiler_params=pltpu.CompilerParams(vmem_limit_bytes=62 * 1024 * 1024),
         name="first",
-    )(place, inputs, x_forward, plain_table, plain_table)
-    owned = exchange((own + other_core(sent)).reshape(owners, modes, lanes))
-
-    block = 16 if modes % 16 == 0 else modes
-    grid = (modes // block,)
-    spectra_spec = pl.BlockSpec((owners, block, lanes), lambda i: (0, i, 0))
+    )(inputs, x_brief, plain_table)
+
     weight_shape = (modes, channels, lanes)
-    weight_spec = pl.BlockSpec((block, channels, lanes), lambda i: (i, 0, 0))
-    weight = spectral_weight.reshape(weight_shape)
-    mode_params = pltpu.CompilerParams(vmem_limit_bytes=24 * 1024 * 1024)
-
-    def mixing(kernel, value, name):
+    weight, own = lax.optimization_barrier((spectral_weight.reshape(weight_shape), own))
+
+    def travel(value, step):
+        return lax.ppermute(value, "dp", [(i, i ^ step) for i in range(owners)]) if step else value
+
+    def to_owners(own, sent):
+        got = other_core(sent)
+        if not paired:
+            return [lax.all_to_all((own + got).reshape(owners, modes, lanes), "dp", 0, 0, tiled=True)]
+        return [travel((own[i] + got[i]).reshape(1, modes, lanes), step) for i, step in enumerate(order)]
+
+    def from_owners(values, steps, tie=None):
+        if not paired:
+            values = [lax.all_to_all(values[0], "dp", 0, 0, tiled=True)]
+        else:
+            values = [travel(values[order.index(step)], step) for step in steps]
+        if tie is not None:
+            values, tie = lax.optimization_barrier((values, tie))
+        values = [value.reshape(part_shape[1:]) for value in values]
+        return values + [other_core(value) for value in values], tie
+
+    mode_params = pltpu.CompilerParams(vmem_limit_bytes=14 * 1024 * 1024)
+
+    def estimate(microseconds):
+        return pl.CostEstimate(flops=microseconds * 10**9, bytes_accessed=10**5, transcendentals=0)
+
+    def mixing(chunk, values, weights, name):
         return pl.pallas_call(
-            kernel,
-            out_shape=jax.ShapeDtypeStruct((owners, modes, lanes), f32),
-            grid=grid,
-            in_specs=[spectra_spec, weight_spec],
-            out_specs=spectra_spec,
+            functools.partial(mode_kernel, chunk, len(values)),
+            out_shape=[jax.ShapeDtypeStruct(value.shape, f32) for value in values],
+            scratch_shapes=[pltpu.VMEM((owners, modes, lanes), f32)] * 2,
             compiler_params=mode_params,
+            cost_estimate=estimate(1),
             name=name,
-        )(value, weight)
-
-    mixture = exchange(mixing(mix_kernel, owned, "mix")).reshape(spectrum_shape)
+        )(*values, *weights)
+
+    large = 48 if modes % 48 == 0 else modes
+    large_spec = pl.BlockSpec((large, channels, lanes), lambda i: (i, 0, 0))
+    def split_weights(weight):
+        return pl.pallas_call(
+            split_kernel,
+            out_shape=[jax.ShapeDtypeStruct(weight_shape, bf16)] * 2,
+            grid=(modes // large,),
+            in_specs=[large_spec],
+            out_specs=[large_spec] * 2,
+            compiler_params=mode_params,
+            cost_estimate=estimate(6),
+            name="split",
+        )(weight)
+
+    def hold(*values):
+        return pl.pallas_call(
+            hold_kernel,
+            out_shape=[jax.ShapeDtypeStruct(value.shape, value.dtype) for value in values],
+            compiler_params=mode_params,
+            cost_estimate=estimate(6),
+            name="hold",
+        )(*values)
+
+    owned = to_owners(own, sent)
+    mixture = list(mixing(mix_chunk, owned, split_weights(weight), "mix"))
+    mixture[0], field_in, cotangent = lax.optimization_barrier((mixture[0], inputs, cotangent))
+    held = hold(field_in, cotangent, x_inverse, x_forward, scaled_table)
+    mixed, held = from_owners(mixture, back_order, held)
 
     field = jax.ShapeDtypeStruct(field_shape, bf16)
     own, sent, slope_high, slope_low = pl.pallas_call(
-        middle_kernel,
-        out_shape=[spectrum, spectrum, field, field],
+        functools.partial(middle_kernel, back_order, order),
+        out_shape=[part_type] * 2 + [field, field],
         grid_spec=pltpu.PrefetchScalarGridSpec(
             num_scalar_prefetch=1,
             grid=(1,),
             in_specs=[
-                entire(spectrum_shape), entire(spectrum_shape), sample, sample, entire(pointwise_weight.shape),
+                *block_specs, sample, sample, entire(pointwise_weight.shape),
                 mine(x_inverse), mine(x_forward), mine(scaled_table), others(scaled_table),
             ],
-            out_specs=[entire(spectrum_shape)] * 2 + [entire(field_shape)] * 2,
-            scratch_shapes=u_scratch + t_scratch + [pltpu.VMEM(field_shape, f32)],
+            out_specs=[entire(part_shape)] * 2 + [entire(field_shape)] * 2,
+            scratch_shapes=u_scratch + t_scratch + spectrum_scratch + [pltpu.VMEM(field_shape, f32)],
         ),
         compiler_params=params,
         name="middle",
-    )(place, mixture, other_core(mixture), inputs, cotangent, pointwise_weight, x_inverse, x_forward, scaled_table, scaled_table)
-    slopes = exchange((own + other_core(sent)).reshape(owners, modes, lanes))
-
-    plane = pl.BlockSpec((1, channels, cells), lambda i: (i, 0, 0))
-    local = pl.pallas_call(
-        local_kernel,
-        out_shape=jax.ShapeDtypeStruct(field_shape, f32),
-        grid=(width,),
-        in_specs=[plane, plane, pl.BlockSpec(pointwise_weight.shape, lambda i: (0, 0))],
-        out_specs=plane,
-        cost_estimate=pl.CostEstimate(flops=4 * 10**9, bytes_accessed=4 * 10**6, transcendentals=0),
+    )(place, *mixed, *held[:2], pointwise_weight, *held[2:], held[4])
+    again, own = lax.optimization_barrier((weight, own))
+    slopes = to_owners(own, sent)
+    local, *weights = pl.pallas_call(
+        local_split_kernel,
+        out_shape=[jax.ShapeDtypeStruct(field_shape, f32)] + [jax.ShapeDtypeStruct(weight_shape, bf16)] * 2,
+        cost_estimate=estimate(6),
+        compiler_params=mode_params,
         name="local",
-    )(slope_high, slope_low, pointwise_weight)
-
-    back = exchange(mixing(adjoint_kernel, slopes, "adjoint")).reshape(spectrum_shape)
-
+    )(slope_high, slope_low, pointwise_weight, again)
+    turned = mixing(adjoint_chunk, slopes, weights, "adjoint")
+
+    block = 24 if modes % 24 == 0 else modes
     whole = jax.ShapeDtypeStruct(weight_shape, f32)
+    weight_spec = pl.BlockSpec((block, channels, lanes), lambda i: (i, 0, 0))
+    value_specs = [pl.BlockSpec((value.shape[0], block, lanes), lambda i: (0, i, 0)) for value in owned]
     new_weight, new_first, new_second = pl.pallas_call(
-        adam_kernel,
+        functools.partial(adam_kernel, len(owned)),
         out_shape=[whole] * 3,
-        grid=grid,
-        in_specs=[spectra_spec, spectra_spec] + [weight_spec] * 3,
+        grid=(modes // block,),
+        in_specs=value_specs * 2 + [weight_spec] * 3,
         out_specs=[weight_spec] * 3,
-        compiler_params=mode_params,
+        scratch_shapes=[pltpu.VMEM((owners, block, lanes), f32)] * 2,
+        compiler_params=pltpu.CompilerParams(vmem_limit_bytes=56 * 1024 * 1024),
         cost_estimate=pl.CostEstimate(flops=10**10, bytes_accessed=3 * 10**7, transcendentals=10**6),
         name="adam",
-    )(owned, slopes, weight, first_moment.reshape(weight_shape), second_moment.reshape(weight_shape))
+    )(*owned, *slopes, weight, first_moment.reshape(weight_shape), second_moment.reshape(weight_shape))
+    mixed, new_first = from_owners(turned, last_order, new_first)
 
     out_field = pl.pallas_call(
-        last_kernel,
+        functools.partial(last_kernel, last_order),
         out_shape=jax.ShapeDtypeStruct(inputs.shape, bf16),
         grid_spec=pltpu.PrefetchScalarGridSpec(
             num_scalar_prefetch=1,
             grid=(1,),
-            in_specs=[
-                entire(spectrum_shape), entire(spectrum_shape), entire(field_shape),
-                mine(x_inverse), mine(plain_table), others(plain_table),
-            ],
+            in_specs=[*block_specs, entire(field_shape), mine(x_inverse), mine(plain_table), others(plain_table)],
             out_specs=sample,
-            scratch_shapes=u_scratch + t_scratch,
+            scratch_shapes=u_scratch + t_scratch + spectrum_scratch,
         ),
         compiler_params=params,
         name="last",
-    )(place, back, other_core(back), local, x_inverse, plain_table, plain_table)
+    )(place, *mixed, local, x_inverse, plain_table, plain_table)
     shape = spectral_weight.shape
     return (out_field, new_weight.reshape(shape), new_first.reshape(shape), new_second.reshape(shape))
 

time: 137 us -> 123 us (0.90)
  blocking collectives: 62.8 us -> 0 us
  starting transfers between devices: 4.2 us -> 49.5 us
  waiting for transfers between devices: 10.5 us -> 13.8 us
  local copies, waits for them, and re-layouts: 11.9 us -> 8.96 us
  Pallas kernels: 45.6 us -> 47.5 us
    all_to_all x3 -> x0, blocking collectives: 62.8 us -> none  [exchange(): return lax.all_to_all(value, 'dp', split_axis=0, concat_axis=0, tiled=True)]
    ppermute x0 -> x28, starting transfers between devices: none -> 44.9 us  [travel(): lax.ppermute(value, 'dp', [(i, i ^ step) for i in range(owners)])]
    ppermute x0 -> x28, waiting for transfers between devices: none -> 7.88 us  [travel(): lax.ppermute(value, 'dp', [(i, i ^ step) for i in range(owners)])]
    all_to_all x1 -> x0, waiting for transfers between devices: 4.98 us -> none  [exchange(): return lax.all_to_all(value, 'dp', split_axis=0, concat_axis=0, tiled=True)]
    ppermute x4 -> x18, starting transfers between devices: 0.66 us -> 4.57 us  [other_core(): return lax.ppermute(value, 'space', [(0, 1), (1, 0)])]
    all_to_all x1 -> x0, starting transfers between devices: 3.54 us -> none  [exchange(): return lax.all_to_all(value, 'dp', split_axis=0, concat_axis=0, tiled=True)]
    unnamed x30 -> x60, local copies, waits for them, and re-layouts: 11.9 us -> 8.96 us
    pallas_call x7 -> x9, Pallas kernels: 45.6 us -> 47.5 us  [the longest x1 13.6 us: body(): pl.pallas_call(functools.partial(adam_kernel, len(owned)), out_shape=[who...]
  transfers between devices with their start and end apart: 5 -> 46, of which waited for: 4 -> 19; matrix products, arithmetic and copies ran while one was open for 0% -> 0% of each run, Pallas kernels for 14% -> 15%
where the time goes in v1:
time: 123 us; the launch traced here: 122 us
  starting transfers between devices  49.5 us (40%)
  Pallas kernels  47.5 us (39%)
  waiting for transfers between devices  13.8 us (11%)
  local copies, waits for them, and re-layouts  8.96 us (7%)
  other arithmetic  1.35 us (1%)
    ppermute x28, starting transfers between devices, travel(): lax.ppermute(value, 'dp', [(i, i ^ step) for i in range(owners)])  44.9 us
    pallas_call x1, Pallas kernels, body(): pl.pallas_call(functools.partial(adam_kernel, len(owned)), out_shape=[who...  13.6 us
    pallas_call x1, Pallas kernels, body(): pl.pallas_call(functools.partial(middle_kernel, back_order, order), out_s...  10.7 us
    unnamed x60, local copies, waits for them, and re-layouts  8.96 us
    pallas_call x2, Pallas kernels, mixing(): pl.pallas_call(functools.partial(mode_kernel, chunk, len(values)), out_sh...  8.57 us
    ppermute x28, waiting for transfers between devices, travel(): lax.ppermute(value, 'dp', [(i, i ^ step) for i in range(owners)])  7.88 us
    ppermute x18, waiting for transfers between devices, other_core(): return lax.ppermute(value, 'space', [(0, 1), (1, 0)])  5.92 us
    pallas_call x1, Pallas kernels, body(): pl.pallas_call(functools.partial(last_kernel, last_order), out_shape=jax....  4.99 us
  transfers between devices with their start and end apart: 46, of which 19 were waited for; matrix products, arithmetic and copies ran while one was open for 0% of the time, Pallas kernels for 15%

profile of v1, /device:TPU:0, one launch (start us, length us, event | category | flops | bytes accessed | tf_op | source)
XLA Modules:
  0.0 122.1 jit_solution(4858618713760974012)
XLA Ops:
  0.6 5.0 %first.1 = (f32[8,2,72,128]{3,2,1,0:T(8,128)}, f32[8,2,72,128]{3,2,1,0:T(8,128)}) custom-call(bf16[1,16,64,512]{3,2,1,0:T(8,128)(2,1)} %refs_0_, bf16[2,288,512]{2,1,0:T(8,128)(2,1)} %constant.20.clone.x_in, bf16[2,288,512]{2,1,0:T(8,128)(2,1)} %constant.18.clone.table_in.refs_18_.refs_19_), custom_call_target="tpu_custom_call" | custom-call | tf_op jit(solution)/shard_map/first/pallas_call | solution.py:496
  5.6 0.5 collective-permute-start
  6.1 1.8 %collective-permute-done = f32[8,2,72,128]{3,2,1,0:T(8,128)S(1)} collective-permute-done((f32[8,2,72,128]{3,2,1,0:T(8,128)}, f32[8,2,72,128]{3,2,1,0:T(8,128)S(1)}, u32[]{:S(2)}, u32[]{:S(2)}) %collective-permute-start) | collective-permute-done | bytes 589856 | tf_op jit(solution)/shard_map/ppermute | solution.py:489
  8.0 1.2 slice_add_fusion.8
  9.2 5.0 %collective-permute-start.6 = (f32[1,144,128]{2,1,0:T(8,128)S(1)}, f32[1,144,128]{2,1,0:T(8,128)S(1)}, u32[]{:S(2)}, u32[]{:S(2)}) collective-permute-start(f32[1,144,128]{2,1,0:T(8,128)S(1)} %bitcast.91), channel_id=1, source_target_pairs={{0,12},{2,14},{4,8},{6,10},{8,4},{10,6},{12,0},{14,2},{1,13},{3,15... | collective-permute-start | bytes 221192 | tf_op jit(solution)/shard_map/ppermute | solution.py:517
  14.2 1.1 collective-permute-start.7
  15.4 0.8 collective-permute-start.5
  16.1 2.0 %collective-permute-start.4 = (f32[1,144,128]{2,1,0:T(8,128)S(1)}, f32[1,144,128]{2,1,0:T(8,128)S(1)}, u32[]{:S(2)}, u32[]{:S(2)}) collective-permute-start(f32[1,144,128]{2,1,0:T(8,128)S(1)} %bitcast.87), channel_id=1, source_target_pairs={{0,8},{2,10},{4,12},{6,14},{8,0},{10,2},{12,4},{14,6},{1,9},{3,11}... | collective-permute-start | bytes 221192 | tf_op jit(solution)/shard_map/ppermute | solution.py:517
  18.1 2.3 %collective-permute-start.3 = (f32[1,144,128]{2,1,0:T(8,128)S(1)}, f32[1,144,128]{2,1,0:T(8,128)S(1)}, u32[]{:S(2)}, u32[]{:S(2)}) collective-permute-start(f32[1,144,128]{2,1,0:T(8,128)S(1)} %bitcast.85), channel_id=1, source_target_pairs={{0,6},{2,4},{4,2},{6,0},{8,14},{10,12},{12,10},{14,8},{1,7},{3,5},... | collective-permute-start | bytes 221192 | tf_op jit(solution)/shard_map/ppermute | solution.py:517
  20.4 0.8 collective-permute-start.2
  21.2 0.7 collective-permute-done.7.refs_7_
  21.9 1.7 %collective-permute-start.1 = (f32[1,144,128]{2,1,0:T(8,128)S(1)}, f32[1,144,128]{2,1,0:T(8,128)S(1)}, u32[]{:S(2)}, u32[]{:S(2)}) collective-permute-start(f32[1,144,128]{2,1,0:T(8,128)S(1)} %bitcast.81), channel_id=1, source_target_pairs={{0,2},{2,0},{4,6},{6,4},{8,10},{10,8},{12,14},{14,12},{1,3},{3,1},... | collective-permute-start | bytes 221192 | tf_op jit(solution)/shard_map/ppermute | solution.py:517
  23.7 2.3 %copy-done.25 = f32[1,16,9,64,128]{4,3,2,1,0:T(8,128)S(1)} copy-done((f32[1,16,9,64,128]{4,3,2,1,0:T(8,128)S(1)}, f32[1,16,9,64,128]{4,3,2,1,0:T(8,128)}, u32[]{:S(2)}) %copy-start.25) | copy-done | bytes 4718616
  26.0 0.6 split.1
  27.5 3.7 %mix.1 = (f32[1,144,128]{2,1,0:T(8,128)S(1)}, f32[1,144,128]{2,1,0:T(8,128)S(1)}, f32[1,144,128]{2,1,0:T(8,128)S(1)}, f32[1,144,128]{2,1,0:T(8,128)S(1)}, f32[1,...) custom-call(f32[1,144,128]{2,1,0:T(8,128)S(1)} %bitcast.40, ...), custom_call_target="tpu_custom_call" | custom-call | flops 1000000000 | bytes 100000 | tf_op jit(solution)/shard_map/mix/pallas_call | solution.py:541
  31.2 4.5 %collective-permute-start.8 = (f32[1,144,128]{2,1,0:T(8,128)S(1)}, f32[1,144,128]{2,1,0:T(8,128)S(1)}, u32[]{:S(2)}, u32[]{:S(2)}) collective-permute-start(f32[1,144,128]{2,1,0:T(8,128)S(1)} %get-tuple-element.74), channel_id=1, source_target_pairs={{0,8},{2,10},{4,12},{6,14},{8,0},{10,2},{12,4},{14,6},{1,9},{3,11}... | collective-permute-start | bytes 221192 | tf_op jit(solution)/shard_map/ppermute | solution.py:517
  36.0 2.1 %collective-permute-start.10 = (f32[1,144,128]{2,1,0:T(8,128)S(1)}, f32[1,144,128]{2,1,0:T(8,128)S(1)}, u32[]{:S(2)}, u32[]{:S(2)}) collective-permute-start(f32[1,144,128]{2,1,0:T(8,128)S(1)} %get-tuple-element.76), channel_id=1, source_target_pairs={{0,12},{2,14},{4,8},{6,10},{8,4},{10,6},{12,0},{14,2},{1,13},{3,15... | collective-permute-start | bytes 221192 | tf_op jit(solution)/shard_map/ppermute | solution.py:517
  38.2 2.3 %collective-permute-start.11 = (f32[1,144,128]{2,1,0:T(8,128)S(1)}, f32[1,144,128]{2,1,0:T(8,128)S(1)}, u32[]{:S(2)}, u32[]{:S(2)}) collective-permute-start(f32[1,144,128]{2,1,0:T(8,128)S(1)} %get-tuple-element.77), channel_id=1, source_target_pairs={{0,14},{2,12},{4,10},{6,8},{8,6},{10,4},{12,2},{14,0},{1,15},{3,13... | collective-permute-start | bytes 221192 | tf_op jit(solution)/shard_map/ppermute | solution.py:517
  40.5 2.7 %collective-permute-done.8 = f32[1,144,128]{2,1,0:T(8,128)S(1)} collective-permute-done((f32[1,144,128]{2,1,0:T(8,128)S(1)}, f32[1,144,128]{2,1,0:T(8,128)S(1)}, u32[]{:S(2)}, u32[]{:S(2)}) %collective-permute-start.8) | collective-permute-done | bytes 73760 | tf_op jit(solution)/shard_map/ppermute | solution.py:517
  43.2 2.7 %collective-permute-done.9 = f32[1,144,128]{2,1,0:T(8,128)S(1)} collective-permute-done((f32[1,144,128]{2,1,0:T(8,128)S(1)}, f32[1,144,128]{2,1,0:T(8,128)S(1)}, u32[]{:S(2)}, u32[]{:S(2)}) %collective-permute-start.9) | collective-permute-done | bytes 73760 | tf_op jit(solution)/shard_map/ppermute | solution.py:517
  45.9 1.2 %collective-permute-start.14 = (f32[1,144,128]{2,1,0:T(8,128)S(1)}, f32[1,144,128]{2,1,0:T(8,128)S(1)}, u32[]{:S(2)}, u32[]{:S(2)}) collective-permute-start(f32[1,144,128]{2,1,0:T(8,128)S(1)} %get-tuple-element.80), channel_id=1, source_target_pairs={{0,2},{2,0},{4,6},{6,4},{8,10},{10,8},{12,14},{14,12},{1,3},{3,1},... | collective-permute-start | bytes 221192 | tf_op jit(solution)/shard_map/ppermute | solution.py:517
  47.5 0.9 copy-done.4
  48.4 0.9 copy-done.6
  49.3 1.0 collective-permute-done.14
  50.3 0.5 collective-permute-start.15
  50.9 0.5 collective-permute-start.18
  53.4 1.2 copy-done.5
  54.6 1.2 copy-done.7
  55.7 10.7 %middle.1 = (f32[8,2,72,128]{3,2,1,0:T(8,128)S(1)}, f32[8,2,72,128]{3,2,1,0:T(8,128)S(1)}, bf16[16,64,512]{2,1,0:T(8,128)(2,1)S(1)}, bf16[16,64,512]{2,1,0:T(8,128)(2,1)S(1)}) custom-call(s32[2]{0:T(128)S(1)} %pad_add_fusion.place, f32[2,72,128]{2,1,0:T(8,128)S(1)} %bitcast.49, f32[2,72,128]{2,1,0:T(8,128)S(1)} %bitcast.51, f32[2,72,128]{2,1,0:T(8,128)S(1)} %bitcast.55, ...), custom_call_target="tpu_custom_call" | custom-call | tf_op jit(solution)/shard_map/middle/pallas_call | solution.py:580
  66.8 1.8 %collective-permute-done.23 = f32[8,2,72,128]{3,2,1,0:T(8,128)S(1)} collective-permute-done((f32[8,2,72,128]{3,2,1,0:T(8,128)S(1)}, f32[8,2,72,128]{3,2,1,0:T(8,128)S(1)}, u32[]{:S(2)}, u32[]{:S(2)}) %collective-permute-start.23) | collective-permute-done | bytes 589856 | tf_op jit(solution)/shard_map/ppermute | solution.py:489
  68.6 1.8 %collective-permute-start.29 = (f32[1,144,128]{2,1,0:T(8,128)S(1)}, f32[1,144,128]{2,1,0:T(8,128)S(1)}, u32[]{:S(2)}, u32[]{:S(2)}) collective-permute-start(f32[1,144,128]{2,1,0:T(8,128)S(1)} %bitcast.92), channel_id=1, source_target_pairs={{0,12},{2,14},{4,8},{6,10},{8,4},{10,6},{12,0},{14,2},{1,13},{3,15... | collective-permute-start | bytes 221192 | tf_op jit(solution)/shard_map/ppermute | solution.py:517
  70.5 2.6 %collective-permute-start.30 = (f32[1,144,128]{2,1,0:T(8,128)S(1)}, f32[1,144,128]{2,1,0:T(8,128)S(1)}, u32[]{:S(2)}, u32[]{:S(2)}) collective-permute-start(f32[1,144,128]{2,1,0:T(8,128)S(1)} %bitcast.90), channel_id=1, source_target_pairs={{0,14},{2,12},{4,10},{6,8},{8,6},{10,4},{12,2},{14,0},{1,15},{3,13... | collective-permute-start | bytes 221192 | tf_op jit(solution)/shard_map/ppermute | solution.py:517
  73.1 3.2 %collective-permute-start.27 = (f32[1,144,128]{2,1,0:T(8,128)S(1)}, f32[1,144,128]{2,1,0:T(8,128)S(1)}, u32[]{:S(2)}, u32[]{:S(2)}) collective-permute-start(f32[1,144,128]{2,1,0:T(8,128)S(1)} %bitcast.84), channel_id=1, source_target_pairs={{0,8},{2,10},{4,12},{6,14},{8,0},{10,2},{12,4},{14,6},{1,9},{3,11}... | collective-permute-start | bytes 221192 | tf_op jit(solution)/shard_map/ppermute | solution.py:517
  76.4 2.6 %collective-permute-start.25 = (f32[1,144,128]{2,1,0:T(8,128)S(1)}, f32[1,144,128]{2,1,0:T(8,128)S(1)}, u32[]{:S(2)}, u32[]{:S(2)}) collective-permute-start(f32[1,144,128]{2,1,0:T(8,128)S(1)} %bitcast.80), channel_id=1, source_target_pairs={{0,4},{2,6},{4,0},{6,2},{8,12},{10,14},{12,8},{14,10},{1,5},{3,7},... | collective-permute-start | bytes 221192 | tf_op jit(solution)/shard_map/ppermute | solution.py:517
  79.0 0.9 collective-permute-start.24
  79.9 2.3 %copy-done.26 = f32[1,16,9,64,128]{4,3,2,1,0:T(8,128)S(1)} copy-done((f32[1,16,9,64,128]{4,3,2,1,0:T(8,128)S(1)}, f32[1,16,9,64,128]{4,3,2,1,0:T(8,128)}, u32[]{:S(2)}) %copy-start.26) | copy-done | bytes 4718616
  82.2 3.7 %local.1 = (f32[16,64,512]{2,1,0:T(8,128)S(1)}, bf16[144,64,128]{2,1,0:T(8,128)(2,1)S(1)}, bf16[144,64,128]{2,1,0:T(8,128)(2,1)S(1)}) custom-call(bf16[16,64,512]{2,1,0:T(8,128)(2,1)S(1)} %get-tuple-element.106.slope_high, bf16[16,64,512]{2,1,0:T(8,128)(2,1)S(1)} %get-tuple-element.107.slope_low, f32[64,64]{1,0:T(8,128)S(1)} %copy-done.24, ...), custom_call_target="tpu_custom_call" | custom-call | flops 6000000000 | bytes 100000 | tf_op jit(solution)/shard_map/local/pallas_call | solution.py:598
  86.0 4.8 %adjoint.1 = (f32[1,144,128]{2,1,0:T(8,128)S(1)}, f32[1,144,128]{2,1,0:T(8,128)S(1)}, f32[1,144,128]{2,1,0:T(8,128)S(1)}, f32[1,144,128]{2,1,0:T(8,128)S(1)}, f3...) custom-call(f32[1,144,128]{2,1,0:T(8,128)S(1)} %bitcast.42, ...), custom_call_target="tpu_custom_call" | custom-call | flops 1000000000 | bytes 100000 | tf_op jit(solution)/shard_map/adjoint/pallas_call | solution.py:541
  90.9 1.2 collective-permute-start.31
  92.1 2.1 %collective-permute-start.33 = (f32[1,144,128]{2,1,0:T(8,128)S(1)}, f32[1,144,128]{2,1,0:T(8,128)S(1)}, u32[]{:S(2)}, u32[]{:S(2)}) collective-permute-start(f32[1,144,128]{2,1,0:T(8,128)S(1)} %get-tuple-element.113), channel_id=1, source_target_pairs={{0,8},{2,10},{4,12},{6,14},{8,0},{10,2},{12,4},{14,6},{1,9},{3,11}... | collective-permute-start | bytes 221192 | tf_op jit(solution)/shard_map/ppermute | solution.py:517
  94.3 1.1 collective-permute-start.34
  95.4 1.8 %collective-permute-start.35 = (f32[1,144,128]{2,1,0:T(8,128)S(1)}, f32[1,144,128]{2,1,0:T(8,128)S(1)}, u32[]{:S(2)}, u32[]{:S(2)}) collective-permute-start(f32[1,144,128]{2,1,0:T(8,128)S(1)} %get-tuple-element.115), channel_id=1, source_target_pairs={{0,12},{2,14},{4,8},{6,10},{8,4},{10,6},{12,0},{14,2},{1,13},{3,15... | collective-permute-start | bytes 221192 | tf_op jit(solution)/shard_map/ppermute | solution.py:517
  97.2 2.6 %collective-permute-start.36 = (f32[1,144,128]{2,1,0:T(8,128)S(1)}, f32[1,144,128]{2,1,0:T(8,128)S(1)}, u32[]{:S(2)}, u32[]{:S(2)}) collective-permute-start(f32[1,144,128]{2,1,0:T(8,128)S(1)} %get-tuple-element.116), channel_id=1, source_target_pairs={{0,14},{2,12},{4,10},{6,8},{8,6},{10,4},{12,2},{14,0},{1,15},{3,13... | collective-permute-start | bytes 221192 | tf_op jit(solution)/shard_map/ppermute | solution.py:517
  99.8 0.5 collective-permute-start.37
  100.3 13.6 %adam.1 = (f32[144,64,128]{2,1,0:T(8,128)}, f32[144,64,128]{2,1,0:T(8,128)}, f32[144,64,128]{2,1,0:T(8,128)}) custom-call(f32[1,144,128]{2,1,0:T(8,128)} %bitcast.41, f32[1,144,128]{2,1,0:T(8,128)} %copy-done.16, f32[1,144,128]{2,1,0:T(8,128)} %copy-done.15, f32[1,144,128]{2,1,0:T(8,128)} %copy-done.14, f32[1,144,128]{2,1,0:T(8,128)} %copy-done.13, ...), custom_call_target="tpu_custom_call" | custom-call | flops 10000000000 | bytes 30000000 | tf_op jit(solution)/shard_map/adam/pallas_call | solution.py:611
  114.1 0.5 collective-permute-start.38
  114.7 0.4 collective-permute-start.41
  117.1 5.0 %last.1 = bf16[1,16,64,512]{3,2,1,0:T(8,128)(2,1)} custom-call(s32[2]{0:T(128)S(1)} %pad_add_fusion.place, f32[2,72,128]{2,1,0:T(8,128)S(1)} %bitcast.53, f32[2,72,128]{2,1,0:T(8,128)S(1)} %bitcast.57, f32[2,72,128]{2,1,0:T(8,128)S(1)} %bitcast.61, f32[2,72,128]{2,1,0:T(8,128)S(1)} %bitcast.65, f32[2,72,128]{2,1,0:T(8,128)S(1)} %bitcast.67, ...), custom_call_target="tpu_custom_call" | custom-call | tf_op jit(solution)/shard_map/last/pallas_call | solution.py:624
  (116 shorter events, 6.2 us)
Async XLA Ops:
  5.6 2.4 %collective-permute-start = (f32[8,2,72,128]{3,2,1,0:T(8,128)}, f32[8,2,72,128]{3,2,1,0:T(8,128)S(1)}, u32[]{:S(2)}, u32[]{:S(2)}) collective-permute-start(f32[8,2,72,128]{3,2,1,0:T(8,128)} %get-tuple-element.71), channel_id=1, source_target_pairs={{0,1},{1,0},{2,3},{3,2},{4,5},{5,4},{6,7},{7,6},{8,9},{9,8},{10,11... | collective-permute-start | bytes 1769480 | tf_op jit(solution)/shard_map/ppermute | solution.py:489
  9.2 11.3 %collective-permute-start.6 = (f32[1,144,128]{2,1,0:T(8,128)S(1)}, f32[1,144,128]{2,1,0:T(8,128)S(1)}, u32[]{:S(2)}, u32[]{:S(2)}) collective-permute-start(f32[1,144,128]{2,1,0:T(8,128)S(1)} %bitcast.91), channel_id=1, source_target_pairs={{0,12},{2,14},{4,8},{6,10},{8,4},{10,6},{12,0},{14,2},{1,13},{3,15... | collective-permute-start | bytes 221192 | tf_op jit(solution)/shard_map/ppermute | solution.py:517
  14.2 7.7 %collective-permute-start.7 = (f32[1,144,128]{2,1,0:T(8,128)S(1)}, f32[1,144,128]{2,1,0:T(8,128)S(1)}, u32[]{:S(2)}, u32[]{:S(2)}) collective-permute-start(f32[1,144,128]{2,1,0:T(8,128)S(1)} %bitcast.89), channel_id=1, source_target_pairs={{0,14},{2,12},{4,10},{6,8},{8,6},{10,4},{12,2},{14,0},{1,15},{3,13... | collective-permute-start | bytes 221192 | tf_op jit(solution)/shard_map/ppermute | solution.py:517
  15.4 11.6 %collective-permute-start.5 = (f32[1,144,128]{2,1,0:T(8,128)S(1)}, f32[1,144,128]{2,1,0:T(8,128)S(1)}, u32[]{:S(2)}, u32[]{:S(2)}) collective-permute-start(f32[1,144,128]{2,1,0:T(8,128)S(1)} %bitcast.88), channel_id=1, source_target_pairs={{0,10},{2,8},{4,14},{6,12},{8,2},{10,0},{12,6},{14,4},{1,11},{3,9}... | collective-permute-start | bytes 221192 | tf_op jit(solution)/shard_map/ppermute | solution.py:517
  16.1 11.0 %collective-permute-start.4 = (f32[1,144,128]{2,1,0:T(8,128)S(1)}, f32[1,144,128]{2,1,0:T(8,128)S(1)}, u32[]{:S(2)}, u32[]{:S(2)}) collective-permute-start(f32[1,144,128]{2,1,0:T(8,128)S(1)} %bitcast.87), channel_id=1, source_target_pairs={{0,8},{2,10},{4,12},{6,14},{8,0},{10,2},{12,4},{14,6},{1,9},{3,11}... | collective-permute-start | bytes 221192 | tf_op jit(solution)/shard_map/ppermute | solution.py:517
  18.1 9.0 %collective-permute-start.3 = (f32[1,144,128]{2,1,0:T(8,128)S(1)}, f32[1,144,128]{2,1,0:T(8,128)S(1)}, u32[]{:S(2)}, u32[]{:S(2)}) collective-permute-start(f32[1,144,128]{2,1,0:T(8,128)S(1)} %bitcast.85), channel_id=1, source_target_pairs={{0,6},{2,4},{4,2},{6,0},{8,14},{10,12},{12,10},{14,8},{1,7},{3,5},... | collective-permute-start | bytes 221192 | tf_op jit(solution)/shard_map/ppermute | solution.py:517
  20.4 7.0 %collective-permute-start.2 = (f32[1,144,128]{2,1,0:T(8,128)S(1)}, f32[1,144,128]{2,1,0:T(8,128)S(1)}, u32[]{:S(2)}, u32[]{:S(2)}) collective-permute-start(f32[1,144,128]{2,1,0:T(8,128)S(1)} %bitcast.83), channel_id=1, source_target_pairs={{0,4},{2,6},{4,0},{6,2},{8,12},{10,14},{12,8},{14,10},{1,5},{3,7},... | collective-permute-start | bytes 221192 | tf_op jit(solution)/shard_map/ppermute | solution.py:517
  21.9 5.5 %collective-permute-start.1 = (f32[1,144,128]{2,1,0:T(8,128)S(1)}, f32[1,144,128]{2,1,0:T(8,128)S(1)}, u32[]{:S(2)}, u32[]{:S(2)}) collective-permute-start(f32[1,144,128]{2,1,0:T(8,128)S(1)} %bitcast.81), channel_id=1, source_target_pairs={{0,2},{2,0},{4,6},{6,4},{8,10},{10,8},{12,14},{14,12},{1,3},{3,1},... | collective-permute-start | bytes 221192 | tf_op jit(solution)/shard_map/ppermute | solution.py:517
  26.6 20.5 %copy-start.1 = (bf16[1,16,64,512]{3,2,1,0:T(8,128)(2,1)S(1)}, bf16[1,16,64,512]{3,2,1,0:T(8,128)(2,1)}, u32[]{:S(2)}) copy-start(bf16[1,16,64,512]{3,2,1,0:T(8,128)(2,1)} %refs_0_) | copy-start | bytes 3145732
  26.6 20.5 %copy-start.2 = (bf16[2,256,864]{2,1,0:T(8,128)(2,1)S(1)}, bf16[2,256,864]{2,1,0:T(8,128)(2,1)}, u32[]{:S(2)}) copy-start(bf16[2,256,864]{2,1,0:T(8,128)(2,1)} %constant.22.clone.refs_2_.refs_17_) | copy-start | bytes 2654212
  31.2 12.0 %collective-permute-start.8 = (f32[1,144,128]{2,1,0:T(8,128)S(1)}, f32[1,144,128]{2,1,0:T(8,128)S(1)}, u32[]{:S(2)}, u32[]{:S(2)}) collective-permute-start(f32[1,144,128]{2,1,0:T(8,128)S(1)} %get-tuple-element.74), channel_id=1, source_target_pairs={{0,8},{2,10},{4,12},{6,14},{8,0},{10,2},{12,4},{14,6},{1,9},{3,11}... | collective-permute-start | bytes 221192 | tf_op jit(solution)/shard_map/ppermute | solution.py:517
  35.7 10.2 %collective-permute-start.9 = (f32[1,144,128]{2,1,0:T(8,128)S(1)}, f32[1,144,128]{2,1,0:T(8,128)S(1)}, u32[]{:S(2)}, u32[]{:S(2)}) collective-permute-start(f32[1,144,128]{2,1,0:T(8,128)S(1)} %get-tuple-element.75), channel_id=1, source_target_pairs={{0,10},{2,8},{4,14},{6,12},{8,2},{10,0},{12,6},{14,4},{1,11},{3,9}... | collective-permute-start | bytes 221192 | tf_op jit(solution)/shard_map/ppermute | solution.py:517
  36.0 13.3 %collective-permute-start.10 = (f32[1,144,128]{2,1,0:T(8,128)S(1)}, f32[1,144,128]{2,1,0:T(8,128)S(1)}, u32[]{:S(2)}, u32[]{:S(2)}) collective-permute-start(f32[1,144,128]{2,1,0:T(8,128)S(1)} %get-tuple-element.76), channel_id=1, source_target_pairs={{0,12},{2,14},{4,8},{6,10},{8,4},{10,6},{12,0},{14,2},{1,13},{3,15... | collective-permute-start | bytes 221192 | tf_op jit(solution)/shard_map/ppermute | solution.py:517
  38.2 11.2 %collective-permute-start.11 = (f32[1,144,128]{2,1,0:T(8,128)S(1)}, f32[1,144,128]{2,1,0:T(8,128)S(1)}, u32[]{:S(2)}, u32[]{:S(2)}) collective-permute-start(f32[1,144,128]{2,1,0:T(8,128)S(1)} %get-tuple-element.77), channel_id=1, source_target_pairs={{0,14},{2,12},{4,10},{6,8},{8,6},{10,4},{12,2},{14,0},{1,15},{3,13... | collective-permute-start | bytes 221192 | tf_op jit(solution)/shard_map/ppermute | solution.py:517
  40.5 8.8 %collective-permute-start.12 = (f32[1,144,128]{2,1,0:T(8,128)S(1)}, f32[1,144,128]{2,1,0:T(8,128)S(1)}, u32[]{:S(2)}, u32[]{:S(2)}) collective-permute-start(f32[1,144,128]{2,1,0:T(8,128)S(1)} %get-tuple-element.78), channel_id=1, source_target_pairs={{0,6},{2,4},{4,2},{6,0},{8,14},{10,12},{12,10},{14,8},{1,7},{3,5},... | collective-permute-start | bytes 221192 | tf_op jit(solution)/shard_map/ppermute | solution.py:517
  43.2 6.1 %collective-permute-start.13 = (f32[1,144,128]{2,1,0:T(8,128)S(1)}, f32[1,144,128]{2,1,0:T(8,128)S(1)}, u32[]{:S(2)}, u32[]{:S(2)}) collective-permute-start(f32[1,144,128]{2,1,0:T(8,128)S(1)} %get-tuple-element.79), channel_id=1, source_target_pairs={{0,4},{2,6},{4,0},{6,2},{8,12},{10,14},{12,8},{14,10},{1,5},{3,7},... | collective-permute-start | bytes 221192 | tf_op jit(solution)/shard_map/ppermute | solution.py:517
  45.9 4.4 %collective-permute-start.14 = (f32[1,144,128]{2,1,0:T(8,128)S(1)}, f32[1,144,128]{2,1,0:T(8,128)S(1)}, u32[]{:S(2)}, u32[]{:S(2)}) collective-permute-start(f32[1,144,128]{2,1,0:T(8,128)S(1)} %get-tuple-element.80), channel_id=1, source_target_pairs={{0,2},{2,0},{4,6},{6,4},{8,10},{10,8},{12,14},{14,12},{1,3},{3,1},... | collective-permute-start | bytes 221192 | tf_op jit(solution)/shard_map/ppermute | solution.py:517
  50.3 1.3 %collective-permute-start.16 = (f32[2,72,128]{2,1,0:T(8,128)S(1)}, f32[2,72,128]{2,1,0:T(8,128)S(1)}, u32[]{:S(2)}, u32[]{:S(2)}) collective-permute-start(f32[2,72,128]{2,1,0:T(8,128)S(1)} %bitcast.50), channel_id=1, source_target_pairs={{0,1},{1,0},{2,3},{3,2},{4,5},{5,4},{6,7},{7,6},{8,9},{9,8},{10,11... | collective-permute-start | bytes 221192 | tf_op jit(solution)/shard_map/ppermute | solution.py:489
  50.3 1.5 %collective-permute-start.15 = (f32[2,72,128]{2,1,0:T(8,128)S(1)}, f32[2,72,128]{2,1,0:T(8,128)S(1)}, u32[]{:S(2)}, u32[]{:S(2)}) collective-permute-start(f32[2,72,128]{2,1,0:T(8,128)S(1)} %bitcast.48), channel_id=1, source_target_pairs={{0,1},{1,0},{2,3},{3,2},{4,5},{5,4},{6,7},{7,6},{8,9},{9,8},{10,11... | collective-permute-start | bytes 221192 | tf_op jit(solution)/shard_map/ppermute | solution.py:489
  50.9 1.3 %collective-permute-start.17 = (f32[2,72,128]{2,1,0:T(8,128)S(1)}, f32[2,72,128]{2,1,0:T(8,128)S(1)}, u32[]{:S(2)}, u32[]{:S(2)}) collective-permute-start(f32[2,72,128]{2,1,0:T(8,128)S(1)} %bitcast.54), channel_id=1, source_target_pairs={{0,1},{1,0},{2,3},{3,2},{4,5},{5,4},{6,7},{7,6},{8,9},{9,8},{10,11... | collective-permute-start | bytes 221192 | tf_op jit(solution)/shard_map/ppermute | solution.py:489
  50.9 1.6 %collective-permute-start.18 = (f32[2,72,128]{2,1,0:T(8,128)S(1)}, f32[2,72,128]{2,1,0:T(8,128)S(1)}, u32[]{:S(2)}, u32[]{:S(2)}) collective-permute-start(f32[2,72,128]{2,1,0:T(8,128)S(1)} %bitcast.58), channel_id=1, source_target_pairs={{0,1},{1,0},{2,3},{3,2},{4,5},{5,4},{6,7},{7,6},{8,9},{9,8},{10,11... | collective-permute-start | bytes 221192 | tf_op jit(solution)/shard_map/ppermute | solution.py:489
  51.4 1.3 %collective-permute-start.19 = (f32[2,72,128]{2,1,0:T(8,128)S(1)}, f32[2,72,128]{2,1,0:T(8,128)S(1)}, u32[]{:S(2)}, u32[]{:S(2)}) collective-permute-start(f32[2,72,128]{2,1,0:T(8,128)S(1)} %bitcast.62), channel_id=1, source_target_pairs={{0,1},{1,0},{2,3},{3,2},{4,5},{5,4},{6,7},{7,6},{8,9},{9,8},{10,11... | collective-permute-start | bytes 221192 | tf_op jit(solution)/shard_map/ppermute | solution.py:489
  51.6 1.3 %collective-permute-start.20 = (f32[2,72,128]{2,1,0:T(8,128)S(1)}, f32[2,72,128]{2,1,0:T(8,128)S(1)}, u32[]{:S(2)}, u32[]{:S(2)}) collective-permute-start(f32[2,72,128]{2,1,0:T(8,128)S(1)} %bitcast.68), channel_id=1, source_target_pairs={{0,1},{1,0},{2,3},{3,2},{4,5},{5,4},{6,7},{7,6},{8,9},{9,8},{10,11... | collective-permute-start | bytes 221192 | tf_op jit(solution)/shard_map/ppermute | solution.py:489
  51.9 1.3 %collective-permute-start.21 = (f32[2,72,128]{2,1,0:T(8,128)S(1)}, f32[2,72,128]{2,1,0:T(8,128)S(1)}, u32[]{:S(2)}, u32[]{:S(2)}) collective-permute-start(f32[2,72,128]{2,1,0:T(8,128)S(1)} %bitcast.72), channel_id=1, source_target_pairs={{0,1},{1,0},{2,3},{3,2},{4,5},{5,4},{6,7},{7,6},{8,9},{9,8},{10,11... | collective-permute-start | bytes 221192 | tf_op jit(solution)/shard_map/ppermute | solution.py:489
  52.1 1.3 %collective-permute-start.22 = (f32[2,72,128]{2,1,0:T(8,128)S(1)}, f32[2,72,128]{2,1,0:T(8,128)S(1)}, u32[]{:S(2)}, u32[]{:S(2)}) collective-permute-start(f32[2,72,128]{2,1,0:T(8,128)S(1)} %bitcast.44), channel_id=1, source_target_pairs={{0,1},{1,0},{2,3},{3,2},{4,5},{5,4},{6,7},{7,6},{8,9},{9,8},{10,11... | collective-permute-start | bytes 221192 | tf_op jit(solution)/shard_map/ppermute | solution.py:489
  66.5 2.1 %collective-permute-start.23 = (f32[8,2,72,128]{3,2,1,0:T(8,128)S(1)}, f32[8,2,72,128]{3,2,1,0:T(8,128)S(1)}, u32[]{:S(2)}, u32[]{:S(2)}) collective-permute-start(f32[8,2,72,128]{3,2,1,0:T(8,128)S(1)} %get-tuple-element.105), channel_id=1, source_target_pairs={{0,1},{1,0},{2,3},{3,2},{4,5},{5,4},{6,7},{7,6},{8,9},{9,8},{10,11... | collective-permute-start | bytes 1769480 | tf_op jit(solution)/shard_map/ppermute | solution.py:489
  68.6 7.7 %collective-permute-start.29 = (f32[1,144,128]{2,1,0:T(8,128)S(1)}, f32[1,144,128]{2,1,0:T(8,128)S(1)}, u32[]{:S(2)}, u32[]{:S(2)}) collective-permute-start(f32[1,144,128]{2,1,0:T(8,128)S(1)} %bitcast.92), channel_id=1, source_target_pairs={{0,12},{2,14},{4,8},{6,10},{8,4},{10,6},{12,0},{14,2},{1,13},{3,15... | collective-permute-start | bytes 221192 | tf_op jit(solution)/shard_map/ppermute | solution.py:517
  70.5 8.5 %collective-permute-start.30 = (f32[1,144,128]{2,1,0:T(8,128)S(1)}, f32[1,144,128]{2,1,0:T(8,128)S(1)}, u32[]{:S(2)}, u32[]{:S(2)}) collective-permute-start(f32[1,144,128]{2,1,0:T(8,128)S(1)} %bitcast.90), channel_id=1, source_target_pairs={{0,14},{2,12},{4,10},{6,8},{8,6},{10,4},{12,2},{14,0},{1,15},{3,13... | collective-permute-start | bytes 221192 | tf_op jit(solution)/shard_map/ppermute | solution.py:517
  73.1 12.8 %collective-permute-start.28 = (f32[1,144,128]{2,1,0:T(8,128)S(1)}, f32[1,144,128]{2,1,0:T(8,128)S(1)}, u32[]{:S(2)}, u32[]{:S(2)}) collective-permute-start(f32[1,144,128]{2,1,0:T(8,128)S(1)} %bitcast.86), channel_id=1, source_target_pairs={{0,10},{2,8},{4,14},{6,12},{8,2},{10,0},{12,6},{14,4},{1,11},{3,9}... | collective-permute-start | bytes 221192 | tf_op jit(solution)/shard_map/ppermute | solution.py:517
  73.1 12.8 %collective-permute-start.27 = (f32[1,144,128]{2,1,0:T(8,128)S(1)}, f32[1,144,128]{2,1,0:T(8,128)S(1)}, u32[]{:S(2)}, u32[]{:S(2)}) collective-permute-start(f32[1,144,128]{2,1,0:T(8,128)S(1)} %bitcast.84), channel_id=1, source_target_pairs={{0,8},{2,10},{4,12},{6,14},{8,0},{10,2},{12,4},{14,6},{1,9},{3,11}... | collective-permute-start | bytes 221192 | tf_op jit(solution)/shard_map/ppermute | solution.py:517
  76.4 9.5 %collective-permute-start.26 = (f32[1,144,128]{2,1,0:T(8,128)S(1)}, f32[1,144,128]{2,1,0:T(8,128)S(1)}, u32[]{:S(2)}, u32[]{:S(2)}) collective-permute-start(f32[1,144,128]{2,1,0:T(8,128)S(1)} %bitcast.82), channel_id=1, source_target_pairs={{0,6},{2,4},{4,2},{6,0},{8,14},{10,12},{12,10},{14,8},{1,7},{3,5},... | collective-permute-start | bytes 221192 | tf_op jit(solution)/shard_map/ppermute | solution.py:517
  76.4 9.6 %collective-permute-start.25 = (f32[1,144,128]{2,1,0:T(8,128)S(1)}, f32[1,144,128]{2,1,0:T(8,128)S(1)}, u32[]{:S(2)}, u32[]{:S(2)}) collective-permute-start(f32[1,144,128]{2,1,0:T(8,128)S(1)} %bitcast.80), channel_id=1, source_target_pairs={{0,4},{2,6},{4,0},{6,2},{8,12},{10,14},{12,8},{14,10},{1,5},{3,7},... | collective-permute-start | bytes 221192 | tf_op jit(solution)/shard_map/ppermute | solution.py:517
  79.0 7.0 %collective-permute-start.24 = (f32[1,144,128]{2,1,0:T(8,128)S(1)}, f32[1,144,128]{2,1,0:T(8,128)S(1)}, u32[]{:S(2)}, u32[]{:S(2)}) collective-permute-start(f32[1,144,128]{2,1,0:T(8,128)S(1)} %bitcast.79), channel_id=1, source_target_pairs={{0,2},{2,0},{4,6},{6,4},{8,10},{10,8},{12,14},{14,12},{1,3},{3,1},... | collective-permute-start | bytes 221192 | tf_op jit(solution)/shard_map/ppermute | solution.py:517
  90.9 6.3 %collective-permute-start.31 = (f32[1,144,128]{2,1,0:T(8,128)S(1)}, f32[1,144,128]{2,1,0:T(8,128)S(1)}, u32[]{:S(2)}, u32[]{:S(2)}) collective-permute-start(f32[1,144,128]{2,1,0:T(8,128)S(1)} %get-tuple-element.111), channel_id=1, source_target_pairs={{0,2},{2,0},{4,6},{6,4},{8,10},{10,8},{12,14},{14,12},{1,3},{3,1},... | collective-permute-start | bytes 221192 | tf_op jit(solution)/shard_map/ppermute | solution.py:517
  92.1 7.7 %collective-permute-start.32 = (f32[1,144,128]{2,1,0:T(8,128)S(1)}, f32[1,144,128]{2,1,0:T(8,128)S(1)}, u32[]{:S(2)}, u32[]{:S(2)}) collective-permute-start(f32[1,144,128]{2,1,0:T(8,128)S(1)} %get-tuple-element.112), channel_id=1, source_target_pairs={{0,4},{2,6},{4,0},{6,2},{8,12},{10,14},{12,8},{14,10},{1,5},{3,7},... | collective-permute-start | bytes 221192 | tf_op jit(solution)/shard_map/ppermute | solution.py:517
  92.1 21.8 %collective-permute-start.33 = (f32[1,144,128]{2,1,0:T(8,128)S(1)}, f32[1,144,128]{2,1,0:T(8,128)S(1)}, u32[]{:S(2)}, u32[]{:S(2)}) collective-permute-start(f32[1,144,128]{2,1,0:T(8,128)S(1)} %get-tuple-element.113), channel_id=1, source_target_pairs={{0,8},{2,10},{4,12},{6,14},{8,0},{10,2},{12,4},{14,6},{1,9},{3,11}... | collective-permute-start | bytes 221192 | tf_op jit(solution)/shard_map/ppermute | solution.py:517
  94.3 19.7 %collective-permute-start.34 = (f32[1,144,128]{2,1,0:T(8,128)S(1)}, f32[1,144,128]{2,1,0:T(8,128)S(1)}, u32[]{:S(2)}, u32[]{:S(2)}) collective-permute-start(f32[1,144,128]{2,1,0:T(8,128)S(1)} %get-tuple-element.114), channel_id=1, source_target_pairs={{0,10},{2,8},{4,14},{6,12},{8,2},{10,0},{12,6},{14,4},{1,11},{3,9}... | collective-permute-start | bytes 221192 | tf_op jit(solution)/shard_map/ppermute | solution.py:517
  95.4 18.6 %collective-permute-start.35 = (f32[1,144,128]{2,1,0:T(8,128)S(1)}, f32[1,144,128]{2,1,0:T(8,128)S(1)}, u32[]{:S(2)}, u32[]{:S(2)}) collective-permute-start(f32[1,144,128]{2,1,0:T(8,128)S(1)} %get-tuple-element.115), channel_id=1, source_target_pairs={{0,12},{2,14},{4,8},{6,10},{8,4},{10,6},{12,0},{14,2},{1,13},{3,15... | collective-permute-start | bytes 221192 | tf_op jit(solution)/shard_map/ppermute | solution.py:517
  97.2 16.8 %collective-permute-start.36 = (f32[1,144,128]{2,1,0:T(8,128)S(1)}, f32[1,144,128]{2,1,0:T(8,128)S(1)}, u32[]{:S(2)}, u32[]{:S(2)}) collective-permute-start(f32[1,144,128]{2,1,0:T(8,128)S(1)} %get-tuple-element.116), channel_id=1, source_target_pairs={{0,14},{2,12},{4,10},{6,8},{8,6},{10,4},{12,2},{14,0},{1,15},{3,13... | collective-permute-start | bytes 221192 | tf_op jit(solution)/shard_map/ppermute | solution.py:517
  99.8 14.2 %collective-permute-start.37 = (f32[1,144,128]{2,1,0:T(8,128)S(1)}, f32[1,144,128]{2,1,0:T(8,128)S(1)}, u32[]{:S(2)}, u32[]{:S(2)}) collective-permute-start(f32[1,144,128]{2,1,0:T(8,128)S(1)} %get-tuple-element.117), channel_id=1, source_target_pairs={{0,6},{2,4},{4,2},{6,0},{8,14},{10,12},{12,10},{14,8},{1,7},{3,5},... | collective-permute-start | bytes 221192 | tf_op jit(solution)/shard_map/ppermute | solution.py:517
  114.0 1.3 %collective-permute-start.39 = (f32[2,72,128]{2,1,0:T(8,128)S(1)}, f32[2,72,128]{2,1,0:T(8,128)S(1)}, u32[]{:S(2)}, u32[]{:S(2)}) collective-permute-start(f32[2,72,128]{2,1,0:T(8,128)S(1)} %bitcast.56), channel_id=1, source_target_pairs={{0,1},{1,0},{2,3},{3,2},{4,5},{5,4},{6,7},{7,6},{8,9},{9,8},{10,11... | collective-permute-start | bytes 221192 | tf_op jit(solution)/shard_map/ppermute | solution.py:489
  114.1 1.5 %collective-permute-start.38 = (f32[2,72,128]{2,1,0:T(8,128)S(1)}, f32[2,72,128]{2,1,0:T(8,128)S(1)}, u32[]{:S(2)}, u32[]{:S(2)}) collective-permute-start(f32[2,72,128]{2,1,0:T(8,128)S(1)} %bitcast.52), channel_id=1, source_target_pairs={{0,1},{1,0},{2,3},{3,2},{4,5},{5,4},{6,7},{7,6},{8,9},{9,8},{10,11... | collective-permute-start | bytes 221192 | tf_op jit(solution)/shard_map/ppermute | solution.py:489
  114.6 1.3 %collective-permute-start.40 = (f32[2,72,128]{2,1,0:T(8,128)S(1)}, f32[2,72,128]{2,1,0:T(8,128)S(1)}, u32[]{:S(2)}, u32[]{:S(2)}) collective-permute-start(f32[2,72,128]{2,1,0:T(8,128)S(1)} %bitcast.60), channel_id=1, source_target_pairs={{0,1},{1,0},{2,3},{3,2},{4,5},{5,4},{6,7},{7,6},{8,9},{9,8},{10,11... | collective-permute-start | bytes 221192 | tf_op jit(solution)/shard_map/ppermute | solution.py:489
  114.7 1.5 %collective-permute-start.41 = (f32[2,72,128]{2,1,0:T(8,128)S(1)}, f32[2,72,128]{2,1,0:T(8,128)S(1)}, u32[]{:S(2)}, u32[]{:S(2)}) collective-permute-start(f32[2,72,128]{2,1,0:T(8,128)S(1)} %bitcast.64), channel_id=1, source_target_pairs={{0,1},{1,0},{2,3},{3,2},{4,5},{5,4},{6,7},{7,6},{8,9},{9,8},{10,11... | collective-permute-start | bytes 221192 | tf_op jit(solution)/shard_map/ppermute | solution.py:489
  115.1 1.3 %collective-permute-start.42 = (f32[2,72,128]{2,1,0:T(8,128)S(1)}, f32[2,72,128]{2,1,0:T(8,128)S(1)}, u32[]{:S(2)}, u32[]{:S(2)}) collective-permute-start(f32[2,72,128]{2,1,0:T(8,128)S(1)} %bitcast.66), channel_id=1, source_target_pairs={{0,1},{1,0},{2,3},{3,2},{4,5},{5,4},{6,7},{7,6},{8,9},{9,8},{10,11... | collective-permute-start | bytes 221192 | tf_op jit(solution)/shard_map/ppermute | solution.py:489
  115.3 1.3 %collective-permute-start.43 = (f32[2,72,128]{2,1,0:T(8,128)S(1)}, f32[2,72,128]{2,1,0:T(8,128)S(1)}, u32[]{:S(2)}, u32[]{:S(2)}) collective-permute-start(f32[2,72,128]{2,1,0:T(8,128)S(1)} %bitcast.70), channel_id=1, source_target_pairs={{0,1},{1,0},{2,3},{3,2},{4,5},{5,4},{6,7},{7,6},{8,9},{9,8},{10,11... | collective-permute-start | bytes 221192 | tf_op jit(solution)/shard_map/ppermute | solution.py:489
  115.6 1.3 %collective-permute-start.44 = (f32[2,72,128]{2,1,0:T(8,128)S(1)}, f32[2,72,128]{2,1,0:T(8,128)S(1)}, u32[]{:S(2)}, u32[]{:S(2)}) collective-permute-start(f32[2,72,128]{2,1,0:T(8,128)S(1)} %bitcast.74), channel_id=1, source_target_pairs={{0,1},{1,0},{2,3},{3,2},{4,5},{5,4},{6,7},{7,6},{8,9},{9,8},{10,11... | collective-permute-start | bytes 221192 | tf_op jit(solution)/shard_map/ppermute | solution.py:489
  115.8 1.3 %collective-permute-start.45 = (f32[2,72,128]{2,1,0:T(8,128)S(1)}, f32[2,72,128]{2,1,0:T(8,128)S(1)}, u32[]{:S(2)}, u32[]{:S(2)}) collective-permute-start(f32[2,72,128]{2,1,0:T(8,128)S(1)} %bitcast.46), channel_id=1, source_target_pairs={{0,1},{1,0},{2,3},{3,2},{4,5},{5,4},{6,7},{7,6},{8,9},{9,8},{10,11... | collective-permute-start | bytes 221192 | tf_op jit(solution)/shard_map/ppermute | solution.py:489
  (28 other events, 341.3 us)

commit v2 on v1

--- a/solution.py
+++ b/solution.py
@@ -234,7 +234,7 @@
     root = math.sqrt(2.0 / math.pi)
     mixer = jnp.concatenate(split(pointwise[...].T), axis=0)
 
-    @pl.loop(0, width)
+    @pl.loop(0, width, unroll=4)
     def _(x):
         local = dot(mixer, field[x])
         value = pre[x] + (local[:channels] + local[channels:])
@@ -276,7 +276,7 @@
     high, low = split(pointwise[...])
     both = jnp.concatenate([high, low], axis=0)
 
-    @pl.loop(0, out.shape[0])
+    @pl.loop(0, out.shape[0], unroll=4)
     def _(x):
         wide = dot(both, high_in[x])
         out[x] = (wide[:channels] + wide[channels:]) + dot(high, low_in[x])
@@ -308,7 +308,7 @@
 
 
 def mode_chunk(modes):
-    return 16 if modes % 16 == 0 else modes
+    return 72 if modes % 72 == 0 else modes
 
 
 def stack(refs, target):
@@ -340,10 +340,11 @@
         high[at], low[at] = split(weight[at])
 
 
-def hold_kernel(*refs):
-    number = len(refs) // 2
-    for source, target in zip(refs[:number], refs[number:]):
-        target[...] = source[...]
+def hold_kernel(field, cotangent, x_inverse, x_forward, table, *targets):
+    space = lax.axis_index("space")
+    values = [field[0], cotangent[0], x_inverse[space], x_forward[space], table[space], table[1 - space]]
+    for target, value in zip(targets, values):
+        target[...] = value
 
 
 def mode_kernel(one_chunk, number, *refs):
@@ -415,9 +416,13 @@
 def adam_kernel(number, *refs):
     spectra_parts, slope_parts, refs = refs[:number], refs[number : 2 * number], refs[2 * number :]
     weight, first, second, weight_out, first_out, second_out, spectra, slopes = refs
-    stack(spectra_parts, spectra)
-    stack(slope_parts, slopes)
     samples, modes, width = spectra.shape
+    here = pl.ds(pl.multiple_of(pl.program_id(0) * modes, 8) if modes % 8 == 0 else 0, modes)
+    for parts, target in ((spectra_parts, spectra), (slope_parts, slopes)):
+        base = 0
+        for part in parts:
+            target[pl.ds(base, part.shape[0])] = part[:, here, :]
+            base += part.shape[0]
     lower = lower_half((samples, width))
     sign = lane_sign((samples, width), 1.0)
     for group in pairs_of(modes):
@@ -561,20 +566,9 @@
             name="split",
         )(weight)
 
-    def hold(*values):
-        return pl.pallas_call(
-            hold_kernel,
-            out_shape=[jax.ShapeDtypeStruct(value.shape, value.dtype) for value in values],
-            compiler_params=mode_params,
-            cost_estimate=estimate(6),
-            name="hold",
-        )(*values)
-
     owned = to_owners(own, sent)
     mixture = list(mixing(mix_chunk, owned, split_weights(weight), "mix"))
-    mixture[0], field_in, cotangent = lax.optimization_barrier((mixture[0], inputs, cotangent))
-    held = hold(field_in, cotangent, x_inverse, x_forward, scaled_table)
-    mixed, held = from_owners(mixture, back_order, held)
+    mixed, _ = from_owners(mixture, back_order)
 
     field = jax.ShapeDtypeStruct(field_shape, bf16)
     own, sent, slope_high, slope_low = pl.pallas_call(
@@ -592,7 +586,7 @@
         ),
         compiler_params=params,
         name="middle",
-    )(place, *mixed, *held[:2], pointwise_weight, *held[2:], held[4])
+    )(place, *mixed, inputs, cotangent, pointwise_weight, x_inverse, x_forward, scaled_table, scaled_table)
     again, own = lax.optimization_barrier((weight, own))
     slopes = to_owners(own, sent)
     local, *weights = pl.pallas_call(
@@ -607,7 +601,7 @@
     block = 24 if modes % 24 == 0 else modes
     whole = jax.ShapeDtypeStruct(weight_shape, f32)
     weight_spec = pl.BlockSpec((block, channels, lanes), lambda i: (i, 0, 0))
-    value_specs = [pl.BlockSpec((value.shape[0], block, lanes), lambda i: (0, i, 0)) for value in owned]
+    value_specs = [pl.BlockSpec(value.shape, lambda i: (0, 0, 0)) for value in owned]
     new_weight, new_first, new_second = pl.pallas_call(
         functools.partial(adam_kernel, len(owned)),
         out_shape=[whole] * 3,
@@ -615,7 +609,7 @@
         in_specs=value_specs * 2 + [weight_spec] * 3,
         out_specs=[weight_spec] * 3,
         scratch_shapes=[pltpu.VMEM((owners, block, lanes), f32)] * 2,
-        compiler_params=pltpu.CompilerParams(vmem_limit_bytes=56 * 1024 * 1024),
+        compiler_params=pltpu.CompilerParams(vmem_limit_bytes=30 * 1024 * 1024),
         cost_estimate=pl.CostEstimate(flops=10**10, bytes_accessed=3 * 10**7, transcendentals=10**6),
         name="adam",
     )(*owned, *slopes, weight, first_moment.reshape(weight_shape), second_moment.reshape(weight_shape))

time: 123 us -> 110 us (0.89)
  Pallas kernels: 47.5 us -> 36.1 us
  local copies, waits for them, and re-layouts: 8.96 us -> 3.67 us
  waiting for transfers between devices: 13.8 us -> 18.6 us
    pallas_call x1, Pallas kernels: 13.6 us -> 7.5 us  [body(): pl.pallas_call(functools.partial(adam_kernel, len(owned)), out_shape=[who...]
    unnamed x60 -> x54, local copies, waits for them, and re-layouts: 8.96 us -> 3.67 us
    ppermute x28, waiting for transfers between devices: 7.88 us -> 12.9 us  [travel(): lax.ppermute(value, 'dp', [(i, i ^ step) for i in range(owners)])]
    pallas_call x2, Pallas kernels: 8.57 us -> 5.77 us  [mixing(): pl.pallas_call(functools.partial(mode_kernel, chunk, len(values)), out_sh...]
    pallas_call x1, Pallas kernels: 3.66 us -> 1.95 us  [body(): pl.pallas_call(local_split_kernel, out_shape=[jax.ShapeDtypeStruct(field_...]
  transfers between devices with their start and end apart: 46 -> 46, of which waited for: 19 -> 23; matrix products, arithmetic and copies ran while one was open for 0% -> 0% of each run, Pallas kernels for 15% -> 9%
where the time goes in v2:
time: 110 us
  starting transfers between devices  49.5 us (45%)
  Pallas kernels  36.1 us (33%)
  waiting for transfers between devices  18.6 us (17%)
  local copies, waits for them, and re-layouts  3.67 us (3%)
  other arithmetic  1.35 us (1%)
    ppermute x28, starting transfers between devices, travel(): lax.ppermute(value, 'dp', [(i, i ^ step) for i in range(owners)])  44.8 us
    ppermute x28, waiting for transfers between devices, travel(): lax.ppermute(value, 'dp', [(i, i ^ step) for i in range(owners)])  12.9 us
    pallas_call x1, Pallas kernels, body(): pl.pallas_call(functools.partial(middle_kernel, back_order, order), out_s...  10.3 us
    pallas_call x1, Pallas kernels, body(): pl.pallas_call(functools.partial(adam_kernel, len(owned)), out_shape=[who...  7.5 us
    pallas_call x2, Pallas kernels, mixing(): pl.pallas_call(functools.partial(mode_kernel, chunk, len(values)), out_sh...  5.77 us
    ppermute x18, waiting for transfers between devices, other_core(): return lax.ppermute(value, 'space', [(0, 1), (1, 0)])  5.7 us
    pallas_call x1, Pallas kernels, body(): pl.pallas_call(functools.partial(first_kernel, order), out_shape=[part_ty...  4.98 us
    pallas_call x1, Pallas kernels, body(): pl.pallas_call(functools.partial(last_kernel, last_order), out_shape=jax....  4.98 us
  transfers between devices with their start and end apart: 46, of which 23 were waited for; matrix products, arithmetic and copies ran while one was open for 0% of the time, Pallas kernels for 9%

profile of v2, /device:TPU:0, one launch (start us, length us, event | category | flops | bytes accessed | tf_op | source)
XLA Modules:
  0.0 110.2 jit_solution(17357686698493168830)
XLA Ops:
  0.6 5.0 %first.1 = (f32[8,2,72,128]{3,2,1,0:T(8,128)}, f32[8,2,72,128]{3,2,1,0:T(8,128)}) custom-call(bf16[1,16,64,512]{3,2,1,0:T(8,128)(2,1)} %refs_16_.1, bf16[2,288,512]{2,1,0:T(8,128)(2,1)} %constant.20.clone.x_in, bf16[2,288,512]{2,1,0:T(8,128)(2,1)} %constant.18.clone.table_in.refs_18_.refs_19_), custom_call_target="tpu_custom_call" | custom-call | tf_op jit(solution)/shard_map/first/pallas_call | solution.py:501
  5.6 0.5 collective-permute-start
  6.1 1.8 %collective-permute-done = f32[8,2,72,128]{3,2,1,0:T(8,128)S(1)} collective-permute-done((f32[8,2,72,128]{3,2,1,0:T(8,128)}, f32[8,2,72,128]{3,2,1,0:T(8,128)S(1)}, u32[]{:S(2)}, u32[]{:S(2)}) %collective-permute-start) | collective-permute-done | bytes 589856 | tf_op jit(solution)/shard_map/ppermute | solution.py:494
  8.0 1.2 %slice_add_fusion.8 = (f32[1,2,72,128]{3,2,1,0:T(8,128)S(1)}, f32[1,2,72,128]{3,2,1,0:T(8,128)S(1)}, f32[1,2,72,128]{3,2,1,0:T(8,128)S(1)}, f32[1,2,72,128]{3,2,...) fusion(f32[8,2,72,128]{3,2,1,0:T(8,128)S(1)} %collective-permut, ...), kind=kLoop, calls=%fused_computation.8 | loop fusion | flops 147456 | bytes 1769472 | tf_op jit(solution)/shard_map/add | solution.py:528
  9.2 5.0 %collective-permute-start.6 = (f32[1,144,128]{2,1,0:T(8,128)S(1)}, f32[1,144,128]{2,1,0:T(8,128)S(1)}, u32[]{:S(2)}, u32[]{:S(2)}) collective-permute-start(f32[1,144,128]{2,1,0:T(8,128)S(1)} %bitcast.81), channel_id=1, source_target_pairs={{0,12},{2,14},{4,8},{6,10},{8,4},{10,6},{12,0},{14,2},{1,13},{3,15... | collective-permute-start | bytes 221192 | tf_op jit(solution)/shard_map/ppermute | solution.py:522
  14.2 1.1 %collective-permute-start.7 = (f32[1,144,128]{2,1,0:T(8,128)S(1)}, f32[1,144,128]{2,1,0:T(8,128)S(1)}, u32[]{:S(2)}, u32[]{:S(2)}) collective-permute-start(f32[1,144,128]{2,1,0:T(8,128)S(1)} %bitcast.79), channel_id=1, source_target_pairs={{0,14},{2,12},{4,10},{6,8},{8,6},{10,4},{12,2},{14,0},{1,15},{3,13... | collective-permute-start | bytes 221192 | tf_op jit(solution)/shard_map/ppermute | solution.py:522
  15.4 0.8 collective-permute-start.5
  16.1 2.0 %collective-permute-start.4 = (f32[1,144,128]{2,1,0:T(8,128)S(1)}, f32[1,144,128]{2,1,0:T(8,128)S(1)}, u32[]{:S(2)}, u32[]{:S(2)}) collective-permute-start(f32[1,144,128]{2,1,0:T(8,128)S(1)} %bitcast.77), channel_id=1, source_target_pairs={{0,8},{2,10},{4,12},{6,14},{8,0},{10,2},{12,4},{14,6},{1,9},{3,11}... | collective-permute-start | bytes 221192 | tf_op jit(solution)/shard_map/ppermute | solution.py:522
  18.1 2.3 %collective-permute-start.3 = (f32[1,144,128]{2,1,0:T(8,128)S(1)}, f32[1,144,128]{2,1,0:T(8,128)S(1)}, u32[]{:S(2)}, u32[]{:S(2)}) collective-permute-start(f32[1,144,128]{2,1,0:T(8,128)S(1)} %bitcast.75), channel_id=1, source_target_pairs={{0,6},{2,4},{4,2},{6,0},{8,14},{10,12},{12,10},{14,8},{1,7},{3,5},... | collective-permute-start | bytes 221192 | tf_op jit(solution)/shard_map/ppermute | solution.py:522
  20.4 0.8 collective-permute-start.2
  21.2 0.7 collective-permute-done.7.refs_7_
  21.9 1.7 %collective-permute-start.1 = (f32[1,144,128]{2,1,0:T(8,128)S(1)}, f32[1,144,128]{2,1,0:T(8,128)S(1)}, u32[]{:S(2)}, u32[]{:S(2)}) collective-permute-start(f32[1,144,128]{2,1,0:T(8,128)S(1)} %bitcast.71), channel_id=1, source_target_pairs={{0,2},{2,0},{4,6},{6,4},{8,10},{10,8},{12,14},{14,12},{1,3},{3,1},... | collective-permute-start | bytes 221192 | tf_op jit(solution)/shard_map/ppermute | solution.py:522
  23.7 2.3 %copy-done.21 = f32[1,16,9,64,128]{4,3,2,1,0:T(8,128)S(1)} copy-done((f32[1,16,9,64,128]{4,3,2,1,0:T(8,128)S(1)}, f32[1,16,9,64,128]{4,3,2,1,0:T(8,128)}, u32[]{:S(2)}) %copy-start.21) | copy-done | bytes 4718616
  26.0 0.6 split.1
  27.4 2.5 %mix.1 = (f32[1,144,128]{2,1,0:T(8,128)}, f32[1,144,128]{2,1,0:T(8,128)}, f32[1,144,128]{2,1,0:T(8,128)}, f32[1,144,128]{2,1,0:T(8,128)S(1)}, f32[1,144,128]{2,1...) custom-call(f32[1,144,128]{2,1,0:T(8,128)S(1)} %bitcast.40, ...), custom_call_target="tpu_custom_call" | custom-call | flops 1000000000 | bytes 100000 | tf_op jit(solution)/shard_map/mix/pallas_call | solution.py:546
  30.0 4.4 %collective-permute-start.8 = (f32[1,144,128]{2,1,0:T(8,128)S(1)}, f32[1,144,128]{2,1,0:T(8,128)}, u32[]{:S(2)}, u32[]{:S(2)}) collective-permute-start(f32[1,144,128]{2,1,0:T(8,128)S(1)} %get-tuple-element.53), channel_id=1, source_target_pairs={{0,8},{2,10},{4,12},{6,14},{8,0},{10,2},{12,4},{14,6},{1,9},{3,11}... | collective-permute-start | bytes 221192 | tf_op jit(solution)/shard_map/ppermute | solution.py:522
  34.8 2.1 %collective-permute-start.10 = (f32[1,144,128]{2,1,0:T(8,128)S(1)}, f32[1,144,128]{2,1,0:T(8,128)}, u32[]{:S(2)}, u32[]{:S(2)}) collective-permute-start(f32[1,144,128]{2,1,0:T(8,128)S(1)} %get-tuple-element.55), channel_id=1, source_target_pairs={{0,12},{2,14},{4,8},{6,10},{8,4},{10,6},{12,0},{14,2},{1,13},{3,15... | collective-permute-start | bytes 221192 | tf_op jit(solution)/shard_map/ppermute | solution.py:522
  36.9 2.3 %collective-permute-start.11 = (f32[1,144,128]{2,1,0:T(8,128)S(1)}, f32[1,144,128]{2,1,0:T(8,128)}, u32[]{:S(2)}, u32[]{:S(2)}) collective-permute-start(f32[1,144,128]{2,1,0:T(8,128)S(1)} %get-tuple-element.56), channel_id=1, source_target_pairs={{0,14},{2,12},{4,10},{6,8},{8,6},{10,4},{12,2},{14,0},{1,15},{3,13... | collective-permute-start | bytes 221192 | tf_op jit(solution)/shard_map/ppermute | solution.py:522
  39.2 2.8 %collective-permute-done.8 = f32[1,144,128]{2,1,0:T(8,128)} collective-permute-done((f32[1,144,128]{2,1,0:T(8,128)S(1)}, f32[1,144,128]{2,1,0:T(8,128)}, u32[]{:S(2)}, u32[]{:S(2)}) %collective-permute-start.8) | collective-permute-done | bytes 73760 | tf_op jit(solution)/shard_map/ppermute | solution.py:522
  42.1 2.7 %collective-permute-done.9 = f32[1,144,128]{2,1,0:T(8,128)} collective-permute-done((f32[1,144,128]{2,1,0:T(8,128)S(1)}, f32[1,144,128]{2,1,0:T(8,128)}, u32[]{:S(2)}, u32[]{:S(2)}) %collective-permute-start.9) | collective-permute-done | bytes 73760 | tf_op jit(solution)/shard_map/ppermute | solution.py:522
  44.7 1.2 %collective-permute-start.14 = (f32[1,144,128]{2,1,0:T(8,128)}, f32[1,144,128]{2,1,0:T(8,128)}, u32[]{:S(2)}, u32[]{:S(2)}) collective-permute-start(f32[1,144,128]{2,1,0:T(8,128)} %get-tuple-element.59), channel_id=1, source_target_pairs={{0,2},{2,0},{4,6},{6,4},{8,10},{10,8},{12,14},{14,12},{1,3},{3,1},... | collective-permute-start | bytes 221192 | tf_op jit(solution)/shard_map/ppermute | solution.py:522
  45.9 0.5 collective-permute-start.15
  46.9 2.5 %collective-permute-done.14 = f32[1,144,128]{2,1,0:T(8,128)} collective-permute-done((f32[1,144,128]{2,1,0:T(8,128)}, f32[1,144,128]{2,1,0:T(8,128)}, u32[]{:S(2)}, u32[]{:S(2)}) %collective-permute-start.14) | collective-permute-done | bytes 73760 | tf_op jit(solution)/shard_map/ppermute | solution.py:522
  49.4 0.5 collective-permute-start.19
  50.0 0.4 collective-permute-start.21
  51.6 1.2 %copy-done.4 = bf16[1,16,64,512]{3,2,1,0:T(8,128)(2,1)S(1)} copy-done((bf16[1,16,64,512]{3,2,1,0:T(8,128)(2,1)S(1)}, bf16[1,16,64,512]{3,2,1,0:T(8,128)(2,1)}, u32[]{:S(2)}) %copy-start.4) | copy-done | bytes 1048600
  52.8 10.3 %middle.1 = (f32[8,2,72,128]{3,2,1,0:T(8,128)S(1)}, f32[8,2,72,128]{3,2,1,0:T(8,128)S(1)}, bf16[16,64,512]{2,1,0:T(8,128)(2,1)S(1)}, bf16[16,64,512]{2,1,0:T(8,128)(2,1)S(1)}) custom-call(s32[2]{0:T(128)S(1)} %pad_add_fusion.place, f32[2,72,128]{2,1,0:T(8,128)} %bitcast.11.refs_0_, f32[2,72,128]{2,1,0:T(8,128)} %bitcast.12.refs_1_, ...), custom_call_target="tpu_custom_call" | custom-call | tf_op jit(solution)/shard_map/middle/pallas_call | solution.py:574
  63.1 0.4 collective-permute-start.23
  63.6 1.6 %collective-permute-done.23 = f32[8,2,72,128]{3,2,1,0:T(8,128)S(1)} collective-permute-done((f32[8,2,72,128]{3,2,1,0:T(8,128)S(1)}, f32[8,2,72,128]{3,2,1,0:T(8,128)S(1)}, u32[]{:S(2)}, u32[]{:S(2)}) %collective-permute-start.23) | collective-permute-done | bytes 589856 | tf_op jit(solution)/shard_map/ppermute | solution.py:494
  65.3 1.9 %collective-permute-start.29 = (f32[1,144,128]{2,1,0:T(8,128)S(1)}, f32[1,144,128]{2,1,0:T(8,128)S(1)}, u32[]{:S(2)}, u32[]{:S(2)}) collective-permute-start(f32[1,144,128]{2,1,0:T(8,128)S(1)} %bitcast.82), channel_id=1, source_target_pairs={{0,12},{2,14},{4,8},{6,10},{8,4},{10,6},{12,0},{14,2},{1,13},{3,15... | collective-permute-start | bytes 221192 | tf_op jit(solution)/shard_map/ppermute | solution.py:522
  67.1 2.7 %collective-permute-start.30 = (f32[1,144,128]{2,1,0:T(8,128)S(1)}, f32[1,144,128]{2,1,0:T(8,128)S(1)}, u32[]{:S(2)}, u32[]{:S(2)}) collective-permute-start(f32[1,144,128]{2,1,0:T(8,128)S(1)} %bitcast.80), channel_id=1, source_target_pairs={{0,14},{2,12},{4,10},{6,8},{8,6},{10,4},{12,2},{14,0},{1,15},{3,13... | collective-permute-start | bytes 221192 | tf_op jit(solution)/shard_map/ppermute | solution.py:522
  69.8 3.2 %collective-permute-start.27 = (f32[1,144,128]{2,1,0:T(8,128)S(1)}, f32[1,144,128]{2,1,0:T(8,128)S(1)}, u32[]{:S(2)}, u32[]{:S(2)}) collective-permute-start(f32[1,144,128]{2,1,0:T(8,128)S(1)} %bitcast.74), channel_id=1, source_target_pairs={{0,8},{2,10},{4,12},{6,14},{8,0},{10,2},{12,4},{14,6},{1,9},{3,11}... | collective-permute-start | bytes 221192 | tf_op jit(solution)/shard_map/ppermute | solution.py:522
  73.0 2.6 %collective-permute-start.25 = (f32[1,144,128]{2,1,0:T(8,128)S(1)}, f32[1,144,128]{2,1,0:T(8,128)S(1)}, u32[]{:S(2)}, u32[]{:S(2)}) collective-permute-start(f32[1,144,128]{2,1,0:T(8,128)S(1)} %bitcast.70), channel_id=1, source_target_pairs={{0,4},{2,6},{4,0},{6,2},{8,12},{10,14},{12,8},{14,10},{1,5},{3,7},... | collective-permute-start | bytes 221192 | tf_op jit(solution)/shard_map/ppermute | solution.py:522
  75.7 0.8 collective-permute-start.24
  76.5 2.0 %local.1 = (f32[16,64,512]{2,1,0:T(8,128)S(1)}, bf16[144,64,128]{2,1,0:T(8,128)(2,1)S(1)}, bf16[144,64,128]{2,1,0:T(8,128)(2,1)S(1)}) custom-call(bf16[16,64,512]{2,1,0:T(8,128)(2,1)S(1)} %get-tuple-element.64.slope_high, bf16[16,64,512]{2,1,0:T(8,128)(2,1)S(1)} %get-tuple-element.65.slope_low, f32[64,64]{1,0:T(8,128)S(1)} %copy-done.20, ...), custom_call_target="tpu_custom_call" | custom-call | flops 6000000000 | bytes 100000 | tf_op jit(solution)/shard_map/local/pallas_call | solution.py:592
  78.9 1.0 collective-permute-done.27.refs_4_.refs_12_
  79.9 1.2 %collective-permute-done.26.refs_3_.refs_11_ = f32[1,144,128]{2,1,0:T(8,128)S(1)} collective-permute-done((f32[1,144,128]{2,1,0:T(8,128)S(1)}, f32[1,144,128]{2,1,0:T(8,128)S(1)}, u32[]{:S(2)}, u32[]{:S(2)}) %collective-permute-start.26) | collective-permute-done | bytes 73760 | tf_op jit(solution)/shard_map/ppermute | solution.py:522
  81.2 0.6 collective-permute-done.25.refs_2_.refs_10_
  81.8 3.2 %adjoint.1 = (f32[1,144,128]{2,1,0:T(8,128)S(1)}, f32[1,144,128]{2,1,0:T(8,128)S(1)}, f32[1,144,128]{2,1,0:T(8,128)S(1)}, f32[1,144,128]{2,1,0:T(8,128)S(1)}, f3...) custom-call(f32[1,144,128]{2,1,0:T(8,128)S(1)} %bitcast.42, ...), custom_call_target="tpu_custom_call" | custom-call | flops 1000000000 | bytes 100000 | tf_op jit(solution)/shard_map/adjoint/pallas_call | solution.py:546
  85.0 0.8 collective-permute-start.31
  85.8 2.3 %collective-permute-start.33 = (f32[1,144,128]{2,1,0:T(8,128)S(1)}, f32[1,144,128]{2,1,0:T(8,128)S(1)}, u32[]{:S(2)}, u32[]{:S(2)}) collective-permute-start(f32[1,144,128]{2,1,0:T(8,128)S(1)} %get-tuple-element.71), channel_id=1, source_target_pairs={{0,8},{2,10},{4,12},{6,14},{8,0},{10,2},{12,4},{14,6},{1,9},{3,11}... | collective-permute-start | bytes 221192 | tf_op jit(solution)/shard_map/ppermute | solution.py:522
  88.2 1.3 %collective-permute-start.34 = (f32[1,144,128]{2,1,0:T(8,128)S(1)}, f32[1,144,128]{2,1,0:T(8,128)S(1)}, u32[]{:S(2)}, u32[]{:S(2)}) collective-permute-start(f32[1,144,128]{2,1,0:T(8,128)S(1)} %get-tuple-element.72), channel_id=1, source_target_pairs={{0,10},{2,8},{4,14},{6,12},{8,2},{10,0},{12,6},{14,4},{1,11},{3,9}... | collective-permute-start | bytes 221192 | tf_op jit(solution)/shard_map/ppermute | solution.py:522
  89.5 1.5 %collective-permute-start.35 = (f32[1,144,128]{2,1,0:T(8,128)S(1)}, f32[1,144,128]{2,1,0:T(8,128)S(1)}, u32[]{:S(2)}, u32[]{:S(2)}) collective-permute-start(f32[1,144,128]{2,1,0:T(8,128)S(1)} %get-tuple-element.73), channel_id=1, source_target_pairs={{0,12},{2,14},{4,8},{6,10},{8,4},{10,6},{12,0},{14,2},{1,13},{3,15... | collective-permute-start | bytes 221192 | tf_op jit(solution)/shard_map/ppermute | solution.py:522
  91.0 2.5 %collective-permute-start.36 = (f32[1,144,128]{2,1,0:T(8,128)S(1)}, f32[1,144,128]{2,1,0:T(8,128)S(1)}, u32[]{:S(2)}, u32[]{:S(2)}) collective-permute-start(f32[1,144,128]{2,1,0:T(8,128)S(1)} %get-tuple-element.74), channel_id=1, source_target_pairs={{0,14},{2,12},{4,10},{6,8},{8,6},{10,4},{12,2},{14,0},{1,15},{3,13... | collective-permute-start | bytes 221192 | tf_op jit(solution)/shard_map/ppermute | solution.py:522
  93.5 0.9 collective-permute-start.37
  94.5 7.5 %adam.1 = (f32[144,64,128]{2,1,0:T(8,128)}, f32[144,64,128]{2,1,0:T(8,128)}, f32[144,64,128]{2,1,0:T(8,128)}) custom-call(f32[1,144,128]{2,1,0:T(8,128)S(1)} %bitcast.41, f32[1,144,128]{2,1,0:T(8,128)S(1)} %copy-done.19, f32[1,144,128]{2,1,0:T(8,128)S(1)} %copy-done.17, f32[1,144,128]{2,1,0:T(8,128)S(1)} %copy-done.15, f32[1,144,128]{2,1,0:T(8,128)S(1)} %copy-done.13, ...), custom_call_target="tpu_custom_call" | custom-call | flops 10000000000 | bytes 30000000 | tf_op jit(solution)/shard_map/adam/pallas_call | solution.py:605
  102.1 0.5 collective-permute-start.38
  105.2 5.0 %last.1 = bf16[1,16,64,512]{3,2,1,0:T(8,128)(2,1)} custom-call(s32[2]{0:T(128)S(1)} %pad_add_fusion.place, f32[2,72,128]{2,1,0:T(8,128)S(1)} %bitcast.47, f32[2,72,128]{2,1,0:T(8,128)S(1)} %bitcast.49, f32[2,72,128]{2,1,0:T(8,128)S(1)} %bitcast.51, f32[2,72,128]{2,1,0:T(8,128)S(1)} %bitcast.53, f32[2,72,128]{2,1,0:T(8,128)S(1)} %bitcast.55, ...), custom_call_target="tpu_custom_call" | custom-call | tf_op jit(solution)/shard_map/last/pallas_call | solution.py:618
  (111 shorter events, 6.0 us)
Async XLA Ops:
  5.6 2.4 %collective-permute-start = (f32[8,2,72,128]{3,2,1,0:T(8,128)}, f32[8,2,72,128]{3,2,1,0:T(8,128)S(1)}, u32[]{:S(2)}, u32[]{:S(2)}) collective-permute-start(f32[8,2,72,128]{3,2,1,0:T(8,128)} %get-tuple-element.50), channel_id=1, source_target_pairs={{0,1},{1,0},{2,3},{3,2},{4,5},{5,4},{6,7},{7,6},{8,9},{9,8},{10,11... | collective-permute-start | bytes 1769480 | tf_op jit(solution)/shard_map/ppermute | solution.py:494
  9.2 11.3 %collective-permute-start.6 = (f32[1,144,128]{2,1,0:T(8,128)S(1)}, f32[1,144,128]{2,1,0:T(8,128)S(1)}, u32[]{:S(2)}, u32[]{:S(2)}) collective-permute-start(f32[1,144,128]{2,1,0:T(8,128)S(1)} %bitcast.81), channel_id=1, source_target_pairs={{0,12},{2,14},{4,8},{6,10},{8,4},{10,6},{12,0},{14,2},{1,13},{3,15... | collective-permute-start | bytes 221192 | tf_op jit(solution)/shard_map/ppermute | solution.py:522
  14.2 7.7 %collective-permute-start.7 = (f32[1,144,128]{2,1,0:T(8,128)S(1)}, f32[1,144,128]{2,1,0:T(8,128)S(1)}, u32[]{:S(2)}, u32[]{:S(2)}) collective-permute-start(f32[1,144,128]{2,1,0:T(8,128)S(1)} %bitcast.79), channel_id=1, source_target_pairs={{0,14},{2,12},{4,10},{6,8},{8,6},{10,4},{12,2},{14,0},{1,15},{3,13... | collective-permute-start | bytes 221192 | tf_op jit(solution)/shard_map/ppermute | solution.py:522
  15.4 11.6 %collective-permute-start.5 = (f32[1,144,128]{2,1,0:T(8,128)S(1)}, f32[1,144,128]{2,1,0:T(8,128)S(1)}, u32[]{:S(2)}, u32[]{:S(2)}) collective-permute-start(f32[1,144,128]{2,1,0:T(8,128)S(1)} %bitcast.78), channel_id=1, source_target_pairs={{0,10},{2,8},{4,14},{6,12},{8,2},{10,0},{12,6},{14,4},{1,11},{3,9}... | collective-permute-start | bytes 221192 | tf_op jit(solution)/shard_map/ppermute | solution.py:522
  16.1 11.0 %collective-permute-start.4 = (f32[1,144,128]{2,1,0:T(8,128)S(1)}, f32[1,144,128]{2,1,0:T(8,128)S(1)}, u32[]{:S(2)}, u32[]{:S(2)}) collective-permute-start(f32[1,144,128]{2,1,0:T(8,128)S(1)} %bitcast.77), channel_id=1, source_target_pairs={{0,8},{2,10},{4,12},{6,14},{8,0},{10,2},{12,4},{14,6},{1,9},{3,11}... | collective-permute-start | bytes 221192 | tf_op jit(solution)/shard_map/ppermute | solution.py:522
  18.1 9.0 %collective-permute-start.3 = (f32[1,144,128]{2,1,0:T(8,128)S(1)}, f32[1,144,128]{2,1,0:T(8,128)S(1)}, u32[]{:S(2)}, u32[]{:S(2)}) collective-permute-start(f32[1,144,128]{2,1,0:T(8,128)S(1)} %bitcast.75), channel_id=1, source_target_pairs={{0,6},{2,4},{4,2},{6,0},{8,14},{10,12},{12,10},{14,8},{1,7},{3,5},... | collective-permute-start | bytes 221192 | tf_op jit(solution)/shard_map/ppermute | solution.py:522
  20.4 7.0 %collective-permute-start.2 = (f32[1,144,128]{2,1,0:T(8,128)S(1)}, f32[1,144,128]{2,1,0:T(8,128)S(1)}, u32[]{:S(2)}, u32[]{:S(2)}) collective-permute-start(f32[1,144,128]{2,1,0:T(8,128)S(1)} %bitcast.73), channel_id=1, source_target_pairs={{0,4},{2,6},{4,0},{6,2},{8,12},{10,14},{12,8},{14,10},{1,5},{3,7},... | collective-permute-start | bytes 221192 | tf_op jit(solution)/shard_map/ppermute | solution.py:522
  21.9 5.5 %collective-permute-start.1 = (f32[1,144,128]{2,1,0:T(8,128)S(1)}, f32[1,144,128]{2,1,0:T(8,128)S(1)}, u32[]{:S(2)}, u32[]{:S(2)}) collective-permute-start(f32[1,144,128]{2,1,0:T(8,128)S(1)} %bitcast.71), channel_id=1, source_target_pairs={{0,2},{2,0},{4,6},{6,4},{8,10},{10,8},{12,14},{14,12},{1,3},{3,1},... | collective-permute-start | bytes 221192 | tf_op jit(solution)/shard_map/ppermute | solution.py:522
  26.6 24.9 %copy-start.1 = (bf16[1,16,64,512]{3,2,1,0:T(8,128)(2,1)S(1)}, bf16[1,16,64,512]{3,2,1,0:T(8,128)(2,1)}, u32[]{:S(2)}) copy-start(bf16[1,16,64,512]{3,2,1,0:T(8,128)(2,1)} %refs_16_.1) | copy-start | bytes 3145732
  26.6 24.9 %copy-start.2 = (bf16[2,256,864]{2,1,0:T(8,128)(2,1)S(1)}, bf16[2,256,864]{2,1,0:T(8,128)(2,1)}, u32[]{:S(2)}) copy-start(bf16[2,256,864]{2,1,0:T(8,128)(2,1)} %constant.22.clone.refs_19_.refs_17_) | copy-start | bytes 2654212
  30.0 12.1 %collective-permute-start.8 = (f32[1,144,128]{2,1,0:T(8,128)S(1)}, f32[1,144,128]{2,1,0:T(8,128)}, u32[]{:S(2)}, u32[]{:S(2)}) collective-permute-start(f32[1,144,128]{2,1,0:T(8,128)S(1)} %get-tuple-element.53), channel_id=1, source_target_pairs={{0,8},{2,10},{4,12},{6,14},{8,0},{10,2},{12,4},{14,6},{1,9},{3,11}... | collective-permute-start | bytes 221192 | tf_op jit(solution)/shard_map/ppermute | solution.py:522
  34.4 10.3 %collective-permute-start.9 = (f32[1,144,128]{2,1,0:T(8,128)S(1)}, f32[1,144,128]{2,1,0:T(8,128)}, u32[]{:S(2)}, u32[]{:S(2)}) collective-permute-start(f32[1,144,128]{2,1,0:T(8,128)S(1)} %get-tuple-element.54), channel_id=1, source_target_pairs={{0,10},{2,8},{4,14},{6,12},{8,2},{10,0},{12,6},{14,4},{1,11},{3,9}... | collective-permute-start | bytes 221192 | tf_op jit(solution)/shard_map/ppermute | solution.py:522
  34.8 11.1 %collective-permute-start.10 = (f32[1,144,128]{2,1,0:T(8,128)S(1)}, f32[1,144,128]{2,1,0:T(8,128)}, u32[]{:S(2)}, u32[]{:S(2)}) collective-permute-start(f32[1,144,128]{2,1,0:T(8,128)S(1)} %get-tuple-element.55), channel_id=1, source_target_pairs={{0,12},{2,14},{4,8},{6,10},{8,4},{10,6},{12,0},{14,2},{1,13},{3,15... | collective-permute-start | bytes 221192 | tf_op jit(solution)/shard_map/ppermute | solution.py:522
  36.9 9.0 %collective-permute-start.11 = (f32[1,144,128]{2,1,0:T(8,128)S(1)}, f32[1,144,128]{2,1,0:T(8,128)}, u32[]{:S(2)}, u32[]{:S(2)}) collective-permute-start(f32[1,144,128]{2,1,0:T(8,128)S(1)} %get-tuple-element.56), channel_id=1, source_target_pairs={{0,14},{2,12},{4,10},{6,8},{8,6},{10,4},{12,2},{14,0},{1,15},{3,13... | collective-permute-start | bytes 221192 | tf_op jit(solution)/shard_map/ppermute | solution.py:522
  39.2 7.2 %collective-permute-start.12 = (f32[1,144,128]{2,1,0:T(8,128)S(1)}, f32[1,144,128]{2,1,0:T(8,128)}, u32[]{:S(2)}, u32[]{:S(2)}) collective-permute-start(f32[1,144,128]{2,1,0:T(8,128)S(1)} %get-tuple-element.57), channel_id=1, source_target_pairs={{0,6},{2,4},{4,2},{6,0},{8,14},{10,12},{12,10},{14,8},{1,7},{3,5},... | collective-permute-start | bytes 221192 | tf_op jit(solution)/shard_map/ppermute | solution.py:522
  42.1 4.7 %collective-permute-start.13 = (f32[1,144,128]{2,1,0:T(8,128)}, f32[1,144,128]{2,1,0:T(8,128)}, u32[]{:S(2)}, u32[]{:S(2)}) collective-permute-start(f32[1,144,128]{2,1,0:T(8,128)} %get-tuple-element.58), channel_id=1, source_target_pairs={{0,4},{2,6},{4,0},{6,2},{8,12},{10,14},{12,8},{14,10},{1,5},{3,7},... | collective-permute-start | bytes 221192 | tf_op jit(solution)/shard_map/ppermute | solution.py:522
  44.7 4.7 %collective-permute-start.14 = (f32[1,144,128]{2,1,0:T(8,128)}, f32[1,144,128]{2,1,0:T(8,128)}, u32[]{:S(2)}, u32[]{:S(2)}) collective-permute-start(f32[1,144,128]{2,1,0:T(8,128)} %get-tuple-element.59), channel_id=1, source_target_pairs={{0,2},{2,0},{4,6},{6,4},{8,10},{10,8},{12,14},{14,12},{1,3},{3,1},... | collective-permute-start | bytes 221192 | tf_op jit(solution)/shard_map/ppermute | solution.py:522
  45.9 3.5 %collective-permute-start.22 = (f32[2,72,128]{2,1,0:T(8,128)}, f32[2,72,128]{2,1,0:T(8,128)}, u32[]{:S(2)}, u32[]{:S(2)}) collective-permute-start(f32[2,72,128]{2,1,0:T(8,128)} %bitcast.18.refs_7_), channel_id=1, source_target_pairs={{0,1},{1,0},{2,3},{3,2},{4,5},{5,4},{6,7},{7,6},{8,9},{9,8},{10,11... | collective-permute-start | bytes 221192 | tf_op jit(solution)/shard_map/ppermute | solution.py:494
  45.9 4.0 %collective-permute-start.15 = (f32[2,72,128]{2,1,0:T(8,128)}, f32[2,72,128]{2,1,0:T(8,128)}, u32[]{:S(2)}, u32[]{:S(2)}) collective-permute-start(f32[2,72,128]{2,1,0:T(8,128)} %bitcast.11.refs_0_), channel_id=1, source_target_pairs={{0,1},{1,0},{2,3},{3,2},{4,5},{5,4},{6,7},{7,6},{8,9},{9,8},{10,11... | collective-permute-start | bytes 221192 | tf_op jit(solution)/shard_map/ppermute | solution.py:494
  46.4 3.6 %collective-permute-start.16 = (f32[2,72,128]{2,1,0:T(8,128)}, f32[2,72,128]{2,1,0:T(8,128)}, u32[]{:S(2)}, u32[]{:S(2)}) collective-permute-start(f32[2,72,128]{2,1,0:T(8,128)} %bitcast.12.refs_1_), channel_id=1, source_target_pairs={{0,1},{1,0},{2,3},{3,2},{4,5},{5,4},{6,7},{7,6},{8,9},{9,8},{10,11... | collective-permute-start | bytes 221192 | tf_op jit(solution)/shard_map/ppermute | solution.py:494
  46.7 3.8 %collective-permute-start.17 = (f32[2,72,128]{2,1,0:T(8,128)}, f32[2,72,128]{2,1,0:T(8,128)S(1)}, u32[]{:S(2)}, u32[]{:S(2)}) collective-permute-start(f32[2,72,128]{2,1,0:T(8,128)} %bitcast.13.refs_2_), channel_id=1, source_target_pairs={{0,1},{1,0},{2,3},{3,2},{4,5},{5,4},{6,7},{7,6},{8,9},{9,8},{10,11... | collective-permute-start | bytes 221192 | tf_op jit(solution)/shard_map/ppermute | solution.py:494
  49.4 1.5 %collective-permute-start.18 = (f32[2,72,128]{2,1,0:T(8,128)}, f32[2,72,128]{2,1,0:T(8,128)S(1)}, u32[]{:S(2)}, u32[]{:S(2)}) collective-permute-start(f32[2,72,128]{2,1,0:T(8,128)} %bitcast.14.refs_3_), channel_id=1, source_target_pairs={{0,1},{1,0},{2,3},{3,2},{4,5},{5,4},{6,7},{7,6},{8,9},{9,8},{10,11... | collective-permute-start | bytes 221192 | tf_op jit(solution)/shard_map/ppermute | solution.py:494
  49.4 1.6 %collective-permute-start.19 = (f32[2,72,128]{2,1,0:T(8,128)}, f32[2,72,128]{2,1,0:T(8,128)S(1)}, u32[]{:S(2)}, u32[]{:S(2)}) collective-permute-start(f32[2,72,128]{2,1,0:T(8,128)} %bitcast.15.refs_4_), channel_id=1, source_target_pairs={{0,1},{1,0},{2,3},{3,2},{4,5},{5,4},{6,7},{7,6},{8,9},{9,8},{10,11... | collective-permute-start | bytes 221192 | tf_op jit(solution)/shard_map/ppermute | solution.py:494
  49.9 1.5 %collective-permute-start.20 = (f32[2,72,128]{2,1,0:T(8,128)}, f32[2,72,128]{2,1,0:T(8,128)S(1)}, u32[]{:S(2)}, u32[]{:S(2)}) collective-permute-start(f32[2,72,128]{2,1,0:T(8,128)} %bitcast.16.refs_5_), channel_id=1, source_target_pairs={{0,1},{1,0},{2,3},{3,2},{4,5},{5,4},{6,7},{7,6},{8,9},{9,8},{10,11... | collective-permute-start | bytes 221192 | tf_op jit(solution)/shard_map/ppermute | solution.py:494
  50.0 1.6 %collective-permute-start.21 = (f32[2,72,128]{2,1,0:T(8,128)}, f32[2,72,128]{2,1,0:T(8,128)S(1)}, u32[]{:S(2)}, u32[]{:S(2)}) collective-permute-start(f32[2,72,128]{2,1,0:T(8,128)} %bitcast.17.refs_6_), channel_id=1, source_target_pairs={{0,1},{1,0},{2,3},{3,2},{4,5},{5,4},{6,7},{7,6},{8,9},{9,8},{10,11... | collective-permute-start | bytes 221192 | tf_op jit(solution)/shard_map/ppermute | solution.py:494
  63.1 2.1 %collective-permute-start.23 = (f32[8,2,72,128]{3,2,1,0:T(8,128)S(1)}, f32[8,2,72,128]{3,2,1,0:T(8,128)S(1)}, u32[]{:S(2)}, u32[]{:S(2)}) collective-permute-start(f32[8,2,72,128]{3,2,1,0:T(8,128)S(1)} %get-tuple-element.63), channel_id=1, source_target_pairs={{0,1},{1,0},{2,3},{3,2},{4,5},{5,4},{6,7},{7,6},{8,9},{9,8},{10,11... | collective-permute-start | bytes 1769480 | tf_op jit(solution)/shard_map/ppermute | solution.py:494
  65.3 7.7 %collective-permute-start.29 = (f32[1,144,128]{2,1,0:T(8,128)S(1)}, f32[1,144,128]{2,1,0:T(8,128)S(1)}, u32[]{:S(2)}, u32[]{:S(2)}) collective-permute-start(f32[1,144,128]{2,1,0:T(8,128)S(1)} %bitcast.82), channel_id=1, source_target_pairs={{0,12},{2,14},{4,8},{6,10},{8,4},{10,6},{12,0},{14,2},{1,13},{3,15... | collective-permute-start | bytes 221192 | tf_op jit(solution)/shard_map/ppermute | solution.py:522
  67.1 8.5 %collective-permute-start.30 = (f32[1,144,128]{2,1,0:T(8,128)S(1)}, f32[1,144,128]{2,1,0:T(8,128)S(1)}, u32[]{:S(2)}, u32[]{:S(2)}) collective-permute-start(f32[1,144,128]{2,1,0:T(8,128)S(1)} %bitcast.80), channel_id=1, source_target_pairs={{0,14},{2,12},{4,10},{6,8},{8,6},{10,4},{12,2},{14,0},{1,15},{3,13... | collective-permute-start | bytes 221192 | tf_op jit(solution)/shard_map/ppermute | solution.py:522
  69.8 9.1 %collective-permute-start.28 = (f32[1,144,128]{2,1,0:T(8,128)S(1)}, f32[1,144,128]{2,1,0:T(8,128)S(1)}, u32[]{:S(2)}, u32[]{:S(2)}) collective-permute-start(f32[1,144,128]{2,1,0:T(8,128)S(1)} %bitcast.76), channel_id=1, source_target_pairs={{0,10},{2,8},{4,14},{6,12},{8,2},{10,0},{12,6},{14,4},{1,11},{3,9}... | collective-permute-start | bytes 221192 | tf_op jit(solution)/shard_map/ppermute | solution.py:522
  69.8 10.1 %collective-permute-start.27 = (f32[1,144,128]{2,1,0:T(8,128)S(1)}, f32[1,144,128]{2,1,0:T(8,128)S(1)}, u32[]{:S(2)}, u32[]{:S(2)}) collective-permute-start(f32[1,144,128]{2,1,0:T(8,128)S(1)} %bitcast.74), channel_id=1, source_target_pairs={{0,8},{2,10},{4,12},{6,14},{8,0},{10,2},{12,4},{14,6},{1,9},{3,11}... | collective-permute-start | bytes 221192 | tf_op jit(solution)/shard_map/ppermute | solution.py:522
  73.0 8.2 %collective-permute-start.26 = (f32[1,144,128]{2,1,0:T(8,128)S(1)}, f32[1,144,128]{2,1,0:T(8,128)S(1)}, u32[]{:S(2)}, u32[]{:S(2)}) collective-permute-start(f32[1,144,128]{2,1,0:T(8,128)S(1)} %bitcast.72), channel_id=1, source_target_pairs={{0,6},{2,4},{4,2},{6,0},{8,14},{10,12},{12,10},{14,8},{1,7},{3,5},... | collective-permute-start | bytes 221192 | tf_op jit(solution)/shard_map/ppermute | solution.py:522
  73.0 8.7 %collective-permute-start.25 = (f32[1,144,128]{2,1,0:T(8,128)S(1)}, f32[1,144,128]{2,1,0:T(8,128)S(1)}, u32[]{:S(2)}, u32[]{:S(2)}) collective-permute-start(f32[1,144,128]{2,1,0:T(8,128)S(1)} %bitcast.70), channel_id=1, source_target_pairs={{0,4},{2,6},{4,0},{6,2},{8,12},{10,14},{12,8},{14,10},{1,5},{3,7},... | collective-permute-start | bytes 221192 | tf_op jit(solution)/shard_map/ppermute | solution.py:522
  75.7 6.1 %collective-permute-start.24 = (f32[1,144,128]{2,1,0:T(8,128)S(1)}, f32[1,144,128]{2,1,0:T(8,128)S(1)}, u32[]{:S(2)}, u32[]{:S(2)}) collective-permute-start(f32[1,144,128]{2,1,0:T(8,128)S(1)} %bitcast.69), channel_id=1, source_target_pairs={{0,2},{2,0},{4,6},{6,4},{8,10},{10,8},{12,14},{14,12},{1,3},{3,1},... | collective-permute-start | bytes 221192 | tf_op jit(solution)/shard_map/ppermute | solution.py:522
  85.0 6.0 %collective-permute-start.31 = (f32[1,144,128]{2,1,0:T(8,128)S(1)}, f32[1,144,128]{2,1,0:T(8,128)S(1)}, u32[]{:S(2)}, u32[]{:S(2)}) collective-permute-start(f32[1,144,128]{2,1,0:T(8,128)S(1)} %get-tuple-element.69), channel_id=1, source_target_pairs={{0,2},{2,0},{4,6},{6,4},{8,10},{10,8},{12,14},{14,12},{1,3},{3,1},... | collective-permute-start | bytes 221192 | tf_op jit(solution)/shard_map/ppermute | solution.py:522
  85.8 7.7 %collective-permute-start.32 = (f32[1,144,128]{2,1,0:T(8,128)S(1)}, f32[1,144,128]{2,1,0:T(8,128)S(1)}, u32[]{:S(2)}, u32[]{:S(2)}) collective-permute-start(f32[1,144,128]{2,1,0:T(8,128)S(1)} %get-tuple-element.70), channel_id=1, source_target_pairs={{0,4},{2,6},{4,0},{6,2},{8,12},{10,14},{12,8},{14,10},{1,5},{3,7},... | collective-permute-start | bytes 221192 | tf_op jit(solution)/shard_map/ppermute | solution.py:522
  85.8 16.2 %collective-permute-start.33 = (f32[1,144,128]{2,1,0:T(8,128)S(1)}, f32[1,144,128]{2,1,0:T(8,128)S(1)}, u32[]{:S(2)}, u32[]{:S(2)}) collective-permute-start(f32[1,144,128]{2,1,0:T(8,128)S(1)} %get-tuple-element.71), channel_id=1, source_target_pairs={{0,8},{2,10},{4,12},{6,14},{8,0},{10,2},{12,4},{14,6},{1,9},{3,11}... | collective-permute-start | bytes 221192 | tf_op jit(solution)/shard_map/ppermute | solution.py:522
  88.2 13.9 %collective-permute-start.34 = (f32[1,144,128]{2,1,0:T(8,128)S(1)}, f32[1,144,128]{2,1,0:T(8,128)S(1)}, u32[]{:S(2)}, u32[]{:S(2)}) collective-permute-start(f32[1,144,128]{2,1,0:T(8,128)S(1)} %get-tuple-element.72), channel_id=1, source_target_pairs={{0,10},{2,8},{4,14},{6,12},{8,2},{10,0},{12,6},{14,4},{1,11},{3,9}... | collective-permute-start | bytes 221192 | tf_op jit(solution)/shard_map/ppermute | solution.py:522
  89.5 12.6 %collective-permute-start.35 = (f32[1,144,128]{2,1,0:T(8,128)S(1)}, f32[1,144,128]{2,1,0:T(8,128)S(1)}, u32[]{:S(2)}, u32[]{:S(2)}) collective-permute-start(f32[1,144,128]{2,1,0:T(8,128)S(1)} %get-tuple-element.73), channel_id=1, source_target_pairs={{0,12},{2,14},{4,8},{6,10},{8,4},{10,6},{12,0},{14,2},{1,13},{3,15... | collective-permute-start | bytes 221192 | tf_op jit(solution)/shard_map/ppermute | solution.py:522
  91.0 11.1 %collective-permute-start.36 = (f32[1,144,128]{2,1,0:T(8,128)S(1)}, f32[1,144,128]{2,1,0:T(8,128)S(1)}, u32[]{:S(2)}, u32[]{:S(2)}) collective-permute-start(f32[1,144,128]{2,1,0:T(8,128)S(1)} %get-tuple-element.74), channel_id=1, source_target_pairs={{0,14},{2,12},{4,10},{6,8},{8,6},{10,4},{12,2},{14,0},{1,15},{3,13... | collective-permute-start | bytes 221192 | tf_op jit(solution)/shard_map/ppermute | solution.py:522
  93.5 8.6 %collective-permute-start.37 = (f32[1,144,128]{2,1,0:T(8,128)S(1)}, f32[1,144,128]{2,1,0:T(8,128)S(1)}, u32[]{:S(2)}, u32[]{:S(2)}) collective-permute-start(f32[1,144,128]{2,1,0:T(8,128)S(1)} %get-tuple-element.75), channel_id=1, source_target_pairs={{0,6},{2,4},{4,2},{6,0},{8,14},{10,12},{12,10},{14,8},{1,7},{3,5},... | collective-permute-start | bytes 221192 | tf_op jit(solution)/shard_map/ppermute | solution.py:522
  102.1 1.3 %collective-permute-start.39 = (f32[2,72,128]{2,1,0:T(8,128)S(1)}, f32[2,72,128]{2,1,0:T(8,128)S(1)}, u32[]{:S(2)}, u32[]{:S(2)}) collective-permute-start(f32[2,72,128]{2,1,0:T(8,128)S(1)} %bitcast.48), channel_id=1, source_target_pairs={{0,1},{1,0},{2,3},{3,2},{4,5},{5,4},{6,7},{7,6},{8,9},{9,8},{10,11... | collective-permute-start | bytes 221192 | tf_op jit(solution)/shard_map/ppermute | solution.py:494
  102.1 1.5 %collective-permute-start.38 = (f32[2,72,128]{2,1,0:T(8,128)S(1)}, f32[2,72,128]{2,1,0:T(8,128)S(1)}, u32[]{:S(2)}, u32[]{:S(2)}) collective-permute-start(f32[2,72,128]{2,1,0:T(8,128)S(1)} %bitcast.46), channel_id=1, source_target_pairs={{0,1},{1,0},{2,3},{3,2},{4,5},{5,4},{6,7},{7,6},{8,9},{9,8},{10,11... | collective-permute-start | bytes 221192 | tf_op jit(solution)/shard_map/ppermute | solution.py:494
  102.6 1.3 %collective-permute-start.40 = (f32[2,72,128]{2,1,0:T(8,128)S(1)}, f32[2,72,128]{2,1,0:T(8,128)S(1)}, u32[]{:S(2)}, u32[]{:S(2)}) collective-permute-start(f32[2,72,128]{2,1,0:T(8,128)S(1)} %bitcast.50), channel_id=1, source_target_pairs={{0,1},{1,0},{2,3},{3,2},{4,5},{5,4},{6,7},{7,6},{8,9},{9,8},{10,11... | collective-permute-start | bytes 221192 | tf_op jit(solution)/shard_map/ppermute | solution.py:494
  102.7 1.5 %collective-permute-start.41 = (f32[2,72,128]{2,1,0:T(8,128)S(1)}, f32[2,72,128]{2,1,0:T(8,128)S(1)}, u32[]{:S(2)}, u32[]{:S(2)}) collective-permute-start(f32[2,72,128]{2,1,0:T(8,128)S(1)} %bitcast.52), channel_id=1, source_target_pairs={{0,1},{1,0},{2,3},{3,2},{4,5},{5,4},{6,7},{7,6},{8,9},{9,8},{10,11... | collective-permute-start | bytes 221192 | tf_op jit(solution)/shard_map/ppermute | solution.py:494
  103.2 1.3 %collective-permute-start.42 = (f32[2,72,128]{2,1,0:T(8,128)S(1)}, f32[2,72,128]{2,1,0:T(8,128)S(1)}, u32[]{:S(2)}, u32[]{:S(2)}) collective-permute-start(f32[2,72,128]{2,1,0:T(8,128)S(1)} %bitcast.54), channel_id=1, source_target_pairs={{0,1},{1,0},{2,3},{3,2},{4,5},{5,4},{6,7},{7,6},{8,9},{9,8},{10,11... | collective-permute-start | bytes 221192 | tf_op jit(solution)/shard_map/ppermute | solution.py:494
  103.4 1.3 %collective-permute-start.43 = (f32[2,72,128]{2,1,0:T(8,128)S(1)}, f32[2,72,128]{2,1,0:T(8,128)S(1)}, u32[]{:S(2)}, u32[]{:S(2)}) collective-permute-start(f32[2,72,128]{2,1,0:T(8,128)S(1)} %bitcast.56), channel_id=1, source_target_pairs={{0,1},{1,0},{2,3},{3,2},{4,5},{5,4},{6,7},{7,6},{8,9},{9,8},{10,11... | collective-permute-start | bytes 221192 | tf_op jit(solution)/shard_map/ppermute | solution.py:494
  103.7 1.3 %collective-permute-start.44 = (f32[2,72,128]{2,1,0:T(8,128)S(1)}, f32[2,72,128]{2,1,0:T(8,128)S(1)}, u32[]{:S(2)}, u32[]{:S(2)}) collective-permute-start(f32[2,72,128]{2,1,0:T(8,128)S(1)} %bitcast.58), channel_id=1, source_target_pairs={{0,1},{1,0},{2,3},{3,2},{4,5},{5,4},{6,7},{7,6},{8,9},{9,8},{10,11... | collective-permute-start | bytes 221192 | tf_op jit(solution)/shard_map/ppermute | solution.py:494
  103.9 1.3 %collective-permute-start.45 = (f32[2,72,128]{2,1,0:T(8,128)S(1)}, f32[2,72,128]{2,1,0:T(8,128)S(1)}, u32[]{:S(2)}, u32[]{:S(2)}) collective-permute-start(f32[2,72,128]{2,1,0:T(8,128)S(1)} %bitcast.44), channel_id=1, source_target_pairs={{0,1},{1,0},{2,3},{3,2},{4,5},{5,4},{6,7},{7,6},{8,9},{9,8},{10,11... | collective-permute-start | bytes 221192 | tf_op jit(solution)/shard_map/ppermute | solution.py:494
  (25 other events, 335.9 us)

commit v3 on v2

--- a/solution.py
+++ b/solution.py
@@ -39,18 +39,33 @@
     return high, low
 
 
+def parity_rows(per_group):
+    half = per_group // 2 * MZ
+    return [(slot % 2) * half + slot // 2 * MZ + kz for slot in range(per_group) for kz in range(MZ)]
+
+
+def padded_rows(per_group):
+    return -(-(per_group // 2 * MZ) // 8) * 8
+
+
 def yz_tables(groups, scaled):
     per_group = MY // groups
-    y_frequency = np.concatenate([np.arange(MY // 2), np.arange(GY - MY // 2, GY)]).reshape(groups, per_group)
-    y_place = np.repeat(np.arange(GY), GZ)
-    z_place = np.tile(np.arange(GZ), GY)
-    turns = y_frequency[:, :, None, None] * y_place / GY + np.arange(MZ)[None, None, :, None] * z_place / GZ
+    y_frequency = np.concatenate([np.arange(MY // 2), np.arange(GY - MY // 2, GY)]).reshape(groups, per_group // 2, 2)
+    y_frequency = np.swapaxes(y_frequency, 1, 2)
+    y_place = np.repeat(np.arange(GY // 2), GZ)
+    z_place = np.tile(np.arange(GZ), GY // 2)
+    turns = y_frequency[..., None, None] * y_place / GY + np.arange(MZ)[None, None, None, :, None] * z_place / GZ
     angle = 2.0 * np.pi * (turns % 1.0)
-    table = np.stack([np.cos(angle), -np.sin(angle)], axis=1)
+    table = np.stack([np.cos(angle), -np.sin(angle)], axis=2)
     if scaled:
         table = table * (np.where(np.arange(MZ) == 0, 1.0, 2.0) / (GX * GY * GZ))[:, None]
-    table = table.reshape(groups, 2 * per_group * MZ, GY * GZ)
-    return np.concatenate(split_np(table), axis=1)
+    table = table.reshape(groups, 2, 2, per_group // 2 * MZ, GY // 2 * GZ)
+    rows = padded_rows(per_group)
+    padded = np.zeros(table.shape[:3] + (rows, table.shape[-1]))
+    padded[:, 0, :, : table.shape[3]] = table[:, 0]
+    padded[:, 1, :, rows - table.shape[3] :] = table[:, 1]
+    padded = padded.reshape(groups, 2, 2 * rows, table.shape[-1])
+    return np.concatenate(split_np(padded), axis=2).reshape(groups, 8 * rows, table.shape[-1])
 
 
 def x_tables(groups):
@@ -98,39 +113,60 @@
         cells = pieces[0].shape[0]
         stacked = pieces[0] if len(pieces) == 1 else jnp.concatenate(pieces, axis=0)
         result = dot(x_table[:, : cells * len(pieces)], stacked)
-        high, low = split(result)
+        middle = result.shape[-1] // 2
+        lower, upper = result[:, :middle], result[:, middle:]
+        high, low = split(jnp.concatenate([lower + upper, lower - upper], axis=1))
         rows = pl.ds(block * CBLOCK, CBLOCK)
         shape = (2 * HALF, CBLOCK, high.shape[-1])
         u_high[:, rows, :] = high.reshape(shape)
         u_low[:, rows, :] = low.reshape(shape)
     if ready is not None:
         ready()
-    table = jnp.concatenate([own[...], other[...]], axis=0)
-    part = own.shape[0] // 2
-    count = part // 2
-    brief = jnp.concatenate([own[:part, :], other[:part, :]], axis=0)
+    rows = own.shape[0] // 8
+    part = 2 * rows
+    count = own_out.shape[1]
+    overlap = 2 * rows - count
+    shared = pl.ds(count - rows, overlap)
+    tables = [
+        jnp.concatenate([own[2 * part * odd : 2 * part * (odd + 1), :], other[2 * part * odd : 2 * part * (odd + 1), :]], axis=0)
+        for odd in range(2)
+    ]
+    briefs = [
+        jnp.concatenate([own[2 * part * odd : 2 * part * odd + part, :], other[2 * part * odd : 2 * part * odd + part, :]], axis=0)
+        for odd in range(2)
+    ]
     width = 2 * channels
-    sign = lane_sign((count, width), -1.0)
+    sign = lane_sign((rows, width), -1.0)
+    half_cells = u_high.shape[-1] // 2
     for first in range(0, HALF, 2):
         several = min(2, HALF - first)
         at = pl.ds(2 * first, 2 * several)
-        high = u_high[at].reshape(several * width, u_high.shape[-1])
-        low = u_low[at].reshape(several * width, u_low.shape[-1])
-        wide = dot_nt(table, high)
-        small = dot_nt(brief, low)
+        high = u_high[at].reshape(several * width, 2 * half_cells)
+        low = u_low[at].reshape(several * width, 2 * half_cells)
+        wide = [dot_nt(tables[odd], high[:, half_cells * odd : half_cells * (odd + 1)]) for odd in range(2)]
+        small = [dot_nt(briefs[odd], low[:, half_cells * odd : half_cells * (odd + 1)]) for odd in range(2)]
         for which, out in enumerate((own_out, other_out)):
             base = 2 * part * which
-            total = (wide[base : base + part] + wide[base + part : base + 2 * part]) + small[
-                part * which : part * (which + 1)
+            totals = [
+                (wide[odd][base : base + part] + wide[odd][base + part : base + 2 * part])
+                + small[odd][part * which : part * (which + 1)]
+                for odd in range(2)
             ]
+
+            def put(kx, even, odd):
+                out[kx, : count - rows] = even[: count - rows]
+                out[kx, shared] = even[count - rows :] + odd[:overlap]
+                out[kx, rows:] = odd[overlap:]
+
             for step in range(several):
                 kx = first + step
-                real = total[:count, step * width : (step + 1) * width]
-                imag = swap(total[count:, step * width : (step + 1) * width])
+                lanes = slice(step * width, (step + 1) * width)
+                real = [total[:rows, lanes] for total in totals]
+                imag = [swap(total[rows:, lanes]) for total in totals]
                 if kx < MX // 2:
-                    out[kx] = real + imag * sign
+                    put(kx, *[r + i * sign for r, i in zip(real, imag)])
                 if kx > 0:
-                    out[MX - kx] = imag - real * sign
+                    put(MX - kx, *[i - r * sign for r, i in zip(real, imag)])
 
 
 def gather(place, order, sources, target):
@@ -146,9 +182,11 @@
 
 
 def from_spectra(channels, own_in, other_in, x_table, own, other, u_high, u_low, t_high, t_low):
-    part = own.shape[0] // 2
-    count = part // 2
+    rows = own.shape[0] // 8
+    part = 2 * rows
+    count = own_in.shape[1]
     width = 2 * channels
+    half_cells = own.shape[1]
     sign = lane_sign((count, width), -1.0)
     for kx in range(HALF):
         pieces = []
@@ -163,19 +201,33 @@
                 ahead, behind = source[kx], source[MX - kx]
                 real, imag = ahead - behind * sign, ahead * sign + behind
             pieces += [real, swap(imag)]
-        turned = jnp.concatenate(pieces, axis=0).T
-        high, low = split(turned)
-        t_high[pl.ds(kx * width, width), :] = high
-        t_low[pl.ds(kx * width, width), :] = low
-    table_high = jnp.concatenate([own[:part, :], other[:part, :]], axis=0)
-    table_low = jnp.concatenate([own[part:, :], other[part:, :]], axis=0)
+        at = pl.ds(kx * width, width)
+        for odd, first in enumerate((0, count - rows)):
+            turned = jnp.concatenate([piece[first : first + rows] for piece in pieces], axis=0).T
+            high, low = split(turned)
+            lanes = pl.ds(half_cells * odd, 2 * part)
+            t_high[at, lanes] = high
+            t_low[at, lanes] = low
+    tables = []
+    for odd in range(2):
+        base = 2 * part * odd
+        tables.append(
+            [
+                jnp.concatenate([own[base + shift : base + shift + part, :], other[base + shift : base + shift + part, :]], axis=0)
+                for shift in (0, part)
+            ]
+        )
     several = 3 if HALF % 3 == 0 else 1
     for first in range(0, HALF, several):
         at = pl.ds(first * width, several * width)
-        high, low = t_high[at, :], t_low[at, :]
-        value = dot(high, table_high) + dot(low, table_high) + dot(high, table_low)
-        value_high, value_low = split(value)
-        shape = (2 * several, channels, value.shape[-1])
+        values = []
+        for odd, (table_high, table_low) in enumerate(tables):
+            lanes = pl.ds(half_cells * odd, 2 * part)
+            high, low = t_high[at, lanes], t_low[at, lanes]
+            values.append(dot(high, table_high) + dot(low, table_high) + dot(high, table_low))
+        even, odd = values
+        value_high, value_low = split(jnp.concatenate([even + odd, even - odd], axis=1))
+        shape = (2 * several, channels, 2 * half_cells)
         u_high[pl.ds(2 * first, 2 * several)] = value_high.reshape(shape)
         u_low[pl.ds(2 * first, 2 * several)] = value_low.reshape(shape)
 
@@ -311,6 +363,10 @@
     return 72 if modes % 72 == 0 else modes
 
 
+def mode_rows(chunk):
+    return parity_rows(chunk // MZ) if chunk > MZ else list(range(chunk))
+
+
 def stack(refs, target):
     base = 0
     for ref in refs:
@@ -357,14 +413,15 @@
     @pl.loop(0, modes // chunk)
     def _(index):
         start = index * chunk
-        rows = [spectra[:, start + mode, :] for mode in range(chunk)]
+        places = mode_rows(chunk)
+        rows = [spectra[:, start + place, :] for place in places]
 
         def weight(first, count):
             values = [part[pl.ds(start + first, count)] for part in weights]
             return [value.reshape(-1, value.shape[-1]) for value in values]
 
-        for mode, value in enumerate(one_chunk(rows, weight)):
-            out[:, start + mode, :] = value
+        for place, value in zip(places, one_chunk(rows, weight)):
+            out[:, start + place, :] = value
 
     unstack(out, refs[:number])
 
@@ -415,14 +472,25 @@
 
 def adam_kernel(number, *refs):
     spectra_parts, slope_parts, refs = refs[:number], refs[number : 2 * number], refs[2 * number :]
-    weight, first, second, weight_out, first_out, second_out, spectra, slopes = refs
+    weight, first, second, weight_out, first_out, second_out, spectra, slopes, all_spectra, all_slopes = refs
     samples, modes, width = spectra.shape
-    here = pl.ds(pl.multiple_of(pl.program_id(0) * modes, 8) if modes % 8 == 0 else 0, modes)
-    for parts, target in ((spectra_parts, spectra), (slope_parts, slopes)):
-        base = 0
-        for part in parts:
-            target[pl.ds(base, part.shape[0])] = part[:, here, :]
-            base += part.shape[0]
+    start = pl.program_id(0) * modes
+
+    @pl.when(pl.program_id(0) == 0)
+    def _():
+        places = mode_rows(mode_chunk(all_spectra.shape[1]))
+        for parts, target in ((spectra_parts, all_spectra), (slope_parts, all_slopes)):
+            base = 0
+            for part in parts:
+                for first in range(0, part.shape[1], MZ):
+                    block = first // len(places) * len(places)
+                    source = pl.ds(block + places[first - block], MZ)
+                    target[pl.ds(base, part.shape[0]), pl.ds(first, MZ), :] = part[:, source, :]
+                base += part.shape[0]
+
+    here = pl.ds(pl.multiple_of(start, 8) if modes % 8 == 0 else 0, modes)
+    spectra[...] = all_spectra[:, here, :]
+    slopes[...] = all_slopes[:, here, :]
     lower = lower_half((samples, width))
     sign = lane_sign((samples, width), 1.0)
     for group in pairs_of(modes):
@@ -487,7 +555,7 @@
     spectrum = jax.ShapeDtypeStruct(spectrum_shape, f32)
     field_shape = (width, channels, cells)
     u_scratch = [pltpu.VMEM((2 * HALF, channels, cells), bf16)] * 2
-    t_scratch = [pltpu.VMEM((HALF * lanes, 2 * groups * count), bf16)] * 2
+    t_scratch = [pltpu.VMEM((HALF * lanes, cells), bf16)] * 2
     params = pltpu.CompilerParams(vmem_limit_bytes=20 * 1024 * 1024)
 
     def other_core(value):
@@ -524,12 +592,17 @@
     def to_owners(own, sent):
         got = other_core(sent)
         if not paired:
-            return [lax.all_to_all((own + got).reshape(owners, modes, lanes), "dp", 0, 0, tiled=True)]
+            total = own + got
+            places = parity_rows(per_group)[::MZ]
+            total = jnp.concatenate([total[:, :, place : place + MZ] for place in places], axis=2)
+            return [lax.all_to_all(total.reshape(owners, modes, lanes), "dp", 0, 0, tiled=True)]
         return [travel((own[i] + got[i]).reshape(1, modes, lanes), step) for i, step in enumerate(order)]
 
     def from_owners(values, steps, tie=None):
         if not paired:
-            values = [lax.all_to_all(values[0], "dp", 0, 0, tiled=True)]
+            value = lax.all_to_all(values[0], "dp", 0, 0, tiled=True).reshape(part_shape)
+            slots = list(range(0, per_group, 2)) + list(range(1, per_group, 2))
+            values = [jnp.concatenate([value[:, :, slot * MZ : (slot + 1) * MZ] for slot in slots], axis=2)]
         else:
             values = [travel(values[order.index(step)], step) for step in steps]
         if tie is not None:
@@ -608,7 +681,7 @@
         grid=(modes // block,),
         in_specs=value_specs * 2 + [weight_spec] * 3,
         out_specs=[weight_spec] * 3,
-        scratch_shapes=[pltpu.VMEM((owners, block, lanes), f32)] * 2,
+        scratch_shapes=[pltpu.VMEM((owners, rows, lanes), f32) for rows in (block, block, modes, modes)],
         compiler_params=pltpu.CompilerParams(vmem_limit_bytes=30 * 1024 * 1024),
         cost_estimate=pl.CostEstimate(flops=10**10, bytes_accessed=3 * 10**7, transcendentals=10**6),
         name="adam",

time: 110 us -> 109 us (level)
  Pallas kernels: 36.1 us -> 33.9 us
  local copies, waits for them, and re-layouts: 3.67 us -> 5.13 us
    unnamed x54 -> x58, local copies, waits for them, and re-layouts: 3.67 us -> 5.13 us
    pallas_call x1, Pallas kernels: 10.3 us -> 9.12 us  [body(): pl.pallas_call(functools.partial(middle_kernel, back_order, order), out_s...]
  transfers between devices with their start and end apart: 46 -> 46, of which waited for: 23 -> 22; matrix products, arithmetic and copies ran while one was open for 0% -> 0% of each run, Pallas kernels for 9% -> 9%
where the time goes in v3:
time: 109 us
  starting transfers between devices  49.7 us (46%)
  Pallas kernels  33.9 us (31%)
  waiting for transfers between devices  17.6 us (16%)
  local copies, waits for them, and re-layouts  5.13 us (5%)
  other arithmetic  1.35 us (1%)
    ppermute x28, starting transfers between devices, travel(): lax.ppermute(value, 'dp', [(i, i ^ step) for i in range(owners)])  44.7 us
    ppermute x28, waiting for transfers between devices, travel(): lax.ppermute(value, 'dp', [(i, i ^ step) for i in range(owners)])  11.9 us
    pallas_call x1, Pallas kernels, body(): pl.pallas_call(functools.partial(middle_kernel, back_order, order), out_s...  9.12 us
    pallas_call x1, Pallas kernels, body(): pl.pallas_call(functools.partial(adam_kernel, len(owned)), out_shape=[who...  7.65 us
    pallas_call x2, Pallas kernels, mixing(): pl.pallas_call(functools.partial(mode_kernel, chunk, len(values)), out_sh...  5.78 us
    ppermute x18, waiting for transfers between devices, other_core(): return lax.ppermute(value, 'space', [(0, 1), (1, 0)])  5.7 us
    unnamed x58, local copies, waits for them, and re-layouts  5.13 us
    ppermute x18, starting transfers between devices, other_core(): return lax.ppermute(value, 'space', [(0, 1), (1, 0)])  4.99 us
  transfers between devices with their start and end apart: 46, of which 22 were waited for; matrix products, arithmetic and copies ran while one was open for 0% of the time, Pallas kernels for 9%

profile of v3, /device:TPU:0, one launch (start us, length us, event | category | flops | bytes accessed | tf_op | source)
XLA Modules:
  0.0 108.7 jit_solution(6256143326847601)
XLA Ops:
  0.6 4.5 %first.1 = (f32[8,2,72,128]{3,2,1,0:T(8,128)}, f32[8,2,72,128]{3,2,1,0:T(8,128)}) custom-call(bf16[1,16,64,512]{3,2,1,0:T(8,128)(2,1)} %refs_16_.1, bf16[2,288,512]{2,1,0:T(8,128)(2,1)} %constant.20.clone.x_in, bf16[2,320,256]{2,1,0:T(8,128)(2,1)} %constant.18.clone.table_in.refs_18_.refs_19_), custom_call_target="tpu_custom_call" | custom-call | tf_op jit(solution)/shard_map/first/pallas_call | solution.py:569
  5.2 0.5 collective-permute-start
  5.7 1.8 %collective-permute-done = f32[8,2,72,128]{3,2,1,0:T(8,128)S(1)} collective-permute-done((f32[8,2,72,128]{3,2,1,0:T(8,128)}, f32[8,2,72,128]{3,2,1,0:T(8,128)S(1)}, u32[]{:S(2)}, u32[]{:S(2)}) %collective-permute-start) | collective-permute-done | bytes 589856 | tf_op jit(solution)/shard_map/ppermute | solution.py:562
  7.5 1.2 %slice_add_fusion.8 = (f32[1,2,72,128]{3,2,1,0:T(8,128)S(1)}, f32[1,2,72,128]{3,2,1,0:T(8,128)S(1)}, f32[1,2,72,128]{3,2,1,0:T(8,128)S(1)}, f32[1,2,72,128]{3,2,...) fusion(f32[8,2,72,128]{3,2,1,0:T(8,128)S(1)} %collective-permut, ...), kind=kLoop, calls=%fused_computation.8 | loop fusion | flops 147456 | bytes 1769472 | tf_op jit(solution)/shard_map/add | solution.py:599
  8.7 5.0 %collective-permute-start.6 = (f32[1,144,128]{2,1,0:T(8,128)S(1)}, f32[1,144,128]{2,1,0:T(8,128)S(1)}, u32[]{:S(2)}, u32[]{:S(2)}) collective-permute-start(f32[1,144,128]{2,1,0:T(8,128)S(1)} %bitcast.85), channel_id=1, source_target_pairs={{0,12},{2,14},{4,8},{6,10},{8,4},{10,6},{12,0},{14,2},{1,13},{3,15... | collective-permute-start | bytes 221192 | tf_op jit(solution)/shard_map/ppermute | solution.py:590
  13.8 1.2 %collective-permute-start.7 = (f32[1,144,128]{2,1,0:T(8,128)S(1)}, f32[1,144,128]{2,1,0:T(8,128)S(1)}, u32[]{:S(2)}, u32[]{:S(2)}) collective-permute-start(f32[1,144,128]{2,1,0:T(8,128)S(1)} %bitcast.83), channel_id=1, source_target_pairs={{0,14},{2,12},{4,10},{6,8},{8,6},{10,4},{12,2},{14,0},{1,15},{3,13... | collective-permute-start | bytes 221192 | tf_op jit(solution)/shard_map/ppermute | solution.py:590
  14.9 0.8 collective-permute-start.5
  15.7 2.0 %collective-permute-start.4 = (f32[1,144,128]{2,1,0:T(8,128)S(1)}, f32[1,144,128]{2,1,0:T(8,128)S(1)}, u32[]{:S(2)}, u32[]{:S(2)}) collective-permute-start(f32[1,144,128]{2,1,0:T(8,128)S(1)} %bitcast.81), channel_id=1, source_target_pairs={{0,8},{2,10},{4,12},{6,14},{8,0},{10,2},{12,4},{14,6},{1,9},{3,11}... | collective-permute-start | bytes 221192 | tf_op jit(solution)/shard_map/ppermute | solution.py:590
  17.7 2.3 %collective-permute-start.3 = (f32[1,144,128]{2,1,0:T(8,128)S(1)}, f32[1,144,128]{2,1,0:T(8,128)S(1)}, u32[]{:S(2)}, u32[]{:S(2)}) collective-permute-start(f32[1,144,128]{2,1,0:T(8,128)S(1)} %bitcast.79), channel_id=1, source_target_pairs={{0,6},{2,4},{4,2},{6,0},{8,14},{10,12},{12,10},{14,8},{1,7},{3,5},... | collective-permute-start | bytes 221192 | tf_op jit(solution)/shard_map/ppermute | solution.py:590
  20.0 0.8 collective-permute-start.2
  20.8 0.7 collective-permute-done.7.refs_7_
  21.5 1.7 %collective-permute-start.1 = (f32[1,144,128]{2,1,0:T(8,128)S(1)}, f32[1,144,128]{2,1,0:T(8,128)S(1)}, u32[]{:S(2)}, u32[]{:S(2)}) collective-permute-start(f32[1,144,128]{2,1,0:T(8,128)S(1)} %bitcast.75), channel_id=1, source_target_pairs={{0,2},{2,0},{4,6},{6,4},{8,10},{10,8},{12,14},{14,12},{1,3},{3,1},... | collective-permute-start | bytes 221192 | tf_op jit(solution)/shard_map/ppermute | solution.py:590
  23.2 2.3 %copy-done.23 = f32[1,16,9,64,128]{4,3,2,1,0:T(8,128)S(1)} copy-done((f32[1,16,9,64,128]{4,3,2,1,0:T(8,128)S(1)}, f32[1,16,9,64,128]{4,3,2,1,0:T(8,128)}, u32[]{:S(2)}) %copy-start.23) | copy-done | bytes 4718616
  25.5 0.6 split.1
  27.0 2.5 %mix.1 = (f32[1,144,128]{2,1,0:T(8,128)S(1)}, f32[1,144,128]{2,1,0:T(8,128)}, f32[1,144,128]{2,1,0:T(8,128)}, f32[1,144,128]{2,1,0:T(8,128)S(1)}, f32[1,144,128]...) custom-call(f32[1,144,128]{2,1,0:T(8,128)S(1)} %bitcast.40, ...), custom_call_target="tpu_custom_call" | custom-call | flops 1000000000 | bytes 100000 | tf_op jit(solution)/shard_map/mix/pallas_call | solution.py:619
  29.5 4.4 %collective-permute-start.8 = (f32[1,144,128]{2,1,0:T(8,128)S(1)}, f32[1,144,128]{2,1,0:T(8,128)}, u32[]{:S(2)}, u32[]{:S(2)}) collective-permute-start(f32[1,144,128]{2,1,0:T(8,128)S(1)} %get-tuple-element.53), channel_id=1, source_target_pairs={{0,8},{2,10},{4,12},{6,14},{8,0},{10,2},{12,4},{14,6},{1,9},{3,11}... | collective-permute-start | bytes 221192 | tf_op jit(solution)/shard_map/ppermute | solution.py:590
  34.2 2.2 %collective-permute-start.10 = (f32[1,144,128]{2,1,0:T(8,128)S(1)}, f32[1,144,128]{2,1,0:T(8,128)S(1)}, u32[]{:S(2)}, u32[]{:S(2)}) collective-permute-start(f32[1,144,128]{2,1,0:T(8,128)S(1)} %get-tuple-element.55), channel_id=1, source_target_pairs={{0,12},{2,14},{4,8},{6,10},{8,4},{10,6},{12,0},{14,2},{1,13},{3,15... | collective-permute-start | bytes 221192 | tf_op jit(solution)/shard_map/ppermute | solution.py:590
  36.4 2.3 %collective-permute-start.11 = (f32[1,144,128]{2,1,0:T(8,128)S(1)}, f32[1,144,128]{2,1,0:T(8,128)}, u32[]{:S(2)}, u32[]{:S(2)}) collective-permute-start(f32[1,144,128]{2,1,0:T(8,128)S(1)} %get-tuple-element.56), channel_id=1, source_target_pairs={{0,14},{2,12},{4,10},{6,8},{8,6},{10,4},{12,2},{14,0},{1,15},{3,13... | collective-permute-start | bytes 221192 | tf_op jit(solution)/shard_map/ppermute | solution.py:590
  38.7 2.9 %collective-permute-done.8 = f32[1,144,128]{2,1,0:T(8,128)} collective-permute-done((f32[1,144,128]{2,1,0:T(8,128)S(1)}, f32[1,144,128]{2,1,0:T(8,128)}, u32[]{:S(2)}, u32[]{:S(2)}) %collective-permute-start.8) | collective-permute-done | bytes 73760 | tf_op jit(solution)/shard_map/ppermute | solution.py:590
  41.6 2.6 %collective-permute-done.9 = f32[1,144,128]{2,1,0:T(8,128)} collective-permute-done((f32[1,144,128]{2,1,0:T(8,128)S(1)}, f32[1,144,128]{2,1,0:T(8,128)}, u32[]{:S(2)}, u32[]{:S(2)}) %collective-permute-start.9) | collective-permute-done | bytes 73760 | tf_op jit(solution)/shard_map/ppermute | solution.py:590
  44.2 1.2 %collective-permute-start.14 = (f32[1,144,128]{2,1,0:T(8,128)}, f32[1,144,128]{2,1,0:T(8,128)}, u32[]{:S(2)}, u32[]{:S(2)}) collective-permute-start(f32[1,144,128]{2,1,0:T(8,128)} %get-tuple-element.59), channel_id=1, source_target_pairs={{0,2},{2,0},{4,6},{6,4},{8,10},{10,8},{12,14},{14,12},{1,3},{3,1},... | collective-permute-start | bytes 221192 | tf_op jit(solution)/shard_map/ppermute | solution.py:590
  45.4 0.6 copy-done.6
  46.1 0.6 collective-permute-start.15
  47.2 1.7 %collective-permute-done.14 = f32[1,144,128]{2,1,0:T(8,128)} collective-permute-done((f32[1,144,128]{2,1,0:T(8,128)}, f32[1,144,128]{2,1,0:T(8,128)}, u32[]{:S(2)}, u32[]{:S(2)}) %collective-permute-start.14) | collective-permute-done | bytes 73760 | tf_op jit(solution)/shard_map/ppermute | solution.py:590
  48.9 0.5 collective-permute-start.19
  51.1 1.2 %copy-done.5 = bf16[2,288,768]{2,1,0:T(8,128)(2,1)S(1)} copy-done((bf16[2,288,768]{2,1,0:T(8,128)(2,1)S(1)}, bf16[2,288,768]{2,1,0:T(8,128)(2,1)}, u32[]{:S(2)}) %copy-start.5) | copy-done | bytes 884760
  52.3 0.9 copy-done.7
  53.1 9.1 %middle.1 = (f32[8,2,72,128]{3,2,1,0:T(8,128)S(1)}, f32[8,2,72,128]{3,2,1,0:T(8,128)S(1)}, bf16[16,64,512]{2,1,0:T(8,128)(2,1)S(1)}, bf16[16,64,512]{2,1,0:T(8,128)(2,1)S(1)}) custom-call(s32[2]{0:T(128)S(1)} %pad_add_fusion.place, f32[2,72,128]{2,1,0:T(8,128)} %bitcast.11.refs_0_, f32[2,72,128]{2,1,0:T(8,128)} %bitcast.12.refs_1_, ...), custom_call_target="tpu_custom_call" | custom-call | tf_op jit(solution)/shard_map/middle/pallas_call | solution.py:647
  62.7 1.6 %collective-permute-done.23 = f32[8,2,72,128]{3,2,1,0:T(8,128)S(1)} collective-permute-done((f32[8,2,72,128]{3,2,1,0:T(8,128)S(1)}, f32[8,2,72,128]{3,2,1,0:T(8,128)S(1)}, u32[]{:S(2)}, u32[]{:S(2)}) %collective-permute-start.23) | collective-permute-done | bytes 589856 | tf_op jit(solution)/shard_map/ppermute | solution.py:562
  64.4 1.9 %collective-permute-start.29 = (f32[1,144,128]{2,1,0:T(8,128)S(1)}, f32[1,144,128]{2,1,0:T(8,128)S(1)}, u32[]{:S(2)}, u32[]{:S(2)}) collective-permute-start(f32[1,144,128]{2,1,0:T(8,128)S(1)} %bitcast.86), channel_id=1, source_target_pairs={{0,12},{2,14},{4,8},{6,10},{8,4},{10,6},{12,0},{14,2},{1,13},{3,15... | collective-permute-start | bytes 221192 | tf_op jit(solution)/shard_map/ppermute | solution.py:590
  66.3 2.7 %collective-permute-start.30 = (f32[1,144,128]{2,1,0:T(8,128)S(1)}, f32[1,144,128]{2,1,0:T(8,128)S(1)}, u32[]{:S(2)}, u32[]{:S(2)}) collective-permute-start(f32[1,144,128]{2,1,0:T(8,128)S(1)} %bitcast.84), channel_id=1, source_target_pairs={{0,14},{2,12},{4,10},{6,8},{8,6},{10,4},{12,2},{14,0},{1,15},{3,13... | collective-permute-start | bytes 221192 | tf_op jit(solution)/shard_map/ppermute | solution.py:590
  68.9 3.2 %collective-permute-start.27 = (f32[1,144,128]{2,1,0:T(8,128)S(1)}, f32[1,144,128]{2,1,0:T(8,128)S(1)}, u32[]{:S(2)}, u32[]{:S(2)}) collective-permute-start(f32[1,144,128]{2,1,0:T(8,128)S(1)} %bitcast.78), channel_id=1, source_target_pairs={{0,8},{2,10},{4,12},{6,14},{8,0},{10,2},{12,4},{14,6},{1,9},{3,11}... | collective-permute-start | bytes 221192 | tf_op jit(solution)/shard_map/ppermute | solution.py:590
  72.1 2.6 %collective-permute-start.25 = (f32[1,144,128]{2,1,0:T(8,128)S(1)}, f32[1,144,128]{2,1,0:T(8,128)S(1)}, u32[]{:S(2)}, u32[]{:S(2)}) collective-permute-start(f32[1,144,128]{2,1,0:T(8,128)S(1)} %bitcast.74), channel_id=1, source_target_pairs={{0,4},{2,6},{4,0},{6,2},{8,12},{10,14},{12,8},{14,10},{1,5},{3,7},... | collective-permute-start | bytes 221192 | tf_op jit(solution)/shard_map/ppermute | solution.py:590
  74.8 0.8 collective-permute-start.24
  75.7 2.0 %local.1 = (f32[16,64,512]{2,1,0:T(8,128)S(1)}, bf16[144,64,128]{2,1,0:T(8,128)(2,1)S(1)}, bf16[144,64,128]{2,1,0:T(8,128)(2,1)S(1)}) custom-call(bf16[16,64,512]{2,1,0:T(8,128)(2,1)S(1)} %get-tuple-element.64.slope_high, bf16[16,64,512]{2,1,0:T(8,128)(2,1)S(1)} %get-tuple-element.65.slope_low, f32[64,64]{1,0:T(8,128)S(1)} %copy-done.22, ...), custom_call_target="tpu_custom_call" | custom-call | flops 6000000000 | bytes 100000 | tf_op jit(solution)/shard_map/local/pallas_call | solution.py:665
  78.0 1.1 collective-permute-done.27.refs_4_.refs_12_
  79.1 1.2 %collective-permute-done.26.refs_3_.refs_11_ = f32[1,144,128]{2,1,0:T(8,128)S(1)} collective-permute-done((f32[1,144,128]{2,1,0:T(8,128)S(1)}, f32[1,144,128]{2,1,0:T(8,128)S(1)}, u32[]{:S(2)}, u32[]{:S(2)}) %collective-permute-start.26) | collective-permute-done | bytes 73760 | tf_op jit(solution)/shard_map/ppermute | solution.py:590
  80.3 0.6 collective-permute-done.25.refs_2_.refs_10_
  80.9 3.3 %adjoint.1 = (f32[1,144,128]{2,1,0:T(8,128)S(1)}, f32[1,144,128]{2,1,0:T(8,128)S(1)}, f32[1,144,128]{2,1,0:T(8,128)S(1)}, f32[1,144,128]{2,1,0:T(8,128)S(1)}, f3...) custom-call(f32[1,144,128]{2,1,0:T(8,128)S(1)} %bitcast.42, ...), custom_call_target="tpu_custom_call" | custom-call | flops 1000000000 | bytes 100000 | tf_op jit(solution)/shard_map/adjoint/pallas_call | solution.py:619
  84.2 0.8 collective-permute-start.31
  85.0 2.3 %collective-permute-start.33 = (f32[1,144,128]{2,1,0:T(8,128)S(1)}, f32[1,144,128]{2,1,0:T(8,128)S(1)}, u32[]{:S(2)}, u32[]{:S(2)}) collective-permute-start(f32[1,144,128]{2,1,0:T(8,128)S(1)} %get-tuple-element.71), channel_id=1, source_target_pairs={{0,8},{2,10},{4,12},{6,14},{8,0},{10,2},{12,4},{14,6},{1,9},{3,11}... | collective-permute-start | bytes 221192 | tf_op jit(solution)/shard_map/ppermute | solution.py:590
  87.3 1.3 %collective-permute-start.34 = (f32[1,144,128]{2,1,0:T(8,128)S(1)}, f32[1,144,128]{2,1,0:T(8,128)S(1)}, u32[]{:S(2)}, u32[]{:S(2)}) collective-permute-start(f32[1,144,128]{2,1,0:T(8,128)S(1)} %get-tuple-element.72), channel_id=1, source_target_pairs={{0,10},{2,8},{4,14},{6,12},{8,2},{10,0},{12,6},{14,4},{1,11},{3,9}... | collective-permute-start | bytes 221192 | tf_op jit(solution)/shard_map/ppermute | solution.py:590
  88.6 1.5 %collective-permute-start.35 = (f32[1,144,128]{2,1,0:T(8,128)S(1)}, f32[1,144,128]{2,1,0:T(8,128)S(1)}, u32[]{:S(2)}, u32[]{:S(2)}) collective-permute-start(f32[1,144,128]{2,1,0:T(8,128)S(1)} %get-tuple-element.73), channel_id=1, source_target_pairs={{0,12},{2,14},{4,8},{6,10},{8,4},{10,6},{12,0},{14,2},{1,13},{3,15... | collective-permute-start | bytes 221192 | tf_op jit(solution)/shard_map/ppermute | solution.py:590
  90.2 2.5 %collective-permute-start.36 = (f32[1,144,128]{2,1,0:T(8,128)S(1)}, f32[1,144,128]{2,1,0:T(8,128)S(1)}, u32[]{:S(2)}, u32[]{:S(2)}) collective-permute-start(f32[1,144,128]{2,1,0:T(8,128)S(1)} %get-tuple-element.74), channel_id=1, source_target_pairs={{0,14},{2,12},{4,10},{6,8},{8,6},{10,4},{12,2},{14,0},{1,15},{3,13... | collective-permute-start | bytes 221192 | tf_op jit(solution)/shard_map/ppermute | solution.py:590
  92.6 0.9 collective-permute-start.37
  93.7 7.7 %adam.1 = (f32[144,64,128]{2,1,0:T(8,128)}, f32[144,64,128]{2,1,0:T(8,128)}, f32[144,64,128]{2,1,0:T(8,128)}) custom-call(f32[1,144,128]{2,1,0:T(8,128)S(1)} %bitcast.41, f32[1,144,128]{2,1,0:T(8,128)S(1)} %copy-done.21, f32[1,144,128]{2,1,0:T(8,128)S(1)} %copy-done.19, f32[1,144,128]{2,1,0:T(8,128)S(1)} %copy-done.17, f32[1,144,128]{2,1,0:T(8,128)S(1)} %copy-done.15, ...), custom_call_target="tpu_custom_call" | custom-call | flops 10000000000 | bytes 30000000 | tf_op jit(solution)/shard_map/adam/pallas_call | solution.py:678
  101.5 0.5 collective-permute-start.38
  104.5 4.2 %last.1 = bf16[1,16,64,512]{3,2,1,0:T(8,128)(2,1)} custom-call(s32[2]{0:T(128)S(1)} %pad_add_fusion.place, f32[2,72,128]{2,1,0:T(8,128)S(1)} %bitcast.49, f32[2,72,128]{2,1,0:T(8,128)S(1)} %bitcast.51, f32[2,72,128]{2,1,0:T(8,128)S(1)} %bitcast.53, f32[2,72,128]{2,1,0:T(8,128)S(1)} %bitcast.55, f32[2,72,128]{2,1,0:T(8,128)S(1)} %bitcast.59, ...), custom_call_target="tpu_custom_call" | custom-call | tf_op jit(solution)/shard_map/last/pallas_call | solution.py:691
  (115 shorter events, 6.8 us)
Async XLA Ops:
  5.2 2.4 %collective-permute-start = (f32[8,2,72,128]{3,2,1,0:T(8,128)}, f32[8,2,72,128]{3,2,1,0:T(8,128)S(1)}, u32[]{:S(2)}, u32[]{:S(2)}) collective-permute-start(f32[8,2,72,128]{3,2,1,0:T(8,128)} %get-tuple-element.50), channel_id=1, source_target_pairs={{0,1},{1,0},{2,3},{3,2},{4,5},{5,4},{6,7},{7,6},{8,9},{9,8},{10,11... | collective-permute-start | bytes 1769480 | tf_op jit(solution)/shard_map/ppermute | solution.py:562
  8.7 11.2 %collective-permute-start.6 = (f32[1,144,128]{2,1,0:T(8,128)S(1)}, f32[1,144,128]{2,1,0:T(8,128)S(1)}, u32[]{:S(2)}, u32[]{:S(2)}) collective-permute-start(f32[1,144,128]{2,1,0:T(8,128)S(1)} %bitcast.85), channel_id=1, source_target_pairs={{0,12},{2,14},{4,8},{6,10},{8,4},{10,6},{12,0},{14,2},{1,13},{3,15... | collective-permute-start | bytes 221192 | tf_op jit(solution)/shard_map/ppermute | solution.py:590
  13.8 7.7 %collective-permute-start.7 = (f32[1,144,128]{2,1,0:T(8,128)S(1)}, f32[1,144,128]{2,1,0:T(8,128)S(1)}, u32[]{:S(2)}, u32[]{:S(2)}) collective-permute-start(f32[1,144,128]{2,1,0:T(8,128)S(1)} %bitcast.83), channel_id=1, source_target_pairs={{0,14},{2,12},{4,10},{6,8},{8,6},{10,4},{12,2},{14,0},{1,15},{3,13... | collective-permute-start | bytes 221192 | tf_op jit(solution)/shard_map/ppermute | solution.py:590
  14.9 11.6 %collective-permute-start.5 = (f32[1,144,128]{2,1,0:T(8,128)S(1)}, f32[1,144,128]{2,1,0:T(8,128)S(1)}, u32[]{:S(2)}, u32[]{:S(2)}) collective-permute-start(f32[1,144,128]{2,1,0:T(8,128)S(1)} %bitcast.82), channel_id=1, source_target_pairs={{0,10},{2,8},{4,14},{6,12},{8,2},{10,0},{12,6},{14,4},{1,11},{3,9}... | collective-permute-start | bytes 221192 | tf_op jit(solution)/shard_map/ppermute | solution.py:590
  15.7 11.0 %collective-permute-start.4 = (f32[1,144,128]{2,1,0:T(8,128)S(1)}, f32[1,144,128]{2,1,0:T(8,128)S(1)}, u32[]{:S(2)}, u32[]{:S(2)}) collective-permute-start(f32[1,144,128]{2,1,0:T(8,128)S(1)} %bitcast.81), channel_id=1, source_target_pairs={{0,8},{2,10},{4,12},{6,14},{8,0},{10,2},{12,4},{14,6},{1,9},{3,11}... | collective-permute-start | bytes 221192 | tf_op jit(solution)/shard_map/ppermute | solution.py:590
  17.7 9.0 %collective-permute-start.3 = (f32[1,144,128]{2,1,0:T(8,128)S(1)}, f32[1,144,128]{2,1,0:T(8,128)S(1)}, u32[]{:S(2)}, u32[]{:S(2)}) collective-permute-start(f32[1,144,128]{2,1,0:T(8,128)S(1)} %bitcast.79), channel_id=1, source_target_pairs={{0,6},{2,4},{4,2},{6,0},{8,14},{10,12},{12,10},{14,8},{1,7},{3,5},... | collective-permute-start | bytes 221192 | tf_op jit(solution)/shard_map/ppermute | solution.py:590
  20.0 7.0 %collective-permute-start.2 = (f32[1,144,128]{2,1,0:T(8,128)S(1)}, f32[1,144,128]{2,1,0:T(8,128)S(1)}, u32[]{:S(2)}, u32[]{:S(2)}) collective-permute-start(f32[1,144,128]{2,1,0:T(8,128)S(1)} %bitcast.77), channel_id=1, source_target_pairs={{0,4},{2,6},{4,0},{6,2},{8,12},{10,14},{12,8},{14,10},{1,5},{3,7},... | collective-permute-start | bytes 221192 | tf_op jit(solution)/shard_map/ppermute | solution.py:590
  21.5 5.5 %collective-permute-start.1 = (f32[1,144,128]{2,1,0:T(8,128)S(1)}, f32[1,144,128]{2,1,0:T(8,128)S(1)}, u32[]{:S(2)}, u32[]{:S(2)}) collective-permute-start(f32[1,144,128]{2,1,0:T(8,128)S(1)} %bitcast.75), channel_id=1, source_target_pairs={{0,2},{2,0},{4,6},{6,4},{8,10},{10,8},{12,14},{14,12},{1,3},{3,1},... | collective-permute-start | bytes 221192 | tf_op jit(solution)/shard_map/ppermute | solution.py:590
  26.2 24.9 %copy-start = (bf16[1,16,64,512]{3,2,1,0:T(8,128)(2,1)S(1)}, bf16[1,16,64,512]{3,2,1,0:T(8,128)(2,1)}, u32[]{:S(2)}) copy-start(bf16[1,16,64,512]{3,2,1,0:T(8,128)(2,1)} %refs_16_.1) | copy-start | bytes 3145732
  26.2 24.9 %copy-start.1 = (bf16[2,256,864]{2,1,0:T(8,128)(2,1)S(1)}, bf16[2,256,864]{2,1,0:T(8,128)(2,1)}, u32[]{:S(2)}) copy-start(bf16[2,256,864]{2,1,0:T(8,128)(2,1)} %constant.22.clone.refs_19_.refs_17_) | copy-start | bytes 2654212
  29.5 12.1 %collective-permute-start.8 = (f32[1,144,128]{2,1,0:T(8,128)S(1)}, f32[1,144,128]{2,1,0:T(8,128)}, u32[]{:S(2)}, u32[]{:S(2)}) collective-permute-start(f32[1,144,128]{2,1,0:T(8,128)S(1)} %get-tuple-element.53), channel_id=1, source_target_pairs={{0,8},{2,10},{4,12},{6,14},{8,0},{10,2},{12,4},{14,6},{1,9},{3,11}... | collective-permute-start | bytes 221192 | tf_op jit(solution)/shard_map/ppermute | solution.py:590
  33.9 10.3 %collective-permute-start.9 = (f32[1,144,128]{2,1,0:T(8,128)S(1)}, f32[1,144,128]{2,1,0:T(8,128)}, u32[]{:S(2)}, u32[]{:S(2)}) collective-permute-start(f32[1,144,128]{2,1,0:T(8,128)S(1)} %get-tuple-element.54), channel_id=1, source_target_pairs={{0,10},{2,8},{4,14},{6,12},{8,2},{10,0},{12,6},{14,4},{1,11},{3,9}... | collective-permute-start | bytes 221192 | tf_op jit(solution)/shard_map/ppermute | solution.py:590
  34.2 11.2 %collective-permute-start.10 = (f32[1,144,128]{2,1,0:T(8,128)S(1)}, f32[1,144,128]{2,1,0:T(8,128)S(1)}, u32[]{:S(2)}, u32[]{:S(2)}) collective-permute-start(f32[1,144,128]{2,1,0:T(8,128)S(1)} %get-tuple-element.55), channel_id=1, source_target_pairs={{0,12},{2,14},{4,8},{6,10},{8,4},{10,6},{12,0},{14,2},{1,13},{3,15... | collective-permute-start | bytes 221192 | tf_op jit(solution)/shard_map/ppermute | solution.py:590
  36.4 9.7 %collective-permute-start.11 = (f32[1,144,128]{2,1,0:T(8,128)S(1)}, f32[1,144,128]{2,1,0:T(8,128)}, u32[]{:S(2)}, u32[]{:S(2)}) collective-permute-start(f32[1,144,128]{2,1,0:T(8,128)S(1)} %get-tuple-element.56), channel_id=1, source_target_pairs={{0,14},{2,12},{4,10},{6,8},{8,6},{10,4},{12,2},{14,0},{1,15},{3,13... | collective-permute-start | bytes 221192 | tf_op jit(solution)/shard_map/ppermute | solution.py:590
  38.7 8.0 %collective-permute-start.12 = (f32[1,144,128]{2,1,0:T(8,128)S(1)}, f32[1,144,128]{2,1,0:T(8,128)}, u32[]{:S(2)}, u32[]{:S(2)}) collective-permute-start(f32[1,144,128]{2,1,0:T(8,128)S(1)} %get-tuple-element.57), channel_id=1, source_target_pairs={{0,6},{2,4},{4,2},{6,0},{8,14},{10,12},{12,10},{14,8},{1,7},{3,5},... | collective-permute-start | bytes 221192 | tf_op jit(solution)/shard_map/ppermute | solution.py:590
  41.6 5.2 %collective-permute-start.13 = (f32[1,144,128]{2,1,0:T(8,128)}, f32[1,144,128]{2,1,0:T(8,128)}, u32[]{:S(2)}, u32[]{:S(2)}) collective-permute-start(f32[1,144,128]{2,1,0:T(8,128)} %get-tuple-element.58), channel_id=1, source_target_pairs={{0,4},{2,6},{4,0},{6,2},{8,12},{10,14},{12,8},{14,10},{1,5},{3,7},... | collective-permute-start | bytes 221192 | tf_op jit(solution)/shard_map/ppermute | solution.py:590
  44.2 4.7 %collective-permute-start.14 = (f32[1,144,128]{2,1,0:T(8,128)}, f32[1,144,128]{2,1,0:T(8,128)}, u32[]{:S(2)}, u32[]{:S(2)}) collective-permute-start(f32[1,144,128]{2,1,0:T(8,128)} %get-tuple-element.59), channel_id=1, source_target_pairs={{0,2},{2,0},{4,6},{6,4},{8,10},{10,8},{12,14},{14,12},{1,3},{3,1},... | collective-permute-start | bytes 221192 | tf_op jit(solution)/shard_map/ppermute | solution.py:590
  46.0 2.9 %collective-permute-start.22 = (f32[2,72,128]{2,1,0:T(8,128)S(1)}, f32[2,72,128]{2,1,0:T(8,128)}, u32[]{:S(2)}, u32[]{:S(2)}) collective-permute-start(f32[2,72,128]{2,1,0:T(8,128)S(1)} %bitcast.46), channel_id=1, source_target_pairs={{0,1},{1,0},{2,3},{3,2},{4,5},{5,4},{6,7},{7,6},{8,9},{9,8},{10,11... | collective-permute-start | bytes 221192 | tf_op jit(solution)/shard_map/ppermute | solution.py:562
  46.1 3.3 %collective-permute-start.15 = (f32[2,72,128]{2,1,0:T(8,128)}, f32[2,72,128]{2,1,0:T(8,128)}, u32[]{:S(2)}, u32[]{:S(2)}) collective-permute-start(f32[2,72,128]{2,1,0:T(8,128)} %bitcast.11.refs_0_), channel_id=1, source_target_pairs={{0,1},{1,0},{2,3},{3,2},{4,5},{5,4},{6,7},{7,6},{8,9},{9,8},{10,11... | collective-permute-start | bytes 221192 | tf_op jit(solution)/shard_map/ppermute | solution.py:562
  46.7 2.8 %collective-permute-start.16 = (f32[2,72,128]{2,1,0:T(8,128)}, f32[2,72,128]{2,1,0:T(8,128)}, u32[]{:S(2)}, u32[]{:S(2)}) collective-permute-start(f32[2,72,128]{2,1,0:T(8,128)} %bitcast.12.refs_1_), channel_id=1, source_target_pairs={{0,1},{1,0},{2,3},{3,2},{4,5},{5,4},{6,7},{7,6},{8,9},{9,8},{10,11... | collective-permute-start | bytes 221192 | tf_op jit(solution)/shard_map/ppermute | solution.py:562
  46.8 3.3 %collective-permute-start.17 = (f32[2,72,128]{2,1,0:T(8,128)}, f32[2,72,128]{2,1,0:T(8,128)S(1)}, u32[]{:S(2)}, u32[]{:S(2)}) collective-permute-start(f32[2,72,128]{2,1,0:T(8,128)} %bitcast.56), channel_id=1, source_target_pairs={{0,1},{1,0},{2,3},{3,2},{4,5},{5,4},{6,7},{7,6},{8,9},{9,8},{10,11... | collective-permute-start | bytes 221192 | tf_op jit(solution)/shard_map/ppermute | solution.py:562
  48.9 1.5 %collective-permute-start.18 = (f32[2,72,128]{2,1,0:T(8,128)}, f32[2,72,128]{2,1,0:T(8,128)S(1)}, u32[]{:S(2)}, u32[]{:S(2)}) collective-permute-start(f32[2,72,128]{2,1,0:T(8,128)} %bitcast.14.refs_3_), channel_id=1, source_target_pairs={{0,1},{1,0},{2,3},{3,2},{4,5},{5,4},{6,7},{7,6},{8,9},{9,8},{10,11... | collective-permute-start | bytes 221192 | tf_op jit(solution)/shard_map/ppermute | solution.py:562
  48.9 1.6 %collective-permute-start.19 = (f32[2,72,128]{2,1,0:T(8,128)}, f32[2,72,128]{2,1,0:T(8,128)S(1)}, u32[]{:S(2)}, u32[]{:S(2)}) collective-permute-start(f32[2,72,128]{2,1,0:T(8,128)} %bitcast.15.refs_4_), channel_id=1, source_target_pairs={{0,1},{1,0},{2,3},{3,2},{4,5},{5,4},{6,7},{7,6},{8,9},{9,8},{10,11... | collective-permute-start | bytes 221192 | tf_op jit(solution)/shard_map/ppermute | solution.py:562
  49.4 1.5 %collective-permute-start.20 = (f32[2,72,128]{2,1,0:T(8,128)}, f32[2,72,128]{2,1,0:T(8,128)S(1)}, u32[]{:S(2)}, u32[]{:S(2)}) collective-permute-start(f32[2,72,128]{2,1,0:T(8,128)} %bitcast.16.refs_5_), channel_id=1, source_target_pairs={{0,1},{1,0},{2,3},{3,2},{4,5},{5,4},{6,7},{7,6},{8,9},{9,8},{10,11... | collective-permute-start | bytes 221192 | tf_op jit(solution)/shard_map/ppermute | solution.py:562
  49.5 1.6 %collective-permute-start.21 = (f32[2,72,128]{2,1,0:T(8,128)}, f32[2,72,128]{2,1,0:T(8,128)S(1)}, u32[]{:S(2)}, u32[]{:S(2)}) collective-permute-start(f32[2,72,128]{2,1,0:T(8,128)} %bitcast.17.refs_6_), channel_id=1, source_target_pairs={{0,1},{1,0},{2,3},{3,2},{4,5},{5,4},{6,7},{7,6},{8,9},{9,8},{10,11... | collective-permute-start | bytes 221192 | tf_op jit(solution)/shard_map/ppermute | solution.py:562
  62.3 2.1 %collective-permute-start.23 = (f32[8,2,72,128]{3,2,1,0:T(8,128)S(1)}, f32[8,2,72,128]{3,2,1,0:T(8,128)S(1)}, u32[]{:S(2)}, u32[]{:S(2)}) collective-permute-start(f32[8,2,72,128]{3,2,1,0:T(8,128)S(1)} %get-tuple-element.63), channel_id=1, source_target_pairs={{0,1},{1,0},{2,3},{3,2},{4,5},{5,4},{6,7},{7,6},{8,9},{9,8},{10,11... | collective-permute-start | bytes 1769480 | tf_op jit(solution)/shard_map/ppermute | solution.py:562
  64.4 7.7 %collective-permute-start.29 = (f32[1,144,128]{2,1,0:T(8,128)S(1)}, f32[1,144,128]{2,1,0:T(8,128)S(1)}, u32[]{:S(2)}, u32[]{:S(2)}) collective-permute-start(f32[1,144,128]{2,1,0:T(8,128)S(1)} %bitcast.86), channel_id=1, source_target_pairs={{0,12},{2,14},{4,8},{6,10},{8,4},{10,6},{12,0},{14,2},{1,13},{3,15... | collective-permute-start | bytes 221192 | tf_op jit(solution)/shard_map/ppermute | solution.py:590
  66.3 8.5 %collective-permute-start.30 = (f32[1,144,128]{2,1,0:T(8,128)S(1)}, f32[1,144,128]{2,1,0:T(8,128)S(1)}, u32[]{:S(2)}, u32[]{:S(2)}) collective-permute-start(f32[1,144,128]{2,1,0:T(8,128)S(1)} %bitcast.84), channel_id=1, source_target_pairs={{0,14},{2,12},{4,10},{6,8},{8,6},{10,4},{12,2},{14,0},{1,15},{3,13... | collective-permute-start | bytes 221192 | tf_op jit(solution)/shard_map/ppermute | solution.py:590
  68.9 9.1 %collective-permute-start.28 = (f32[1,144,128]{2,1,0:T(8,128)S(1)}, f32[1,144,128]{2,1,0:T(8,128)S(1)}, u32[]{:S(2)}, u32[]{:S(2)}) collective-permute-start(f32[1,144,128]{2,1,0:T(8,128)S(1)} %bitcast.80), channel_id=1, source_target_pairs={{0,10},{2,8},{4,14},{6,12},{8,2},{10,0},{12,6},{14,4},{1,11},{3,9}... | collective-permute-start | bytes 221192 | tf_op jit(solution)/shard_map/ppermute | solution.py:590
  68.9 10.2 %collective-permute-start.27 = (f32[1,144,128]{2,1,0:T(8,128)S(1)}, f32[1,144,128]{2,1,0:T(8,128)S(1)}, u32[]{:S(2)}, u32[]{:S(2)}) collective-permute-start(f32[1,144,128]{2,1,0:T(8,128)S(1)} %bitcast.78), channel_id=1, source_target_pairs={{0,8},{2,10},{4,12},{6,14},{8,0},{10,2},{12,4},{14,6},{1,9},{3,11}... | collective-permute-start | bytes 221192 | tf_op jit(solution)/shard_map/ppermute | solution.py:590
  72.1 8.1 %collective-permute-start.26 = (f32[1,144,128]{2,1,0:T(8,128)S(1)}, f32[1,144,128]{2,1,0:T(8,128)S(1)}, u32[]{:S(2)}, u32[]{:S(2)}) collective-permute-start(f32[1,144,128]{2,1,0:T(8,128)S(1)} %bitcast.76), channel_id=1, source_target_pairs={{0,6},{2,4},{4,2},{6,0},{8,14},{10,12},{12,10},{14,8},{1,7},{3,5},... | collective-permute-start | bytes 221192 | tf_op jit(solution)/shard_map/ppermute | solution.py:590
  72.1 8.8 %collective-permute-start.25 = (f32[1,144,128]{2,1,0:T(8,128)S(1)}, f32[1,144,128]{2,1,0:T(8,128)S(1)}, u32[]{:S(2)}, u32[]{:S(2)}) collective-permute-start(f32[1,144,128]{2,1,0:T(8,128)S(1)} %bitcast.74), channel_id=1, source_target_pairs={{0,4},{2,6},{4,0},{6,2},{8,12},{10,14},{12,8},{14,10},{1,5},{3,7},... | collective-permute-start | bytes 221192 | tf_op jit(solution)/shard_map/ppermute | solution.py:590
  74.8 6.1 %collective-permute-start.24 = (f32[1,144,128]{2,1,0:T(8,128)S(1)}, f32[1,144,128]{2,1,0:T(8,128)S(1)}, u32[]{:S(2)}, u32[]{:S(2)}) collective-permute-start(f32[1,144,128]{2,1,0:T(8,128)S(1)} %bitcast.73), channel_id=1, source_target_pairs={{0,2},{2,0},{4,6},{6,4},{8,10},{10,8},{12,14},{14,12},{1,3},{3,1},... | collective-permute-start | bytes 221192 | tf_op jit(solution)/shard_map/ppermute | solution.py:590
  84.2 6.0 %collective-permute-start.31 = (f32[1,144,128]{2,1,0:T(8,128)S(1)}, f32[1,144,128]{2,1,0:T(8,128)S(1)}, u32[]{:S(2)}, u32[]{:S(2)}) collective-permute-start(f32[1,144,128]{2,1,0:T(8,128)S(1)} %get-tuple-element.69), channel_id=1, source_target_pairs={{0,2},{2,0},{4,6},{6,4},{8,10},{10,8},{12,14},{14,12},{1,3},{3,1},... | collective-permute-start | bytes 221192 | tf_op jit(solution)/shard_map/ppermute | solution.py:590
  85.0 7.7 %collective-permute-start.32 = (f32[1,144,128]{2,1,0:T(8,128)S(1)}, f32[1,144,128]{2,1,0:T(8,128)S(1)}, u32[]{:S(2)}, u32[]{:S(2)}) collective-permute-start(f32[1,144,128]{2,1,0:T(8,128)S(1)} %get-tuple-element.70), channel_id=1, source_target_pairs={{0,4},{2,6},{4,0},{6,2},{8,12},{10,14},{12,8},{14,10},{1,5},{3,7},... | collective-permute-start | bytes 221192 | tf_op jit(solution)/shard_map/ppermute | solution.py:590
  85.0 16.4 %collective-permute-start.33 = (f32[1,144,128]{2,1,0:T(8,128)S(1)}, f32[1,144,128]{2,1,0:T(8,128)S(1)}, u32[]{:S(2)}, u32[]{:S(2)}) collective-permute-start(f32[1,144,128]{2,1,0:T(8,128)S(1)} %get-tuple-element.71), channel_id=1, source_target_pairs={{0,8},{2,10},{4,12},{6,14},{8,0},{10,2},{12,4},{14,6},{1,9},{3,11}... | collective-permute-start | bytes 221192 | tf_op jit(solution)/shard_map/ppermute | solution.py:590
  87.3 14.0 %collective-permute-start.34 = (f32[1,144,128]{2,1,0:T(8,128)S(1)}, f32[1,144,128]{2,1,0:T(8,128)S(1)}, u32[]{:S(2)}, u32[]{:S(2)}) collective-permute-start(f32[1,144,128]{2,1,0:T(8,128)S(1)} %get-tuple-element.72), channel_id=1, source_target_pairs={{0,10},{2,8},{4,14},{6,12},{8,2},{10,0},{12,6},{14,4},{1,11},{3,9}... | collective-permute-start | bytes 221192 | tf_op jit(solution)/shard_map/ppermute | solution.py:590
  88.6 12.7 %collective-permute-start.35 = (f32[1,144,128]{2,1,0:T(8,128)S(1)}, f32[1,144,128]{2,1,0:T(8,128)S(1)}, u32[]{:S(2)}, u32[]{:S(2)}) collective-permute-start(f32[1,144,128]{2,1,0:T(8,128)S(1)} %get-tuple-element.73), channel_id=1, source_target_pairs={{0,12},{2,14},{4,8},{6,10},{8,4},{10,6},{12,0},{14,2},{1,13},{3,15... | collective-permute-start | bytes 221192 | tf_op jit(solution)/shard_map/ppermute | solution.py:590
  90.2 11.2 %collective-permute-start.36 = (f32[1,144,128]{2,1,0:T(8,128)S(1)}, f32[1,144,128]{2,1,0:T(8,128)S(1)}, u32[]{:S(2)}, u32[]{:S(2)}) collective-permute-start(f32[1,144,128]{2,1,0:T(8,128)S(1)} %get-tuple-element.74), channel_id=1, source_target_pairs={{0,14},{2,12},{4,10},{6,8},{8,6},{10,4},{12,2},{14,0},{1,15},{3,13... | collective-permute-start | bytes 221192 | tf_op jit(solution)/shard_map/ppermute | solution.py:590
  92.6 8.7 %collective-permute-start.37 = (f32[1,144,128]{2,1,0:T(8,128)S(1)}, f32[1,144,128]{2,1,0:T(8,128)S(1)}, u32[]{:S(2)}, u32[]{:S(2)}) collective-permute-start(f32[1,144,128]{2,1,0:T(8,128)S(1)} %get-tuple-element.75), channel_id=1, source_target_pairs={{0,6},{2,4},{4,2},{6,0},{8,14},{10,12},{12,10},{14,8},{1,7},{3,5},... | collective-permute-start | bytes 221192 | tf_op jit(solution)/shard_map/ppermute | solution.py:590
  101.4 1.3 %collective-permute-start.39 = (f32[2,72,128]{2,1,0:T(8,128)S(1)}, f32[2,72,128]{2,1,0:T(8,128)S(1)}, u32[]{:S(2)}, u32[]{:S(2)}) collective-permute-start(f32[2,72,128]{2,1,0:T(8,128)S(1)} %bitcast.50), channel_id=1, source_target_pairs={{0,1},{1,0},{2,3},{3,2},{4,5},{5,4},{6,7},{7,6},{8,9},{9,8},{10,11... | collective-permute-start | bytes 221192 | tf_op jit(solution)/shard_map/ppermute | solution.py:562
  101.5 1.5 %collective-permute-start.38 = (f32[2,72,128]{2,1,0:T(8,128)S(1)}, f32[2,72,128]{2,1,0:T(8,128)S(1)}, u32[]{:S(2)}, u32[]{:S(2)}) collective-permute-start(f32[2,72,128]{2,1,0:T(8,128)S(1)} %bitcast.48), channel_id=1, source_target_pairs={{0,1},{1,0},{2,3},{3,2},{4,5},{5,4},{6,7},{7,6},{8,9},{9,8},{10,11... | collective-permute-start | bytes 221192 | tf_op jit(solution)/shard_map/ppermute | solution.py:562
  102.0 1.3 %collective-permute-start.40 = (f32[2,72,128]{2,1,0:T(8,128)S(1)}, f32[2,72,128]{2,1,0:T(8,128)S(1)}, u32[]{:S(2)}, u32[]{:S(2)}) collective-permute-start(f32[2,72,128]{2,1,0:T(8,128)S(1)} %bitcast.52), channel_id=1, source_target_pairs={{0,1},{1,0},{2,3},{3,2},{4,5},{5,4},{6,7},{7,6},{8,9},{9,8},{10,11... | collective-permute-start | bytes 221192 | tf_op jit(solution)/shard_map/ppermute | solution.py:562
  102.0 1.5 %collective-permute-start.41 = (f32[2,72,128]{2,1,0:T(8,128)S(1)}, f32[2,72,128]{2,1,0:T(8,128)S(1)}, u32[]{:S(2)}, u32[]{:S(2)}) collective-permute-start(f32[2,72,128]{2,1,0:T(8,128)S(1)} %bitcast.54), channel_id=1, source_target_pairs={{0,1},{1,0},{2,3},{3,2},{4,5},{5,4},{6,7},{7,6},{8,9},{9,8},{10,11... | collective-permute-start | bytes 221192 | tf_op jit(solution)/shard_map/ppermute | solution.py:562
  102.5 1.3 %collective-permute-start.42 = (f32[2,72,128]{2,1,0:T(8,128)S(1)}, f32[2,72,128]{2,1,0:T(8,128)S(1)}, u32[]{:S(2)}, u32[]{:S(2)}) collective-permute-start(f32[2,72,128]{2,1,0:T(8,128)S(1)} %bitcast.58), channel_id=1, source_target_pairs={{0,1},{1,0},{2,3},{3,2},{4,5},{5,4},{6,7},{7,6},{8,9},{9,8},{10,11... | collective-permute-start | bytes 221192 | tf_op jit(solution)/shard_map/ppermute | solution.py:562
  102.7 1.3 %collective-permute-start.43 = (f32[2,72,128]{2,1,0:T(8,128)S(1)}, f32[2,72,128]{2,1,0:T(8,128)S(1)}, u32[]{:S(2)}, u32[]{:S(2)}) collective-permute-start(f32[2,72,128]{2,1,0:T(8,128)S(1)} %bitcast.60), channel_id=1, source_target_pairs={{0,1},{1,0},{2,3},{3,2},{4,5},{5,4},{6,7},{7,6},{8,9},{9,8},{10,11... | collective-permute-start | bytes 221192 | tf_op jit(solution)/shard_map/ppermute | solution.py:562
  103.0 1.3 %collective-permute-start.44 = (f32[2,72,128]{2,1,0:T(8,128)S(1)}, f32[2,72,128]{2,1,0:T(8,128)S(1)}, u32[]{:S(2)}, u32[]{:S(2)}) collective-permute-start(f32[2,72,128]{2,1,0:T(8,128)S(1)} %bitcast.62), channel_id=1, source_target_pairs={{0,1},{1,0},{2,3},{3,2},{4,5},{5,4},{6,7},{7,6},{8,9},{9,8},{10,11... | collective-permute-start | bytes 221192 | tf_op jit(solution)/shard_map/ppermute | solution.py:562
  103.2 1.3 %collective-permute-start.45 = (f32[2,72,128]{2,1,0:T(8,128)S(1)}, f32[2,72,128]{2,1,0:T(8,128)S(1)}, u32[]{:S(2)}, u32[]{:S(2)}) collective-permute-start(f32[2,72,128]{2,1,0:T(8,128)S(1)} %bitcast.44), channel_id=1, source_target_pairs={{0,1},{1,0},{2,3},{3,2},{4,5},{5,4},{6,7},{7,6},{8,9},{9,8},{10,11... | collective-permute-start | bytes 221192 | tf_op jit(solution)/shard_map/ppermute | solution.py:562
  (27 other events, 406.1 us)

commit v4 on v3

--- a/solution.py
+++ b/solution.py
@@ -70,15 +70,13 @@
 
 def x_tables(groups):
     width = GX // groups
-    place = np.arange(GX).reshape(groups, 1, width)
+    place = np.arange(width).reshape(1, 1, width)
     angle = 2.0 * np.pi * (np.arange(HALF)[None, :, None] * place % GX) / GX
-    table = np.stack([np.cos(angle), -np.sin(angle)], axis=2).reshape(groups, 2 * HALF, width)
-    wide = np.einsum("gkx,cd->gkcxd", table, np.eye(CBLOCK)).reshape(groups, 2 * HALF * CBLOCK, width * CBLOCK)
+    table = np.stack([np.cos(angle), -np.sin(angle)], axis=2).reshape(1, 2 * HALF, width)
+    wide = np.einsum("gkx,cd->gkcxd", table, np.eye(CBLOCK)).reshape(1, 2 * HALF * CBLOCK, width * CBLOCK)
     high, low = split_np(wide)
-    forward = np.concatenate([high, low, high], axis=2)
-    flip = lambda t: np.swapaxes(t, 1, 2)
-    inverse = np.concatenate([flip(high), flip(low), flip(high)], axis=2)
-    return forward, np.ascontiguousarray(inverse)
+    turned = np.swapaxes(np.concatenate([high, low, high], axis=1), 1, 2)
+    return np.concatenate([high, low], axis=2)[0], np.ascontiguousarray(turned[0])
 
 
 def dot(a, b):
@@ -107,12 +105,17 @@
     return pltpu.roll(value, value.shape[-1] // 2, value.ndim - 1)
 
 
-def to_spectra(channels, fields, x_table, own, other, own_out, other_out, u_high, u_low, ready=None):
+def turning(space):
+    return jnp.where(space == 1, -1.0, 1.0).astype(f32)
+
+
+def to_spectra(turn, channels, fields, x_table, own, other, own_out, other_out, u_high, u_low, ready=None):
     for block in range(channels // CBLOCK):
         pieces = fields(block)
         cells = pieces[0].shape[0]
-        stacked = pieces[0] if len(pieces) == 1 else jnp.concatenate(pieces, axis=0)
-        result = dot(x_table[:, : cells * len(pieces)], stacked)
+        result = dot(x_table[...], jnp.concatenate([pieces[0], pieces[0]], axis=0))
+        if len(pieces) > 1:
+            result = result + dot(x_table[:, :cells], pieces[1])
         middle = result.shape[-1] // 2
         lower, upper = result[:, :middle], result[:, middle:]
         high, low = split(jnp.concatenate([lower + upper, lower - upper], axis=1))
@@ -161,8 +164,9 @@
             for step in range(several):
                 kx = first + step
                 lanes = slice(step * width, (step + 1) * width)
-                real = [total[:rows, lanes] for total in totals]
-                imag = [swap(total[rows:, lanes]) for total in totals]
+                parts = [total[:, lanes] * turn if kx % 2 == 1 else total[:, lanes] for total in totals]
+                real = [value[:rows] for value in parts]
+                imag = [swap(value[rows:]) for value in parts]
                 if kx < MX // 2:
                     put(kx, *[r + i * sign for r, i in zip(real, imag)])
                 if kx > 0:
@@ -181,7 +185,7 @@
         target[index] = source[pl.ds((place[1] ^ step) * block, block)]
 
 
-def from_spectra(channels, own_in, other_in, x_table, own, other, u_high, u_low, t_high, t_low):
+def from_spectra(turn, channels, own_in, other_in, back_to_cells, own, other, u_high, u_low, t_high, t_low):
     rows = own.shape[0] // 8
     part = 2 * rows
     count = own_in.shape[1]
@@ -200,6 +204,8 @@
             else:
                 ahead, behind = source[kx], source[MX - kx]
                 real, imag = ahead - behind * sign, ahead * sign + behind
+            if kx % 2 == 1:
+                real, imag = real * turn, imag * turn
             pieces += [real, swap(imag)]
         at = pl.ds(kx * width, width)
         for odd, first in enumerate((0, count - rows)):
@@ -231,12 +237,13 @@
         u_high[pl.ds(2 * first, 2 * several)] = value_high.reshape(shape)
         u_low[pl.ds(2 * first, 2 * several)] = value_low.reshape(shape)
 
+
     def block(index):
         rows = pl.ds(index * CBLOCK, CBLOCK)
         shape = (2 * HALF * CBLOCK, u_high.shape[-1])
         high = u_high[:, rows, :].reshape(shape)
         low = u_low[:, rows, :].reshape(shape)
-        return dot(x_table[...], jnp.concatenate([high, high, low], axis=0))
+        return back_to_cells(high, low)
 
     return block
 
@@ -247,7 +254,7 @@
     blocks, width, _, cells = field.shape
     space = lax.axis_index("space")
     place = (space, lax.axis_index("dp") if len(order) > 1 else 0)
-    copies = [pltpu.make_async_copy(x_in.at[space], x_table, sems.at[0])]
+    copies = [pltpu.make_async_copy(x_in, x_table, sems.at[0])]
     for block in range(blocks):
         piece = field_in.at[0, :, pl.ds(block * CBLOCK, CBLOCK), :]
         copies.append(pltpu.make_async_copy(piece, field.at[block], sems.at[1 + block]))
@@ -260,14 +267,14 @@
     def fields(block):
         copies[1 + block].wait()
         piece = field[block].reshape(width * CBLOCK, cells)
-        return [piece, piece]
+        return [piece]
 
     def ready():
         copies[1 + blocks].wait()
         copies[2 + blocks].wait()
 
     channels = blocks * CBLOCK
-    to_spectra(channels, fields, x_table, own, other, own_out, other_out, u_high, u_low, ready)
+    to_spectra(turning(space), channels, fields, x_table, own, other, own_out, other_out, u_high, u_low, ready)
     scatter(place, order, other_out, other_part)
     scatter(place, order, own_out, own_part)
 
@@ -275,12 +282,18 @@
 def middle_kernel(back_order, order, place, *refs):
     number = len(back_order)
     own_blocks, other_blocks = refs[:number], refs[number : 2 * number]
-    field, cotangent, pointwise, x_inverse, x_forward, own, other, *refs = refs[2 * number :]
+    field, cotangent, pointwise, x_table, own, other, *refs = refs[2 * number :]
     own_part, other_part, slope_high, slope_low, u_high, u_low, t_high, t_low, own_in, other_in, pre = refs
     gather(place, back_order, own_blocks, own_in)
     gather(place, back_order, other_blocks, other_in)
     width, channels, cells = field.shape
-    block = from_spectra(channels, own_in, other_in, x_inverse, own, other, u_high, u_low, t_high, t_low)
+    places = x_table.shape[1] // 2
+    turned = x_table[...].astype(f32).T.astype(bf16)
+
+    def product(high, low):
+        return (dot(turned[:places], high) + dot(turned[places:], high)) + dot(turned[:places], low)
+
+    block = from_spectra(turning(place[0]), channels, own_in, other_in, product, own, other, u_high, u_low, t_high, t_low)
     for index in range(channels // CBLOCK):
         pre[:, pl.ds(index * CBLOCK, CBLOCK), :] = block(index).reshape(width, CBLOCK, cells)
     root = math.sqrt(2.0 / math.pi)
@@ -302,9 +315,9 @@
         rows = pl.ds(index * CBLOCK, CBLOCK)
         shape = (width * CBLOCK, cells)
         high = slope_high[:, rows, :].reshape(shape)
-        return [high, high, slope_low[:, rows, :].reshape(shape)]
-
-    to_spectra(channels, fields, x_forward, own, other, own_in, other_in, u_high, u_low)
+        return [high, slope_low[:, rows, :].reshape(shape)]
+
+    to_spectra(turning(place[0]), channels, fields, x_table, own, other, own_in, other_in, u_high, u_low)
     scatter(place, order, other_in, other_part)
     scatter(place, order, own_in, own_part)
 
@@ -316,7 +329,8 @@
     gather(place, order, own_blocks, own_in)
     gather(place, order, other_blocks, other_in)
     width, channels, cells = out.shape
-    block = from_spectra(channels, own_in, other_in, x_inverse, own, other, u_high, u_low, t_high, t_low)
+    product = lambda high, low: dot(x_inverse[...], jnp.concatenate([high, high, low], axis=0))
+    block = from_spectra(turning(place[0]), channels, own_in, other_in, product, own, other, u_high, u_low, t_high, t_low)
     for index in range(channels // CBLOCK):
         rows = pl.ds(index * CBLOCK, CBLOCK)
         value = block(index).reshape(width, CBLOCK, cells) + local[:, rows, :]
@@ -394,13 +408,6 @@
     def _(index):
         at = pl.ds(index * chunk, chunk)
         high[at], low[at] = split(weight[at])
-
-
-def hold_kernel(field, cotangent, x_inverse, x_forward, table, *targets):
-    space = lax.axis_index("space")
-    values = [field[0], cotangent[0], x_inverse[space], x_forward[space], table[space], table[1 - space]]
-    for target, value in zip(targets, values):
-        target[...] = value
 
 
 def mode_kernel(one_chunk, number, *refs):
@@ -537,9 +544,7 @@
 
     plain_table = jnp.asarray(yz_tables(groups, False))
     scaled_table = jnp.asarray(yz_tables(groups, True))
-    x_forward, x_inverse = x_tables(groups)
-    x_brief = jnp.asarray(x_forward[:, :, : 2 * width * CBLOCK])
-    x_forward, x_inverse = jnp.asarray(x_forward), jnp.asarray(x_inverse)
+    x_table, x_inverse = map(jnp.asarray, x_tables(groups))
 
     def mine(array):
         return pl.BlockSpec((None,) + array.shape[1:], lambda i, s: (s[0], 0, 0))
@@ -572,7 +577,7 @@
         in_specs=[pl.BlockSpec(memory_space=pltpu.HBM)] * 3,
         scratch_shapes=[
             pltpu.VMEM((channels // CBLOCK, width, CBLOCK, cells), bf16),
-            pltpu.VMEM(x_brief.shape[1:], bf16),
+            pltpu.VMEM(x_table.shape, bf16),
             table_scratch,
             table_scratch,
             pltpu.SemaphoreType.DMA((channels // CBLOCK + 3,)),
@@ -581,7 +586,7 @@
         + spectrum_scratch,
         compiler_params=pltpu.CompilerParams(vmem_limit_bytes=62 * 1024 * 1024),
         name="first",
-    )(inputs, x_brief, plain_table)
+    )(inputs, x_table, plain_table)
 
     weight_shape = (modes, channels, lanes)
     weight, own = lax.optimization_barrier((spectral_weight.reshape(weight_shape), own))
@@ -652,14 +657,14 @@
             grid=(1,),
             in_specs=[
                 *block_specs, sample, sample, entire(pointwise_weight.shape),
-                mine(x_inverse), mine(x_forward), mine(scaled_table), others(scaled_table),
+                entire(x_table.shape), mine(scaled_table), others(scaled_table),
             ],
             out_specs=[entire(part_shape)] * 2 + [entire(field_shape)] * 2,
             scratch_shapes=u_scratch + t_scratch + spectrum_scratch + [pltpu.VMEM(field_shape, f32)],
         ),
         compiler_params=params,
         name="middle",
-    )(place, *mixed, inputs, cotangent, pointwise_weight, x_inverse, x_forward, scaled_table, scaled_table)
+    )(place, *mixed, inputs, cotangent, pointwise_weight, x_table, scaled_table, scaled_table)
     again, own = lax.optimization_barrier((weight, own))
     slopes = to_owners(own, sent)
     local, *weights = pl.pallas_call(
@@ -694,7 +699,7 @@
         grid_spec=pltpu.PrefetchScalarGridSpec(
             num_scalar_prefetch=1,
             grid=(1,),
-            in_specs=[*block_specs, entire(field_shape), mine(x_inverse), mine(plain_table), others(plain_table)],
+            in_specs=[*block_specs, entire(field_shape), entire(x_inverse.shape), mine(plain_table), others(plain_table)],
             out_specs=sample,
             scratch_shapes=u_scratch + t_scratch + spectrum_scratch,
         ),

time: 109 us -> 107 us (0.982)
  local copies, waits for them, and re-layouts: 5.13 us -> 3.21 us
    unnamed x58 -> x56, local copies, waits for them, and re-layouts: 5.13 us -> 3.21 us
  transfers between devices with their start and end apart: 46 -> 46, of which waited for: 22 -> 23; matrix products, arithmetic and copies ran while one was open for 0% -> 0% of each run, Pallas kernels for 9% -> 10%
where the time goes in v4:
time: 107 us
  starting transfers between devices  49.8 us (47%)
  Pallas kernels  34 us (32%)
  waiting for transfers between devices  17.8 us (17%)
  local copies, waits for them, and re-layouts  3.21 us (3%)
  other arithmetic  1.35 us (1%)
    ppermute x28, starting transfers between devices, travel(): lax.ppermute(value, 'dp', [(i, i ^ step) for i in range(owners)])  44.8 us
    ppermute x28, waiting for transfers between devices, travel(): lax.ppermute(value, 'dp', [(i, i ^ step) for i in range(owners)])  12.3 us
    pallas_call x1, Pallas kernels, body(): pl.pallas_call(functools.partial(middle_kernel, back_order, order), out_s...  9.36 us
    pallas_call x1, Pallas kernels, body(): pl.pallas_call(functools.partial(adam_kernel, len(owned)), out_shape=[who...  7.64 us
    pallas_call x2, Pallas kernels, mixing(): pl.pallas_call(functools.partial(mode_kernel, chunk, len(values)), out_sh...  5.75 us
    ppermute x18, waiting for transfers between devices, other_core(): return lax.ppermute(value, 'space', [(0, 1), (1, 0)])  5.48 us
    ppermute x18, starting transfers between devices, other_core(): return lax.ppermute(value, 'space', [(0, 1), (1, 0)])  5.01 us
    pallas_call x1, Pallas kernels, body(): pl.pallas_call(functools.partial(first_kernel, order), out_shape=[part_ty...  4.51 us
  transfers between devices with their start and end apart: 46, of which 23 were waited for; matrix products, arithmetic and copies ran while one was open for 0% of the time, Pallas kernels for 10%

profile of v4, /device:TPU:0, one launch (start us, length us, event | category | flops | bytes accessed | tf_op | source)
XLA Modules:
  0.0 107.1 jit_solution(13632075190266059638)
XLA Ops:
  0.6 4.5 %first.1 = (f32[8,2,72,128]{3,2,1,0:T(8,128)}, f32[8,2,72,128]{3,2,1,0:T(8,128)}) custom-call(bf16[1,16,64,512]{3,2,1,0:T(8,128)(2,1)} %refs_16_.1, bf16[288,512]{1,0:T(8,128)(2,1)} %constant.18.clone.x_in.refs_19_, bf16[2,320,256]{2,1,0:T(8,128)(2,1)} %constant.16.clone.table_in.refs_18_.refs_19_), custom_call_target="tpu_custom_call" | custom-call | tf_op jit(solution)/shard_map/first/pallas_call | solution.py:574
  5.1 0.5 collective-permute-start
  5.7 1.8 %collective-permute-done = f32[8,2,72,128]{3,2,1,0:T(8,128)S(1)} collective-permute-done((f32[8,2,72,128]{3,2,1,0:T(8,128)}, f32[8,2,72,128]{3,2,1,0:T(8,128)S(1)}, u32[]{:S(2)}, u32[]{:S(2)}) %collective-permute-start) | collective-permute-done | bytes 589856 | tf_op jit(solution)/shard_map/ppermute | solution.py:567
  7.5 1.2 %slice_add_fusion.8 = (f32[1,2,72,128]{3,2,1,0:T(8,128)S(1)}, f32[1,2,72,128]{3,2,1,0:T(8,128)S(1)}, f32[1,2,72,128]{3,2,1,0:T(8,128)S(1)}, f32[1,2,72,128]{3,2,...) fusion(f32[8,2,72,128]{3,2,1,0:T(8,128)S(1)} %collective-permut, ...), kind=kLoop, calls=%fused_computation.8 | loop fusion | flops 147456 | bytes 1769472 | tf_op jit(solution)/shard_map/add | solution.py:604
  8.7 5.0 %collective-permute-start.6 = (f32[1,144,128]{2,1,0:T(8,128)S(1)}, f32[1,144,128]{2,1,0:T(8,128)S(1)}, u32[]{:S(2)}, u32[]{:S(2)}) collective-permute-start(f32[1,144,128]{2,1,0:T(8,128)S(1)} %bitcast.97), channel_id=1, source_target_pairs={{0,12},{2,14},{4,8},{6,10},{8,4},{10,6},{12,0},{14,2},{1,13},{3,15... | collective-permute-start | bytes 221192 | tf_op jit(solution)/shard_map/ppermute | solution.py:595
  13.7 1.2 %collective-permute-start.7 = (f32[1,144,128]{2,1,0:T(8,128)S(1)}, f32[1,144,128]{2,1,0:T(8,128)S(1)}, u32[]{:S(2)}, u32[]{:S(2)}) collective-permute-start(f32[1,144,128]{2,1,0:T(8,128)S(1)} %bitcast.95), channel_id=1, source_target_pairs={{0,14},{2,12},{4,10},{6,8},{8,6},{10,4},{12,2},{14,0},{1,15},{3,13... | collective-permute-start | bytes 221192 | tf_op jit(solution)/shard_map/ppermute | solution.py:595
  14.9 0.8 collective-permute-start.5
  15.7 2.0 %collective-permute-start.4 = (f32[1,144,128]{2,1,0:T(8,128)S(1)}, f32[1,144,128]{2,1,0:T(8,128)S(1)}, u32[]{:S(2)}, u32[]{:S(2)}) collective-permute-start(f32[1,144,128]{2,1,0:T(8,128)S(1)} %bitcast.93), channel_id=1, source_target_pairs={{0,8},{2,10},{4,12},{6,14},{8,0},{10,2},{12,4},{14,6},{1,9},{3,11}... | collective-permute-start | bytes 221192 | tf_op jit(solution)/shard_map/ppermute | solution.py:595
  17.6 2.3 %collective-permute-start.3 = (f32[1,144,128]{2,1,0:T(8,128)S(1)}, f32[1,144,128]{2,1,0:T(8,128)S(1)}, u32[]{:S(2)}, u32[]{:S(2)}) collective-permute-start(f32[1,144,128]{2,1,0:T(8,128)S(1)} %bitcast.91), channel_id=1, source_target_pairs={{0,6},{2,4},{4,2},{6,0},{8,14},{10,12},{12,10},{14,8},{1,7},{3,5},... | collective-permute-start | bytes 221192 | tf_op jit(solution)/shard_map/ppermute | solution.py:595
  20.0 0.8 collective-permute-start.2
  20.8 0.7 collective-permute-done.7.refs_7_
  21.5 1.7 %collective-permute-start.1 = (f32[1,144,128]{2,1,0:T(8,128)S(1)}, f32[1,144,128]{2,1,0:T(8,128)S(1)}, u32[]{:S(2)}, u32[]{:S(2)}) collective-permute-start(f32[1,144,128]{2,1,0:T(8,128)S(1)} %bitcast.87), channel_id=1, source_target_pairs={{0,2},{2,0},{4,6},{6,4},{8,10},{10,8},{12,14},{14,12},{1,3},{3,1},... | collective-permute-start | bytes 221192 | tf_op jit(solution)/shard_map/ppermute | solution.py:595
  23.2 2.3 %copy-done.22 = f32[1,16,9,64,128]{4,3,2,1,0:T(8,128)S(1)} copy-done((f32[1,16,9,64,128]{4,3,2,1,0:T(8,128)S(1)}, f32[1,16,9,64,128]{4,3,2,1,0:T(8,128)}, u32[]{:S(2)}) %copy-start.22) | copy-done | bytes 4718616
  25.5 0.6 split.1
  27.0 2.5 %mix.1 = (f32[1,144,128]{2,1,0:T(8,128)S(1)}, f32[1,144,128]{2,1,0:T(8,128)}, f32[1,144,128]{2,1,0:T(8,128)}, f32[1,144,128]{2,1,0:T(8,128)S(1)}, f32[1,144,128]...) custom-call(f32[1,144,128]{2,1,0:T(8,128)S(1)} %bitcast.40, ...), custom_call_target="tpu_custom_call" | custom-call | flops 1000000000 | bytes 100000 | tf_op jit(solution)/shard_map/mix/pallas_call | solution.py:624
  29.5 4.4 %collective-permute-start.8 = (f32[1,144,128]{2,1,0:T(8,128)S(1)}, f32[1,144,128]{2,1,0:T(8,128)S(1)}, u32[]{:S(2)}, u32[]{:S(2)}) collective-permute-start(f32[1,144,128]{2,1,0:T(8,128)S(1)} %get-tuple-element.53), channel_id=1, source_target_pairs={{0,8},{2,10},{4,12},{6,14},{8,0},{10,2},{12,4},{14,6},{1,9},{3,11}... | collective-permute-start | bytes 221192 | tf_op jit(solution)/shard_map/ppermute | solution.py:595
  34.2 2.2 %collective-permute-start.10 = (f32[1,144,128]{2,1,0:T(8,128)S(1)}, f32[1,144,128]{2,1,0:T(8,128)S(1)}, u32[]{:S(2)}, u32[]{:S(2)}) collective-permute-start(f32[1,144,128]{2,1,0:T(8,128)S(1)} %get-tuple-element.55), channel_id=1, source_target_pairs={{0,12},{2,14},{4,8},{6,10},{8,4},{10,6},{12,0},{14,2},{1,13},{3,15... | collective-permute-start | bytes 221192 | tf_op jit(solution)/shard_map/ppermute | solution.py:595
  36.4 2.2 %collective-permute-start.11 = (f32[1,144,128]{2,1,0:T(8,128)S(1)}, f32[1,144,128]{2,1,0:T(8,128)S(1)}, u32[]{:S(2)}, u32[]{:S(2)}) collective-permute-start(f32[1,144,128]{2,1,0:T(8,128)S(1)} %get-tuple-element.56), channel_id=1, source_target_pairs={{0,14},{2,12},{4,10},{6,8},{8,6},{10,4},{12,2},{14,0},{1,15},{3,13... | collective-permute-start | bytes 221192 | tf_op jit(solution)/shard_map/ppermute | solution.py:595
  38.7 2.8 %collective-permute-done.8 = f32[1,144,128]{2,1,0:T(8,128)S(1)} collective-permute-done((f32[1,144,128]{2,1,0:T(8,128)S(1)}, f32[1,144,128]{2,1,0:T(8,128)S(1)}, u32[]{:S(2)}, u32[]{:S(2)}) %collective-permute-start.8) | collective-permute-done | bytes 73760 | tf_op jit(solution)/shard_map/ppermute | solution.py:595
  41.5 2.7 %collective-permute-done.9 = f32[1,144,128]{2,1,0:T(8,128)S(1)} collective-permute-done((f32[1,144,128]{2,1,0:T(8,128)S(1)}, f32[1,144,128]{2,1,0:T(8,128)S(1)}, u32[]{:S(2)}, u32[]{:S(2)}) %collective-permute-start.9) | collective-permute-done | bytes 73760 | tf_op jit(solution)/shard_map/ppermute | solution.py:595
  44.1 1.2 %collective-permute-start.14 = (f32[1,144,128]{2,1,0:T(8,128)}, f32[1,144,128]{2,1,0:T(8,128)S(1)}, u32[]{:S(2)}, u32[]{:S(2)}) collective-permute-start(f32[1,144,128]{2,1,0:T(8,128)} %get-tuple-element.59), channel_id=1, source_target_pairs={{0,2},{2,0},{4,6},{6,4},{8,10},{10,8},{12,14},{14,12},{1,3},{3,1},... | collective-permute-start | bytes 221192 | tf_op jit(solution)/shard_map/ppermute | solution.py:595
  45.3 0.5 collective-permute-start.15
  46.0 0.5 collective-permute-start.17
  46.5 2.2 %collective-permute-done.14 = f32[1,144,128]{2,1,0:T(8,128)S(1)} collective-permute-done((f32[1,144,128]{2,1,0:T(8,128)}, f32[1,144,128]{2,1,0:T(8,128)S(1)}, u32[]{:S(2)}, u32[]{:S(2)}) %collective-permute-start.14) | collective-permute-done | bytes 73760 | tf_op jit(solution)/shard_map/ppermute | solution.py:595
  48.7 0.5 collective-permute-start.19
  49.3 0.4 collective-permute-start.21
  50.7 0.7 copy-done.20
  51.4 9.4 %middle.1 = (f32[8,2,72,128]{3,2,1,0:T(8,128)S(1)}, f32[8,2,72,128]{3,2,1,0:T(8,128)S(1)}, bf16[16,64,512]{2,1,0:T(8,128)(2,1)S(1)}, bf16[16,64,512]{2,1,0:T(8,128)(2,1)S(1)}) custom-call(s32[2]{0:T(128)S(1)} %pad_add_fusion.place, f32[2,72,128]{2,1,0:T(8,128)S(1)} %bitcast.53, f32[2,72,128]{2,1,0:T(8,128)S(1)} %bitcast.57, f32[2,72,128]{2,1,0:T(8,128)S(1)} %bitcast.61, ...), custom_call_target="tpu_custom_call" | custom-call | tf_op jit(solution)/shard_map/middle/pallas_call | solution.py:652
  61.2 1.6 %collective-permute-done.23 = f32[8,2,72,128]{3,2,1,0:T(8,128)S(1)} collective-permute-done((f32[8,2,72,128]{3,2,1,0:T(8,128)S(1)}, f32[8,2,72,128]{3,2,1,0:T(8,128)S(1)}, u32[]{:S(2)}, u32[]{:S(2)}) %collective-permute-start.23) | collective-permute-done | bytes 589856 | tf_op jit(solution)/shard_map/ppermute | solution.py:567
  62.9 1.9 %collective-permute-start.29 = (f32[1,144,128]{2,1,0:T(8,128)S(1)}, f32[1,144,128]{2,1,0:T(8,128)S(1)}, u32[]{:S(2)}, u32[]{:S(2)}) collective-permute-start(f32[1,144,128]{2,1,0:T(8,128)S(1)} %bitcast.98), channel_id=1, source_target_pairs={{0,12},{2,14},{4,8},{6,10},{8,4},{10,6},{12,0},{14,2},{1,13},{3,15... | collective-permute-start | bytes 221192 | tf_op jit(solution)/shard_map/ppermute | solution.py:595
  64.8 2.7 %collective-permute-start.30 = (f32[1,144,128]{2,1,0:T(8,128)S(1)}, f32[1,144,128]{2,1,0:T(8,128)S(1)}, u32[]{:S(2)}, u32[]{:S(2)}) collective-permute-start(f32[1,144,128]{2,1,0:T(8,128)S(1)} %bitcast.96), channel_id=1, source_target_pairs={{0,14},{2,12},{4,10},{6,8},{8,6},{10,4},{12,2},{14,0},{1,15},{3,13... | collective-permute-start | bytes 221192 | tf_op jit(solution)/shard_map/ppermute | solution.py:595
  67.4 3.2 %collective-permute-start.27 = (f32[1,144,128]{2,1,0:T(8,128)S(1)}, f32[1,144,128]{2,1,0:T(8,128)S(1)}, u32[]{:S(2)}, u32[]{:S(2)}) collective-permute-start(f32[1,144,128]{2,1,0:T(8,128)S(1)} %bitcast.90), channel_id=1, source_target_pairs={{0,8},{2,10},{4,12},{6,14},{8,0},{10,2},{12,4},{14,6},{1,9},{3,11}... | collective-permute-start | bytes 221192 | tf_op jit(solution)/shard_map/ppermute | solution.py:595
  70.7 2.6 %collective-permute-start.25 = (f32[1,144,128]{2,1,0:T(8,128)S(1)}, f32[1,144,128]{2,1,0:T(8,128)S(1)}, u32[]{:S(2)}, u32[]{:S(2)}) collective-permute-start(f32[1,144,128]{2,1,0:T(8,128)S(1)} %bitcast.86), channel_id=1, source_target_pairs={{0,4},{2,6},{4,0},{6,2},{8,12},{10,14},{12,8},{14,10},{1,5},{3,7},... | collective-permute-start | bytes 221192 | tf_op jit(solution)/shard_map/ppermute | solution.py:595
  73.3 0.8 collective-permute-start.24
  74.2 2.0 %local.1 = (f32[16,64,512]{2,1,0:T(8,128)S(1)}, bf16[144,64,128]{2,1,0:T(8,128)(2,1)S(1)}, bf16[144,64,128]{2,1,0:T(8,128)(2,1)S(1)}) custom-call(bf16[16,64,512]{2,1,0:T(8,128)(2,1)S(1)} %get-tuple-element.64.slope_high, bf16[16,64,512]{2,1,0:T(8,128)(2,1)S(1)} %get-tuple-element.65.slope_low, f32[64,64]{1,0:T(8,128)S(1)} %copy-done.21, ...), custom_call_target="tpu_custom_call" | custom-call | flops 6000000000 | bytes 100000 | tf_op jit(solution)/shard_map/local/pallas_call | solution.py:670
  76.6 1.0 collective-permute-done.27.refs_4_.refs_12_
  77.6 1.2 %collective-permute-done.26.refs_3_.refs_11_ = f32[1,144,128]{2,1,0:T(8,128)S(1)} collective-permute-done((f32[1,144,128]{2,1,0:T(8,128)S(1)}, f32[1,144,128]{2,1,0:T(8,128)S(1)}, u32[]{:S(2)}, u32[]{:S(2)}) %collective-permute-start.26) | collective-permute-done | bytes 73760 | tf_op jit(solution)/shard_map/ppermute | solution.py:595
  78.8 0.6 collective-permute-done.25.refs_2_.refs_10_
  79.4 3.2 %adjoint.1 = (f32[1,144,128]{2,1,0:T(8,128)S(1)}, f32[1,144,128]{2,1,0:T(8,128)S(1)}, f32[1,144,128]{2,1,0:T(8,128)S(1)}, f32[1,144,128]{2,1,0:T(8,128)S(1)}, f3...) custom-call(f32[1,144,128]{2,1,0:T(8,128)S(1)} %bitcast.42, ...), custom_call_target="tpu_custom_call" | custom-call | flops 1000000000 | bytes 100000 | tf_op jit(solution)/shard_map/adjoint/pallas_call | solution.py:624
  82.6 0.8 collective-permute-start.31
  83.5 2.3 %collective-permute-start.33 = (f32[1,144,128]{2,1,0:T(8,128)S(1)}, f32[1,144,128]{2,1,0:T(8,128)S(1)}, u32[]{:S(2)}, u32[]{:S(2)}) collective-permute-start(f32[1,144,128]{2,1,0:T(8,128)S(1)} %get-tuple-element.71), channel_id=1, source_target_pairs={{0,8},{2,10},{4,12},{6,14},{8,0},{10,2},{12,4},{14,6},{1,9},{3,11}... | collective-permute-start | bytes 221192 | tf_op jit(solution)/shard_map/ppermute | solution.py:595
  85.8 1.3 %collective-permute-start.34 = (f32[1,144,128]{2,1,0:T(8,128)S(1)}, f32[1,144,128]{2,1,0:T(8,128)S(1)}, u32[]{:S(2)}, u32[]{:S(2)}) collective-permute-start(f32[1,144,128]{2,1,0:T(8,128)S(1)} %get-tuple-element.72), channel_id=1, source_target_pairs={{0,10},{2,8},{4,14},{6,12},{8,2},{10,0},{12,6},{14,4},{1,11},{3,9}... | collective-permute-start | bytes 221192 | tf_op jit(solution)/shard_map/ppermute | solution.py:595
  87.1 1.5 %collective-permute-start.35 = (f32[1,144,128]{2,1,0:T(8,128)S(1)}, f32[1,144,128]{2,1,0:T(8,128)S(1)}, u32[]{:S(2)}, u32[]{:S(2)}) collective-permute-start(f32[1,144,128]{2,1,0:T(8,128)S(1)} %get-tuple-element.73), channel_id=1, source_target_pairs={{0,12},{2,14},{4,8},{6,10},{8,4},{10,6},{12,0},{14,2},{1,13},{3,15... | collective-permute-start | bytes 221192 | tf_op jit(solution)/shard_map/ppermute | solution.py:595
  88.6 2.5 %collective-permute-start.36 = (f32[1,144,128]{2,1,0:T(8,128)S(1)}, f32[1,144,128]{2,1,0:T(8,128)S(1)}, u32[]{:S(2)}, u32[]{:S(2)}) collective-permute-start(f32[1,144,128]{2,1,0:T(8,128)S(1)} %get-tuple-element.74), channel_id=1, source_target_pairs={{0,14},{2,12},{4,10},{6,8},{8,6},{10,4},{12,2},{14,0},{1,15},{3,13... | collective-permute-start | bytes 221192 | tf_op jit(solution)/shard_map/ppermute | solution.py:595
  91.1 0.9 collective-permute-start.37
  92.2 7.6 %adam.1 = (f32[144,64,128]{2,1,0:T(8,128)}, f32[144,64,128]{2,1,0:T(8,128)}, f32[144,64,128]{2,1,0:T(8,128)}) custom-call(f32[1,144,128]{2,1,0:T(8,128)S(1)} %bitcast.41, f32[1,144,128]{2,1,0:T(8,128)S(1)} %copy-done.19, f32[1,144,128]{2,1,0:T(8,128)S(1)} %copy-done.17, f32[1,144,128]{2,1,0:T(8,128)S(1)} %copy-done.15, f32[1,144,128]{2,1,0:T(8,128)S(1)} %copy-done.13, ...), custom_call_target="tpu_custom_call" | custom-call | flops 10000000000 | bytes 30000000 | tf_op jit(solution)/shard_map/adam/pallas_call | solution.py:683
  99.9 0.5 collective-permute-start.38
  103.0 4.2 %last.1 = bf16[1,16,64,512]{3,2,1,0:T(8,128)(2,1)} custom-call(s32[2]{0:T(128)S(1)} %pad_add_fusion.place, f32[2,72,128]{2,1,0:T(8,128)S(1)} %bitcast.49, f32[2,72,128]{2,1,0:T(8,128)S(1)} %bitcast.51, f32[2,72,128]{2,1,0:T(8,128)S(1)} %bitcast.55, f32[2,72,128]{2,1,0:T(8,128)S(1)} %bitcast.59, f32[2,72,128]{2,1,0:T(8,128)S(1)} %bitcast.63, ...), custom_call_target="tpu_custom_call" | custom-call | tf_op jit(solution)/shard_map/last/pallas_call | solution.py:696
  (113 shorter events, 5.8 us)
Async XLA Ops:
  5.1 2.4 %collective-permute-start = (f32[8,2,72,128]{3,2,1,0:T(8,128)}, f32[8,2,72,128]{3,2,1,0:T(8,128)S(1)}, u32[]{:S(2)}, u32[]{:S(2)}) collective-permute-start(f32[8,2,72,128]{3,2,1,0:T(8,128)} %get-tuple-element.50), channel_id=1, source_target_pairs={{0,1},{1,0},{2,3},{3,2},{4,5},{5,4},{6,7},{7,6},{8,9},{9,8},{10,11... | collective-permute-start | bytes 1769480 | tf_op jit(solution)/shard_map/ppermute | solution.py:567
  8.7 11.2 %collective-permute-start.6 = (f32[1,144,128]{2,1,0:T(8,128)S(1)}, f32[1,144,128]{2,1,0:T(8,128)S(1)}, u32[]{:S(2)}, u32[]{:S(2)}) collective-permute-start(f32[1,144,128]{2,1,0:T(8,128)S(1)} %bitcast.97), channel_id=1, source_target_pairs={{0,12},{2,14},{4,8},{6,10},{8,4},{10,6},{12,0},{14,2},{1,13},{3,15... | collective-permute-start | bytes 221192 | tf_op jit(solution)/shard_map/ppermute | solution.py:595
  13.7 7.7 %collective-permute-start.7 = (f32[1,144,128]{2,1,0:T(8,128)S(1)}, f32[1,144,128]{2,1,0:T(8,128)S(1)}, u32[]{:S(2)}, u32[]{:S(2)}) collective-permute-start(f32[1,144,128]{2,1,0:T(8,128)S(1)} %bitcast.95), channel_id=1, source_target_pairs={{0,14},{2,12},{4,10},{6,8},{8,6},{10,4},{12,2},{14,0},{1,15},{3,13... | collective-permute-start | bytes 221192 | tf_op jit(solution)/shard_map/ppermute | solution.py:595
  14.9 11.6 %collective-permute-start.5 = (f32[1,144,128]{2,1,0:T(8,128)S(1)}, f32[1,144,128]{2,1,0:T(8,128)S(1)}, u32[]{:S(2)}, u32[]{:S(2)}) collective-permute-start(f32[1,144,128]{2,1,0:T(8,128)S(1)} %bitcast.94), channel_id=1, source_target_pairs={{0,10},{2,8},{4,14},{6,12},{8,2},{10,0},{12,6},{14,4},{1,11},{3,9}... | collective-permute-start | bytes 221192 | tf_op jit(solution)/shard_map/ppermute | solution.py:595
  15.7 11.0 %collective-permute-start.4 = (f32[1,144,128]{2,1,0:T(8,128)S(1)}, f32[1,144,128]{2,1,0:T(8,128)S(1)}, u32[]{:S(2)}, u32[]{:S(2)}) collective-permute-start(f32[1,144,128]{2,1,0:T(8,128)S(1)} %bitcast.93), channel_id=1, source_target_pairs={{0,8},{2,10},{4,12},{6,14},{8,0},{10,2},{12,4},{14,6},{1,9},{3,11}... | collective-permute-start | bytes 221192 | tf_op jit(solution)/shard_map/ppermute | solution.py:595
  17.6 9.0 %collective-permute-start.3 = (f32[1,144,128]{2,1,0:T(8,128)S(1)}, f32[1,144,128]{2,1,0:T(8,128)S(1)}, u32[]{:S(2)}, u32[]{:S(2)}) collective-permute-start(f32[1,144,128]{2,1,0:T(8,128)S(1)} %bitcast.91), channel_id=1, source_target_pairs={{0,6},{2,4},{4,2},{6,0},{8,14},{10,12},{12,10},{14,8},{1,7},{3,5},... | collective-permute-start | bytes 221192 | tf_op jit(solution)/shard_map/ppermute | solution.py:595
  20.0 7.0 %collective-permute-start.2 = (f32[1,144,128]{2,1,0:T(8,128)S(1)}, f32[1,144,128]{2,1,0:T(8,128)S(1)}, u32[]{:S(2)}, u32[]{:S(2)}) collective-permute-start(f32[1,144,128]{2,1,0:T(8,128)S(1)} %bitcast.89), channel_id=1, source_target_pairs={{0,4},{2,6},{4,0},{6,2},{8,12},{10,14},{12,8},{14,10},{1,5},{3,7},... | collective-permute-start | bytes 221192 | tf_op jit(solution)/shard_map/ppermute | solution.py:595
  21.5 5.5 %collective-permute-start.1 = (f32[1,144,128]{2,1,0:T(8,128)S(1)}, f32[1,144,128]{2,1,0:T(8,128)S(1)}, u32[]{:S(2)}, u32[]{:S(2)}) collective-permute-start(f32[1,144,128]{2,1,0:T(8,128)S(1)} %bitcast.87), channel_id=1, source_target_pairs={{0,2},{2,0},{4,6},{6,4},{8,10},{10,8},{12,14},{14,12},{1,3},{3,1},... | collective-permute-start | bytes 221192 | tf_op jit(solution)/shard_map/ppermute | solution.py:595
  26.2 24.5 %copy-start = (bf16[1,16,64,512]{3,2,1,0:T(8,128)(2,1)S(1)}, bf16[1,16,64,512]{3,2,1,0:T(8,128)(2,1)}, u32[]{:S(2)}) copy-start(bf16[1,16,64,512]{3,2,1,0:T(8,128)(2,1)} %refs_16_.1) | copy-start | bytes 3145732
  26.2 24.5 %copy-start.2 = (bf16[2,320,256]{2,1,0:T(8,128)(2,1)S(1)}, bf16[2,320,256]{2,1,0:T(8,128)(2,1)}, u32[]{:S(2)}) copy-start(bf16[2,320,256]{2,1,0:T(8,128)(2,1)} %constant.17.clone.refs_20_.refs_21_) | copy-start | bytes 983044
  29.5 12.0 %collective-permute-start.8 = (f32[1,144,128]{2,1,0:T(8,128)S(1)}, f32[1,144,128]{2,1,0:T(8,128)S(1)}, u32[]{:S(2)}, u32[]{:S(2)}) collective-permute-start(f32[1,144,128]{2,1,0:T(8,128)S(1)} %get-tuple-element.53), channel_id=1, source_target_pairs={{0,8},{2,10},{4,12},{6,14},{8,0},{10,2},{12,4},{14,6},{1,9},{3,11}... | collective-permute-start | bytes 221192 | tf_op jit(solution)/shard_map/ppermute | solution.py:595
  33.9 10.2 %collective-permute-start.9 = (f32[1,144,128]{2,1,0:T(8,128)S(1)}, f32[1,144,128]{2,1,0:T(8,128)S(1)}, u32[]{:S(2)}, u32[]{:S(2)}) collective-permute-start(f32[1,144,128]{2,1,0:T(8,128)S(1)} %get-tuple-element.54), channel_id=1, source_target_pairs={{0,10},{2,8},{4,14},{6,12},{8,2},{10,0},{12,6},{14,4},{1,11},{3,9}... | collective-permute-start | bytes 221192 | tf_op jit(solution)/shard_map/ppermute | solution.py:595
  34.2 11.1 %collective-permute-start.10 = (f32[1,144,128]{2,1,0:T(8,128)S(1)}, f32[1,144,128]{2,1,0:T(8,128)S(1)}, u32[]{:S(2)}, u32[]{:S(2)}) collective-permute-start(f32[1,144,128]{2,1,0:T(8,128)S(1)} %get-tuple-element.55), channel_id=1, source_target_pairs={{0,12},{2,14},{4,8},{6,10},{8,4},{10,6},{12,0},{14,2},{1,13},{3,15... | collective-permute-start | bytes 221192 | tf_op jit(solution)/shard_map/ppermute | solution.py:595
  36.4 8.9 %collective-permute-start.11 = (f32[1,144,128]{2,1,0:T(8,128)S(1)}, f32[1,144,128]{2,1,0:T(8,128)S(1)}, u32[]{:S(2)}, u32[]{:S(2)}) collective-permute-start(f32[1,144,128]{2,1,0:T(8,128)S(1)} %get-tuple-element.56), channel_id=1, source_target_pairs={{0,14},{2,12},{4,10},{6,8},{8,6},{10,4},{12,2},{14,0},{1,15},{3,13... | collective-permute-start | bytes 221192 | tf_op jit(solution)/shard_map/ppermute | solution.py:595
  38.7 7.2 %collective-permute-start.12 = (f32[1,144,128]{2,1,0:T(8,128)S(1)}, f32[1,144,128]{2,1,0:T(8,128)S(1)}, u32[]{:S(2)}, u32[]{:S(2)}) collective-permute-start(f32[1,144,128]{2,1,0:T(8,128)S(1)} %get-tuple-element.57), channel_id=1, source_target_pairs={{0,6},{2,4},{4,2},{6,0},{8,14},{10,12},{12,10},{14,8},{1,7},{3,5},... | collective-permute-start | bytes 221192 | tf_op jit(solution)/shard_map/ppermute | solution.py:595
  41.5 4.6 %collective-permute-start.13 = (f32[1,144,128]{2,1,0:T(8,128)}, f32[1,144,128]{2,1,0:T(8,128)S(1)}, u32[]{:S(2)}, u32[]{:S(2)}) collective-permute-start(f32[1,144,128]{2,1,0:T(8,128)} %get-tuple-element.58), channel_id=1, source_target_pairs={{0,4},{2,6},{4,0},{6,2},{8,12},{10,14},{12,8},{14,10},{1,5},{3,7},... | collective-permute-start | bytes 221192 | tf_op jit(solution)/shard_map/ppermute | solution.py:595
  44.1 4.6 %collective-permute-start.14 = (f32[1,144,128]{2,1,0:T(8,128)}, f32[1,144,128]{2,1,0:T(8,128)S(1)}, u32[]{:S(2)}, u32[]{:S(2)}) collective-permute-start(f32[1,144,128]{2,1,0:T(8,128)} %get-tuple-element.59), channel_id=1, source_target_pairs={{0,2},{2,0},{4,6},{6,4},{8,10},{10,8},{12,14},{14,12},{1,3},{3,1},... | collective-permute-start | bytes 221192 | tf_op jit(solution)/shard_map/ppermute | solution.py:595
  45.3 3.4 %collective-permute-start.22 = (f32[2,72,128]{2,1,0:T(8,128)S(1)}, f32[2,72,128]{2,1,0:T(8,128)S(1)}, u32[]{:S(2)}, u32[]{:S(2)}) collective-permute-start(f32[2,72,128]{2,1,0:T(8,128)S(1)} %bitcast.46), channel_id=1, source_target_pairs={{0,1},{1,0},{2,3},{3,2},{4,5},{5,4},{6,7},{7,6},{8,9},{9,8},{10,11... | collective-permute-start | bytes 221192 | tf_op jit(solution)/shard_map/ppermute | solution.py:567
  45.3 3.9 %collective-permute-start.15 = (f32[2,72,128]{2,1,0:T(8,128)S(1)}, f32[2,72,128]{2,1,0:T(8,128)S(1)}, u32[]{:S(2)}, u32[]{:S(2)}) collective-permute-start(f32[2,72,128]{2,1,0:T(8,128)S(1)} %bitcast.52), channel_id=1, source_target_pairs={{0,1},{1,0},{2,3},{3,2},{4,5},{5,4},{6,7},{7,6},{8,9},{9,8},{10,11... | collective-permute-start | bytes 221192 | tf_op jit(solution)/shard_map/ppermute | solution.py:567
  45.8 3.4 %collective-permute-start.16 = (f32[2,72,128]{2,1,0:T(8,128)S(1)}, f32[2,72,128]{2,1,0:T(8,128)}, u32[]{:S(2)}, u32[]{:S(2)}) collective-permute-start(f32[2,72,128]{2,1,0:T(8,128)S(1)} %bitcast.56), channel_id=1, source_target_pairs={{0,1},{1,0},{2,3},{3,2},{4,5},{5,4},{6,7},{7,6},{8,9},{9,8},{10,11... | collective-permute-start | bytes 221192 | tf_op jit(solution)/shard_map/ppermute | solution.py:567
  46.0 3.8 %collective-permute-start.17 = (f32[2,72,128]{2,1,0:T(8,128)S(1)}, f32[2,72,128]{2,1,0:T(8,128)S(1)}, u32[]{:S(2)}, u32[]{:S(2)}) collective-permute-start(f32[2,72,128]{2,1,0:T(8,128)S(1)} %bitcast.60), channel_id=1, source_target_pairs={{0,1},{1,0},{2,3},{3,2},{4,5},{5,4},{6,7},{7,6},{8,9},{9,8},{10,11... | collective-permute-start | bytes 221192 | tf_op jit(solution)/shard_map/ppermute | solution.py:567
  48.7 1.3 %collective-permute-start.18 = (f32[2,72,128]{2,1,0:T(8,128)S(1)}, f32[2,72,128]{2,1,0:T(8,128)S(1)}, u32[]{:S(2)}, u32[]{:S(2)}) collective-permute-start(f32[2,72,128]{2,1,0:T(8,128)S(1)} %bitcast.64), channel_id=1, source_target_pairs={{0,1},{1,0},{2,3},{3,2},{4,5},{5,4},{6,7},{7,6},{8,9},{9,8},{10,11... | collective-permute-start | bytes 221192 | tf_op jit(solution)/shard_map/ppermute | solution.py:567
  48.7 1.4 %collective-permute-start.19 = (f32[2,72,128]{2,1,0:T(8,128)S(1)}, f32[2,72,128]{2,1,0:T(8,128)S(1)}, u32[]{:S(2)}, u32[]{:S(2)}) collective-permute-start(f32[2,72,128]{2,1,0:T(8,128)S(1)} %bitcast.66), channel_id=1, source_target_pairs={{0,1},{1,0},{2,3},{3,2},{4,5},{5,4},{6,7},{7,6},{8,9},{9,8},{10,11... | collective-permute-start | bytes 221192 | tf_op jit(solution)/shard_map/ppermute | solution.py:567
  49.2 1.3 %collective-permute-start.20 = (f32[2,72,128]{2,1,0:T(8,128)S(1)}, f32[2,72,128]{2,1,0:T(8,128)S(1)}, u32[]{:S(2)}, u32[]{:S(2)}) collective-permute-start(f32[2,72,128]{2,1,0:T(8,128)S(1)} %bitcast.70), channel_id=1, source_target_pairs={{0,1},{1,0},{2,3},{3,2},{4,5},{5,4},{6,7},{7,6},{8,9},{9,8},{10,11... | collective-permute-start | bytes 221192 | tf_op jit(solution)/shard_map/ppermute | solution.py:567
  49.3 1.4 %collective-permute-start.21 = (f32[2,72,128]{2,1,0:T(8,128)S(1)}, f32[2,72,128]{2,1,0:T(8,128)S(1)}, u32[]{:S(2)}, u32[]{:S(2)}) collective-permute-start(f32[2,72,128]{2,1,0:T(8,128)S(1)} %bitcast.74), channel_id=1, source_target_pairs={{0,1},{1,0},{2,3},{3,2},{4,5},{5,4},{6,7},{7,6},{8,9},{9,8},{10,11... | collective-permute-start | bytes 221192 | tf_op jit(solution)/shard_map/ppermute | solution.py:567
  60.8 2.1 %collective-permute-start.23 = (f32[8,2,72,128]{3,2,1,0:T(8,128)S(1)}, f32[8,2,72,128]{3,2,1,0:T(8,128)S(1)}, u32[]{:S(2)}, u32[]{:S(2)}) collective-permute-start(f32[8,2,72,128]{3,2,1,0:T(8,128)S(1)} %get-tuple-element.63), channel_id=1, source_target_pairs={{0,1},{1,0},{2,3},{3,2},{4,5},{5,4},{6,7},{7,6},{8,9},{9,8},{10,11... | collective-permute-start | bytes 1769480 | tf_op jit(solution)/shard_map/ppermute | solution.py:567
  62.9 7.7 %collective-permute-start.29 = (f32[1,144,128]{2,1,0:T(8,128)S(1)}, f32[1,144,128]{2,1,0:T(8,128)S(1)}, u32[]{:S(2)}, u32[]{:S(2)}) collective-permute-start(f32[1,144,128]{2,1,0:T(8,128)S(1)} %bitcast.98), channel_id=1, source_target_pairs={{0,12},{2,14},{4,8},{6,10},{8,4},{10,6},{12,0},{14,2},{1,13},{3,15... | collective-permute-start | bytes 221192 | tf_op jit(solution)/shard_map/ppermute | solution.py:595
  64.8 8.5 %collective-permute-start.30 = (f32[1,144,128]{2,1,0:T(8,128)S(1)}, f32[1,144,128]{2,1,0:T(8,128)S(1)}, u32[]{:S(2)}, u32[]{:S(2)}) collective-permute-start(f32[1,144,128]{2,1,0:T(8,128)S(1)} %bitcast.96), channel_id=1, source_target_pairs={{0,14},{2,12},{4,10},{6,8},{8,6},{10,4},{12,2},{14,0},{1,15},{3,13... | collective-permute-start | bytes 221192 | tf_op jit(solution)/shard_map/ppermute | solution.py:595
  67.4 9.1 %collective-permute-start.28 = (f32[1,144,128]{2,1,0:T(8,128)S(1)}, f32[1,144,128]{2,1,0:T(8,128)S(1)}, u32[]{:S(2)}, u32[]{:S(2)}) collective-permute-start(f32[1,144,128]{2,1,0:T(8,128)S(1)} %bitcast.92), channel_id=1, source_target_pairs={{0,10},{2,8},{4,14},{6,12},{8,2},{10,0},{12,6},{14,4},{1,11},{3,9}... | collective-permute-start | bytes 221192 | tf_op jit(solution)/shard_map/ppermute | solution.py:595
  67.4 10.1 %collective-permute-start.27 = (f32[1,144,128]{2,1,0:T(8,128)S(1)}, f32[1,144,128]{2,1,0:T(8,128)S(1)}, u32[]{:S(2)}, u32[]{:S(2)}) collective-permute-start(f32[1,144,128]{2,1,0:T(8,128)S(1)} %bitcast.90), channel_id=1, source_target_pairs={{0,8},{2,10},{4,12},{6,14},{8,0},{10,2},{12,4},{14,6},{1,9},{3,11}... | collective-permute-start | bytes 221192 | tf_op jit(solution)/shard_map/ppermute | solution.py:595
  70.6 8.2 %collective-permute-start.26 = (f32[1,144,128]{2,1,0:T(8,128)S(1)}, f32[1,144,128]{2,1,0:T(8,128)S(1)}, u32[]{:S(2)}, u32[]{:S(2)}) collective-permute-start(f32[1,144,128]{2,1,0:T(8,128)S(1)} %bitcast.88), channel_id=1, source_target_pairs={{0,6},{2,4},{4,2},{6,0},{8,14},{10,12},{12,10},{14,8},{1,7},{3,5},... | collective-permute-start | bytes 221192 | tf_op jit(solution)/shard_map/ppermute | solution.py:595
  70.7 8.7 %collective-permute-start.25 = (f32[1,144,128]{2,1,0:T(8,128)S(1)}, f32[1,144,128]{2,1,0:T(8,128)S(1)}, u32[]{:S(2)}, u32[]{:S(2)}) collective-permute-start(f32[1,144,128]{2,1,0:T(8,128)S(1)} %bitcast.86), channel_id=1, source_target_pairs={{0,4},{2,6},{4,0},{6,2},{8,12},{10,14},{12,8},{14,10},{1,5},{3,7},... | collective-permute-start | bytes 221192 | tf_op jit(solution)/shard_map/ppermute | solution.py:595
  73.3 6.1 %collective-permute-start.24 = (f32[1,144,128]{2,1,0:T(8,128)S(1)}, f32[1,144,128]{2,1,0:T(8,128)S(1)}, u32[]{:S(2)}, u32[]{:S(2)}) collective-permute-start(f32[1,144,128]{2,1,0:T(8,128)S(1)} %bitcast.85), channel_id=1, source_target_pairs={{0,2},{2,0},{4,6},{6,4},{8,10},{10,8},{12,14},{14,12},{1,3},{3,1},... | collective-permute-start | bytes 221192 | tf_op jit(solution)/shard_map/ppermute | solution.py:595
  82.6 6.0 %collective-permute-start.31 = (f32[1,144,128]{2,1,0:T(8,128)S(1)}, f32[1,144,128]{2,1,0:T(8,128)S(1)}, u32[]{:S(2)}, u32[]{:S(2)}) collective-permute-start(f32[1,144,128]{2,1,0:T(8,128)S(1)} %get-tuple-element.69), channel_id=1, source_target_pairs={{0,2},{2,0},{4,6},{6,4},{8,10},{10,8},{12,14},{14,12},{1,3},{3,1},... | collective-permute-start | bytes 221192 | tf_op jit(solution)/shard_map/ppermute | solution.py:595
  83.5 7.7 %collective-permute-start.32 = (f32[1,144,128]{2,1,0:T(8,128)S(1)}, f32[1,144,128]{2,1,0:T(8,128)S(1)}, u32[]{:S(2)}, u32[]{:S(2)}) collective-permute-start(f32[1,144,128]{2,1,0:T(8,128)S(1)} %get-tuple-element.70), channel_id=1, source_target_pairs={{0,4},{2,6},{4,0},{6,2},{8,12},{10,14},{12,8},{14,10},{1,5},{3,7},... | collective-permute-start | bytes 221192 | tf_op jit(solution)/shard_map/ppermute | solution.py:595
  83.5 16.4 %collective-permute-start.33 = (f32[1,144,128]{2,1,0:T(8,128)S(1)}, f32[1,144,128]{2,1,0:T(8,128)S(1)}, u32[]{:S(2)}, u32[]{:S(2)}) collective-permute-start(f32[1,144,128]{2,1,0:T(8,128)S(1)} %get-tuple-element.71), channel_id=1, source_target_pairs={{0,8},{2,10},{4,12},{6,14},{8,0},{10,2},{12,4},{14,6},{1,9},{3,11}... | collective-permute-start | bytes 221192 | tf_op jit(solution)/shard_map/ppermute | solution.py:595
  85.8 14.0 %collective-permute-start.34 = (f32[1,144,128]{2,1,0:T(8,128)S(1)}, f32[1,144,128]{2,1,0:T(8,128)S(1)}, u32[]{:S(2)}, u32[]{:S(2)}) collective-permute-start(f32[1,144,128]{2,1,0:T(8,128)S(1)} %get-tuple-element.72), channel_id=1, source_target_pairs={{0,10},{2,8},{4,14},{6,12},{8,2},{10,0},{12,6},{14,4},{1,11},{3,9}... | collective-permute-start | bytes 221192 | tf_op jit(solution)/shard_map/ppermute | solution.py:595
  87.1 12.7 %collective-permute-start.35 = (f32[1,144,128]{2,1,0:T(8,128)S(1)}, f32[1,144,128]{2,1,0:T(8,128)S(1)}, u32[]{:S(2)}, u32[]{:S(2)}) collective-permute-start(f32[1,144,128]{2,1,0:T(8,128)S(1)} %get-tuple-element.73), channel_id=1, source_target_pairs={{0,12},{2,14},{4,8},{6,10},{8,4},{10,6},{12,0},{14,2},{1,13},{3,15... | collective-permute-start | bytes 221192 | tf_op jit(solution)/shard_map/ppermute | solution.py:595
  88.6 11.2 %collective-permute-start.36 = (f32[1,144,128]{2,1,0:T(8,128)S(1)}, f32[1,144,128]{2,1,0:T(8,128)S(1)}, u32[]{:S(2)}, u32[]{:S(2)}) collective-permute-start(f32[1,144,128]{2,1,0:T(8,128)S(1)} %get-tuple-element.74), channel_id=1, source_target_pairs={{0,14},{2,12},{4,10},{6,8},{8,6},{10,4},{12,2},{14,0},{1,15},{3,13... | collective-permute-start | bytes 221192 | tf_op jit(solution)/shard_map/ppermute | solution.py:595
  91.1 8.7 %collective-permute-start.37 = (f32[1,144,128]{2,1,0:T(8,128)S(1)}, f32[1,144,128]{2,1,0:T(8,128)S(1)}, u32[]{:S(2)}, u32[]{:S(2)}) collective-permute-start(f32[1,144,128]{2,1,0:T(8,128)S(1)} %get-tuple-element.75), channel_id=1, source_target_pairs={{0,6},{2,4},{4,2},{6,0},{8,14},{10,12},{12,10},{14,8},{1,7},{3,5},... | collective-permute-start | bytes 221192 | tf_op jit(solution)/shard_map/ppermute | solution.py:595
  99.9 1.3 %collective-permute-start.39 = (f32[2,72,128]{2,1,0:T(8,128)S(1)}, f32[2,72,128]{2,1,0:T(8,128)S(1)}, u32[]{:S(2)}, u32[]{:S(2)}) collective-permute-start(f32[2,72,128]{2,1,0:T(8,128)S(1)} %bitcast.50), channel_id=1, source_target_pairs={{0,1},{1,0},{2,3},{3,2},{4,5},{5,4},{6,7},{7,6},{8,9},{9,8},{10,11... | collective-permute-start | bytes 221192 | tf_op jit(solution)/shard_map/ppermute | solution.py:567
  99.9 1.5 %collective-permute-start.38 = (f32[2,72,128]{2,1,0:T(8,128)S(1)}, f32[2,72,128]{2,1,0:T(8,128)S(1)}, u32[]{:S(2)}, u32[]{:S(2)}) collective-permute-start(f32[2,72,128]{2,1,0:T(8,128)S(1)} %bitcast.48), channel_id=1, source_target_pairs={{0,1},{1,0},{2,3},{3,2},{4,5},{5,4},{6,7},{7,6},{8,9},{9,8},{10,11... | collective-permute-start | bytes 221192 | tf_op jit(solution)/shard_map/ppermute | solution.py:567
  100.4 1.3 %collective-permute-start.40 = (f32[2,72,128]{2,1,0:T(8,128)S(1)}, f32[2,72,128]{2,1,0:T(8,128)S(1)}, u32[]{:S(2)}, u32[]{:S(2)}) collective-permute-start(f32[2,72,128]{2,1,0:T(8,128)S(1)} %bitcast.54), channel_id=1, source_target_pairs={{0,1},{1,0},{2,3},{3,2},{4,5},{5,4},{6,7},{7,6},{8,9},{9,8},{10,11... | collective-permute-start | bytes 221192 | tf_op jit(solution)/shard_map/ppermute | solution.py:567
  100.5 1.5 %collective-permute-start.41 = (f32[2,72,128]{2,1,0:T(8,128)S(1)}, f32[2,72,128]{2,1,0:T(8,128)S(1)}, u32[]{:S(2)}, u32[]{:S(2)}) collective-permute-start(f32[2,72,128]{2,1,0:T(8,128)S(1)} %bitcast.58), channel_id=1, source_target_pairs={{0,1},{1,0},{2,3},{3,2},{4,5},{5,4},{6,7},{7,6},{8,9},{9,8},{10,11... | collective-permute-start | bytes 221192 | tf_op jit(solution)/shard_map/ppermute | solution.py:567
  101.0 1.3 %collective-permute-start.42 = (f32[2,72,128]{2,1,0:T(8,128)S(1)}, f32[2,72,128]{2,1,0:T(8,128)S(1)}, u32[]{:S(2)}, u32[]{:S(2)}) collective-permute-start(f32[2,72,128]{2,1,0:T(8,128)S(1)} %bitcast.62), channel_id=1, source_target_pairs={{0,1},{1,0},{2,3},{3,2},{4,5},{5,4},{6,7},{7,6},{8,9},{9,8},{10,11... | collective-permute-start | bytes 221192 | tf_op jit(solution)/shard_map/ppermute | solution.py:567
  101.2 1.3 %collective-permute-start.43 = (f32[2,72,128]{2,1,0:T(8,128)S(1)}, f32[2,72,128]{2,1,0:T(8,128)S(1)}, u32[]{:S(2)}, u32[]{:S(2)}) collective-permute-start(f32[2,72,128]{2,1,0:T(8,128)S(1)} %bitcast.68), channel_id=1, source_target_pairs={{0,1},{1,0},{2,3},{3,2},{4,5},{5,4},{6,7},{7,6},{8,9},{9,8},{10,11... | collective-permute-start | bytes 221192 | tf_op jit(solution)/shard_map/ppermute | solution.py:567
  101.5 1.3 %collective-permute-start.44 = (f32[2,72,128]{2,1,0:T(8,128)S(1)}, f32[2,72,128]{2,1,0:T(8,128)S(1)}, u32[]{:S(2)}, u32[]{:S(2)}) collective-permute-start(f32[2,72,128]{2,1,0:T(8,128)S(1)} %bitcast.72), channel_id=1, source_target_pairs={{0,1},{1,0},{2,3},{3,2},{4,5},{5,4},{6,7},{7,6},{8,9},{9,8},{10,11... | collective-permute-start | bytes 221192 | tf_op jit(solution)/shard_map/ppermute | solution.py:567
  101.7 1.3 %collective-permute-start.45 = (f32[2,72,128]{2,1,0:T(8,128)S(1)}, f32[2,72,128]{2,1,0:T(8,128)S(1)}, u32[]{:S(2)}, u32[]{:S(2)}) collective-permute-start(f32[2,72,128]{2,1,0:T(8,128)S(1)} %bitcast.44), channel_id=1, source_target_pairs={{0,1},{1,0},{2,3},{3,2},{4,5},{5,4},{6,7},{7,6},{8,9},{9,8},{10,11... | collective-permute-start | bytes 221192 | tf_op jit(solution)/shard_map/ppermute | solution.py:567
  (26 other events, 410.5 us)

commit v5 on v4

--- a/solution.py
+++ b/solution.py
@@ -19,8 +19,8 @@
 HALF = MX // 2 + 1
 CBLOCK = 16
 ORDER = (0, 1, 2, 3, 4, 5, 6, 7)
-BACK_ORDER = (4, 5, 6, 7, 3, 2, 1, 0)
-LAST_ORDER = (1, 2, 4, 5, 6, 7, 3, 0)
+BACK_ORDER = (6, 7, 5, 4, 3, 2, 1, 0)
+LAST_ORDER = (1, 2, 6, 7, 5, 4, 3, 0)
 
 beta_first = 0.9
 beta_second = 0.999

time: 107 us -> 109 us (1.019)
  starting transfers between devices: 49.8 us -> 56.2 us
  waiting for transfers between devices: 17.8 us -> 12.5 us
    ppermute x28, starting transfers between devices: 44.8 us -> 51.5 us  [travel(): lax.ppermute(value, 'dp', [(i, i ^ step) for i in range(owners)])]
    ppermute x28, waiting for transfers between devices: 12.3 us -> 6.58 us  [travel(): lax.ppermute(value, 'dp', [(i, i ^ step) for i in range(owners)])]
  transfers between devices with their start and end apart: 46 -> 46, of which waited for: 23 -> 21; matrix products, arithmetic and copies ran while one was open for 0% -> 0% of each run, Pallas kernels for 10% -> 9%
where the time goes in v5:
time: 109 us; the launch traced here: 108 us
  starting transfers between devices  56.2 us (52%)
  Pallas kernels  34 us (31%)
  waiting for transfers between devices  12.5 us (11%)
  local copies, waits for them, and re-layouts  3.21 us (3%)
  other arithmetic  1.35 us (1%)
    ppermute x28, starting transfers between devices, travel(): lax.ppermute(value, 'dp', [(i, i ^ step) for i in range(owners)])  51.5 us
    pallas_call x1, Pallas kernels, body(): pl.pallas_call(functools.partial(middle_kernel, back_order, order), out_s...  9.36 us
    pallas_call x1, Pallas kernels, body(): pl.pallas_call(functools.partial(adam_kernel, len(owned)), out_shape=[who...  7.64 us
    ppermute x28, waiting for transfers between devices, travel(): lax.ppermute(value, 'dp', [(i, i ^ step) for i in range(owners)])  6.58 us
    ppermute x18, waiting for transfers between devices, other_core(): return lax.ppermute(value, 'space', [(0, 1), (1, 0)])  5.93 us
    pallas_call x2, Pallas kernels, mixing(): pl.pallas_call(functools.partial(mode_kernel, chunk, len(values)), out_sh...  5.75 us
    ppermute x18, starting transfers between devices, other_core(): return lax.ppermute(value, 'space', [(0, 1), (1, 0)])  4.72 us
    pallas_call x1, Pallas kernels, body(): pl.pallas_call(functools.partial(first_kernel, order), out_shape=[part_ty...  4.51 us
  transfers between devices with their start and end apart: 46, of which 21 were waited for; matrix products, arithmetic and copies ran while one was open for 0% of the time, Pallas kernels for 9%

profile of v5, /device:TPU:0, one launch (start us, length us, event | category | flops | bytes accessed | tf_op | source)
XLA Modules:
  0.0 108.3 jit_solution(10294290417847776825)
XLA Ops:
  0.6 4.5 %first.1 = (f32[8,2,72,128]{3,2,1,0:T(8,128)}, f32[8,2,72,128]{3,2,1,0:T(8,128)}) custom-call(bf16[1,16,64,512]{3,2,1,0:T(8,128)(2,1)} %refs_16_.1, bf16[288,512]{1,0:T(8,128)(2,1)} %constant.18.clone.x_in.refs_19_, bf16[2,320,256]{2,1,0:T(8,128)(2,1)} %constant.16.clone.table_in.refs_18_.refs_19_), custom_call_target="tpu_custom_call" | custom-call | tf_op jit(solution)/shard_map/first/pallas_call | solution.py:574
  5.1 0.5 collective-permute-start
  5.7 1.8 %collective-permute-done = f32[8,2,72,128]{3,2,1,0:T(8,128)S(1)} collective-permute-done((f32[8,2,72,128]{3,2,1,0:T(8,128)}, f32[8,2,72,128]{3,2,1,0:T(8,128)S(1)}, u32[]{:S(2)}, u32[]{:S(2)}) %collective-permute-start) | collective-permute-done | bytes 589856 | tf_op jit(solution)/shard_map/ppermute | solution.py:567
  7.5 1.2 %slice_add_fusion.8 = (f32[1,2,72,128]{3,2,1,0:T(8,128)S(1)}, f32[1,2,72,128]{3,2,1,0:T(8,128)S(1)}, f32[1,2,72,128]{3,2,1,0:T(8,128)S(1)}, f32[1,2,72,128]{3,2,...) fusion(f32[8,2,72,128]{3,2,1,0:T(8,128)S(1)} %collective-permut, ...), kind=kLoop, calls=%fused_computation.8 | loop fusion | flops 147456 | bytes 1769472 | tf_op jit(solution)/shard_map/add | solution.py:604
  8.7 5.0 %collective-permute-start.6 = (f32[1,144,128]{2,1,0:T(8,128)S(1)}, f32[1,144,128]{2,1,0:T(8,128)S(1)}, u32[]{:S(2)}, u32[]{:S(2)}) collective-permute-start(f32[1,144,128]{2,1,0:T(8,128)S(1)} %bitcast.97), channel_id=1, source_target_pairs={{0,12},{2,14},{4,8},{6,10},{8,4},{10,6},{12,0},{14,2},{1,13},{3,15... | collective-permute-start | bytes 221192 | tf_op jit(solution)/shard_map/ppermute | solution.py:595
  13.7 1.2 %collective-permute-start.7 = (f32[1,144,128]{2,1,0:T(8,128)S(1)}, f32[1,144,128]{2,1,0:T(8,128)S(1)}, u32[]{:S(2)}, u32[]{:S(2)}) collective-permute-start(f32[1,144,128]{2,1,0:T(8,128)S(1)} %bitcast.95), channel_id=1, source_target_pairs={{0,14},{2,12},{4,10},{6,8},{8,6},{10,4},{12,2},{14,0},{1,15},{3,13... | collective-permute-start | bytes 221192 | tf_op jit(solution)/shard_map/ppermute | solution.py:595
  14.9 0.8 collective-permute-start.5
  15.7 2.0 %collective-permute-start.4 = (f32[1,144,128]{2,1,0:T(8,128)S(1)}, f32[1,144,128]{2,1,0:T(8,128)S(1)}, u32[]{:S(2)}, u32[]{:S(2)}) collective-permute-start(f32[1,144,128]{2,1,0:T(8,128)S(1)} %bitcast.93), channel_id=1, source_target_pairs={{0,8},{2,10},{4,12},{6,14},{8,0},{10,2},{12,4},{14,6},{1,9},{3,11}... | collective-permute-start | bytes 221192 | tf_op jit(solution)/shard_map/ppermute | solution.py:595
  17.6 2.3 %collective-permute-start.3 = (f32[1,144,128]{2,1,0:T(8,128)S(1)}, f32[1,144,128]{2,1,0:T(8,128)S(1)}, u32[]{:S(2)}, u32[]{:S(2)}) collective-permute-start(f32[1,144,128]{2,1,0:T(8,128)S(1)} %bitcast.91), channel_id=1, source_target_pairs={{0,6},{2,4},{4,2},{6,0},{8,14},{10,12},{12,10},{14,8},{1,7},{3,5},... | collective-permute-start | bytes 221192 | tf_op jit(solution)/shard_map/ppermute | solution.py:595
  20.0 0.8 collective-permute-start.2
  20.8 0.7 collective-permute-done.7.refs_7_
  21.5 1.7 %collective-permute-start.1 = (f32[1,144,128]{2,1,0:T(8,128)S(1)}, f32[1,144,128]{2,1,0:T(8,128)S(1)}, u32[]{:S(2)}, u32[]{:S(2)}) collective-permute-start(f32[1,144,128]{2,1,0:T(8,128)S(1)} %bitcast.87), channel_id=1, source_target_pairs={{0,2},{2,0},{4,6},{6,4},{8,10},{10,8},{12,14},{14,12},{1,3},{3,1},... | collective-permute-start | bytes 221192 | tf_op jit(solution)/shard_map/ppermute | solution.py:595
  23.2 2.3 %copy-done.22 = f32[1,16,9,64,128]{4,3,2,1,0:T(8,128)S(1)} copy-done((f32[1,16,9,64,128]{4,3,2,1,0:T(8,128)S(1)}, f32[1,16,9,64,128]{4,3,2,1,0:T(8,128)}, u32[]{:S(2)}) %copy-start.22) | copy-done | bytes 4718616
  25.5 0.6 split.1
  27.0 2.5 %mix.1 = (f32[1,144,128]{2,1,0:T(8,128)S(1)}, f32[1,144,128]{2,1,0:T(8,128)}, f32[1,144,128]{2,1,0:T(8,128)}, f32[1,144,128]{2,1,0:T(8,128)S(1)}, f32[1,144,128]...) custom-call(f32[1,144,128]{2,1,0:T(8,128)S(1)} %bitcast.40, ...), custom_call_target="tpu_custom_call" | custom-call | flops 1000000000 | bytes 100000 | tf_op jit(solution)/shard_map/mix/pallas_call | solution.py:624
  29.5 3.4 %collective-permute-start.8 = (f32[1,144,128]{2,1,0:T(8,128)S(1)}, f32[1,144,128]{2,1,0:T(8,128)S(1)}, u32[]{:S(2)}, u32[]{:S(2)}) collective-permute-start(f32[1,144,128]{2,1,0:T(8,128)S(1)} %get-tuple-element.53), channel_id=1, source_target_pairs={{0,12},{2,14},{4,8},{6,10},{8,4},{10,6},{12,0},{14,2},{1,13},{3,15... | collective-permute-start | bytes 221192 | tf_op jit(solution)/shard_map/ppermute | solution.py:595
  32.9 1.1 collective-permute-start.9
  34.0 2.9 %collective-permute-start.10 = (f32[1,144,128]{2,1,0:T(8,128)S(1)}, f32[1,144,128]{2,1,0:T(8,128)S(1)}, u32[]{:S(2)}, u32[]{:S(2)}) collective-permute-start(f32[1,144,128]{2,1,0:T(8,128)S(1)} %get-tuple-element.55), channel_id=1, source_target_pairs={{0,10},{2,8},{4,14},{6,12},{8,2},{10,0},{12,6},{14,4},{1,11},{3,9}... | collective-permute-start | bytes 221192 | tf_op jit(solution)/shard_map/ppermute | solution.py:595
  37.1 1.6 %collective-permute-start.12 = (f32[1,144,128]{2,1,0:T(8,128)S(1)}, f32[1,144,128]{2,1,0:T(8,128)S(1)}, u32[]{:S(2)}, u32[]{:S(2)}) collective-permute-start(f32[1,144,128]{2,1,0:T(8,128)S(1)} %get-tuple-element.57), channel_id=1, source_target_pairs={{0,6},{2,4},{4,2},{6,0},{8,14},{10,12},{12,10},{14,8},{1,7},{3,5},... | collective-permute-start | bytes 221192 | tf_op jit(solution)/shard_map/ppermute | solution.py:595
  38.8 1.8 %collective-permute-start.13 = (f32[1,144,128]{2,1,0:T(8,128)}, f32[1,144,128]{2,1,0:T(8,128)S(1)}, u32[]{:S(2)}, u32[]{:S(2)}) collective-permute-start(f32[1,144,128]{2,1,0:T(8,128)} %get-tuple-element.58), channel_id=1, source_target_pairs={{0,4},{2,6},{4,0},{6,2},{8,12},{10,14},{12,8},{14,10},{1,5},{3,7},... | collective-permute-start | bytes 221192 | tf_op jit(solution)/shard_map/ppermute | solution.py:595
  40.8 1.9 %collective-permute-start.14 = (f32[1,144,128]{2,1,0:T(8,128)}, f32[1,144,128]{2,1,0:T(8,128)S(1)}, u32[]{:S(2)}, u32[]{:S(2)}) collective-permute-start(f32[1,144,128]{2,1,0:T(8,128)} %get-tuple-element.59), channel_id=1, source_target_pairs={{0,2},{2,0},{4,6},{6,4},{8,10},{10,8},{12,14},{14,12},{1,3},{3,1},... | collective-permute-start | bytes 221192 | tf_op jit(solution)/shard_map/ppermute | solution.py:595
  42.7 2.6 %collective-permute-done.10 = f32[1,144,128]{2,1,0:T(8,128)S(1)} collective-permute-done((f32[1,144,128]{2,1,0:T(8,128)S(1)}, f32[1,144,128]{2,1,0:T(8,128)S(1)}, u32[]{:S(2)}, u32[]{:S(2)}) %collective-permute-start.10) | collective-permute-done | bytes 73760 | tf_op jit(solution)/shard_map/ppermute | solution.py:595
  45.2 0.5 collective-permute-start.15
  45.9 0.5 collective-permute-start.17
  48.5 0.7 copy-done.20
  49.3 9.4 %middle.1 = (f32[8,2,72,128]{3,2,1,0:T(8,128)S(1)}, f32[8,2,72,128]{3,2,1,0:T(8,128)S(1)}, bf16[16,64,512]{2,1,0:T(8,128)(2,1)S(1)}, bf16[16,64,512]{2,1,0:T(8,128)(2,1)S(1)}) custom-call(s32[2]{0:T(128)S(1)} %pad_add_fusion.place, f32[2,72,128]{2,1,0:T(8,128)S(1)} %bitcast.53, f32[2,72,128]{2,1,0:T(8,128)S(1)} %bitcast.57, f32[2,72,128]{2,1,0:T(8,128)S(1)} %bitcast.61, ...), custom_call_target="tpu_custom_call" | custom-call | tf_op jit(solution)/shard_map/middle/pallas_call | solution.py:652
  58.9 1.8 %collective-permute-done.23 = f32[8,2,72,128]{3,2,1,0:T(8,128)S(1)} collective-permute-done((f32[8,2,72,128]{3,2,1,0:T(8,128)S(1)}, f32[8,2,72,128]{3,2,1,0:T(8,128)S(1)}, u32[]{:S(2)}, u32[]{:S(2)}) %collective-permute-start.23) | collective-permute-done | bytes 589856 | tf_op jit(solution)/shard_map/ppermute | solution.py:567
  60.8 2.6 %collective-permute-start.29 = (f32[1,144,128]{2,1,0:T(8,128)S(1)}, f32[1,144,128]{2,1,0:T(8,128)S(1)}, u32[]{:S(2)}, u32[]{:S(2)}) collective-permute-start(f32[1,144,128]{2,1,0:T(8,128)S(1)} %bitcast.98), channel_id=1, source_target_pairs={{0,12},{2,14},{4,8},{6,10},{8,4},{10,6},{12,0},{14,2},{1,13},{3,15... | collective-permute-start | bytes 221192 | tf_op jit(solution)/shard_map/ppermute | solution.py:595
  63.4 1.7 %collective-permute-start.30 = (f32[1,144,128]{2,1,0:T(8,128)S(1)}, f32[1,144,128]{2,1,0:T(8,128)S(1)}, u32[]{:S(2)}, u32[]{:S(2)}) collective-permute-start(f32[1,144,128]{2,1,0:T(8,128)S(1)} %bitcast.96), channel_id=1, source_target_pairs={{0,14},{2,12},{4,10},{6,8},{8,6},{10,4},{12,2},{14,0},{1,15},{3,13... | collective-permute-start | bytes 221192 | tf_op jit(solution)/shard_map/ppermute | solution.py:595
  65.1 2.4 %collective-permute-start.28 = (f32[1,144,128]{2,1,0:T(8,128)S(1)}, f32[1,144,128]{2,1,0:T(8,128)S(1)}, u32[]{:S(2)}, u32[]{:S(2)}) collective-permute-start(f32[1,144,128]{2,1,0:T(8,128)S(1)} %bitcast.92), channel_id=1, source_target_pairs={{0,10},{2,8},{4,14},{6,12},{8,2},{10,0},{12,6},{14,4},{1,11},{3,9}... | collective-permute-start | bytes 221192 | tf_op jit(solution)/shard_map/ppermute | solution.py:595
  67.5 1.0 collective-permute-start.27
  68.5 1.2 %collective-permute-start.26 = (f32[1,144,128]{2,1,0:T(8,128)S(1)}, f32[1,144,128]{2,1,0:T(8,128)S(1)}, u32[]{:S(2)}, u32[]{:S(2)}) collective-permute-start(f32[1,144,128]{2,1,0:T(8,128)S(1)} %bitcast.88), channel_id=1, source_target_pairs={{0,6},{2,4},{4,2},{6,0},{8,14},{10,12},{12,10},{14,8},{1,7},{3,5},... | collective-permute-start | bytes 221192 | tf_op jit(solution)/shard_map/ppermute | solution.py:595
  69.7 3.6 %collective-permute-start.25 = (f32[1,144,128]{2,1,0:T(8,128)S(1)}, f32[1,144,128]{2,1,0:T(8,128)S(1)}, u32[]{:S(2)}, u32[]{:S(2)}) collective-permute-start(f32[1,144,128]{2,1,0:T(8,128)S(1)} %bitcast.86), channel_id=1, source_target_pairs={{0,4},{2,6},{4,0},{6,2},{8,12},{10,14},{12,8},{14,10},{1,5},{3,7},... | collective-permute-start | bytes 221192 | tf_op jit(solution)/shard_map/ppermute | solution.py:595
  73.3 1.0 collective-permute-start.24
  74.4 2.0 %local.1 = (f32[16,64,512]{2,1,0:T(8,128)S(1)}, bf16[144,64,128]{2,1,0:T(8,128)(2,1)S(1)}, bf16[144,64,128]{2,1,0:T(8,128)(2,1)S(1)}) custom-call(bf16[16,64,512]{2,1,0:T(8,128)(2,1)S(1)} %get-tuple-element.64.slope_high, bf16[16,64,512]{2,1,0:T(8,128)(2,1)S(1)} %get-tuple-element.65.slope_low, f32[64,64]{1,0:T(8,128)S(1)} %copy-done.21, ...), custom_call_target="tpu_custom_call" | custom-call | flops 6000000000 | bytes 100000 | tf_op jit(solution)/shard_map/local/pallas_call | solution.py:670
  76.4 0.9 collective-permute-done.28.refs_5_.refs_13_
  77.3 1.1 %collective-permute-done.27.refs_4_.refs_12_ = f32[1,144,128]{2,1,0:T(8,128)S(1)} collective-permute-done((f32[1,144,128]{2,1,0:T(8,128)S(1)}, f32[1,144,128]{2,1,0:T(8,128)S(1)}, u32[]{:S(2)}, u32[]{:S(2)}) %collective-permute-start.27) | collective-permute-done | bytes 73760 | tf_op jit(solution)/shard_map/ppermute | solution.py:595
  78.8 3.2 %adjoint.1 = (f32[1,144,128]{2,1,0:T(8,128)S(1)}, f32[1,144,128]{2,1,0:T(8,128)S(1)}, f32[1,144,128]{2,1,0:T(8,128)S(1)}, f32[1,144,128]{2,1,0:T(8,128)S(1)}, f3...) custom-call(f32[1,144,128]{2,1,0:T(8,128)S(1)} %bitcast.42, ...), custom_call_target="tpu_custom_call" | custom-call | flops 1000000000 | bytes 100000 | tf_op jit(solution)/shard_map/adjoint/pallas_call | solution.py:624
  82.0 1.2 %collective-permute-start.31 = (f32[1,144,128]{2,1,0:T(8,128)S(1)}, f32[1,144,128]{2,1,0:T(8,128)S(1)}, u32[]{:S(2)}, u32[]{:S(2)}) collective-permute-start(f32[1,144,128]{2,1,0:T(8,128)S(1)} %get-tuple-element.69), channel_id=1, source_target_pairs={{0,2},{2,0},{4,6},{6,4},{8,10},{10,8},{12,14},{14,12},{1,3},{3,1},... | collective-permute-start | bytes 221192 | tf_op jit(solution)/shard_map/ppermute | solution.py:595
  83.3 1.8 %collective-permute-start.32 = (f32[1,144,128]{2,1,0:T(8,128)S(1)}, f32[1,144,128]{2,1,0:T(8,128)S(1)}, u32[]{:S(2)}, u32[]{:S(2)}) collective-permute-start(f32[1,144,128]{2,1,0:T(8,128)S(1)} %get-tuple-element.70), channel_id=1, source_target_pairs={{0,4},{2,6},{4,0},{6,2},{8,12},{10,14},{12,8},{14,10},{1,5},{3,7},... | collective-permute-start | bytes 221192 | tf_op jit(solution)/shard_map/ppermute | solution.py:595
  85.0 2.6 %collective-permute-start.33 = (f32[1,144,128]{2,1,0:T(8,128)S(1)}, f32[1,144,128]{2,1,0:T(8,128)S(1)}, u32[]{:S(2)}, u32[]{:S(2)}) collective-permute-start(f32[1,144,128]{2,1,0:T(8,128)S(1)} %get-tuple-element.71), channel_id=1, source_target_pairs={{0,12},{2,14},{4,8},{6,10},{8,4},{10,6},{12,0},{14,2},{1,13},{3,15... | collective-permute-start | bytes 221192 | tf_op jit(solution)/shard_map/ppermute | solution.py:595
  87.6 1.9 %collective-permute-start.34 = (f32[1,144,128]{2,1,0:T(8,128)S(1)}, f32[1,144,128]{2,1,0:T(8,128)S(1)}, u32[]{:S(2)}, u32[]{:S(2)}) collective-permute-start(f32[1,144,128]{2,1,0:T(8,128)S(1)} %get-tuple-element.72), channel_id=1, source_target_pairs={{0,14},{2,12},{4,10},{6,8},{8,6},{10,4},{12,2},{14,0},{1,15},{3,13... | collective-permute-start | bytes 221192 | tf_op jit(solution)/shard_map/ppermute | solution.py:595
  89.5 3.2 %collective-permute-start.36 = (f32[1,144,128]{2,1,0:T(8,128)S(1)}, f32[1,144,128]{2,1,0:T(8,128)S(1)}, u32[]{:S(2)}, u32[]{:S(2)}) collective-permute-start(f32[1,144,128]{2,1,0:T(8,128)S(1)} %get-tuple-element.74), channel_id=1, source_target_pairs={{0,8},{2,10},{4,12},{6,14},{8,0},{10,2},{12,4},{14,6},{1,9},{3,11}... | collective-permute-start | bytes 221192 | tf_op jit(solution)/shard_map/ppermute | solution.py:595
  92.7 0.5 collective-permute-start.37
  93.3 7.6 %adam.1 = (f32[144,64,128]{2,1,0:T(8,128)}, f32[144,64,128]{2,1,0:T(8,128)}, f32[144,64,128]{2,1,0:T(8,128)}) custom-call(f32[1,144,128]{2,1,0:T(8,128)S(1)} %bitcast.41, f32[1,144,128]{2,1,0:T(8,128)S(1)} %copy-done.19, f32[1,144,128]{2,1,0:T(8,128)S(1)} %copy-done.17, f32[1,144,128]{2,1,0:T(8,128)S(1)} %copy-done.15, f32[1,144,128]{2,1,0:T(8,128)S(1)} %copy-done.13, ...), custom_call_target="tpu_custom_call" | custom-call | flops 10000000000 | bytes 30000000 | tf_op jit(solution)/shard_map/adam/pallas_call | solution.py:683
  101.1 0.5 collective-permute-start.38
  101.7 0.4 collective-permute-start.41
  104.1 4.2 %last.1 = bf16[1,16,64,512]{3,2,1,0:T(8,128)(2,1)} custom-call(s32[2]{0:T(128)S(1)} %pad_add_fusion.place, f32[2,72,128]{2,1,0:T(8,128)S(1)} %bitcast.49, f32[2,72,128]{2,1,0:T(8,128)S(1)} %bitcast.51, f32[2,72,128]{2,1,0:T(8,128)S(1)} %bitcast.55, f32[2,72,128]{2,1,0:T(8,128)S(1)} %bitcast.59, f32[2,72,128]{2,1,0:T(8,128)S(1)} %bitcast.63, ...), custom_call_target="tpu_custom_call" | custom-call | tf_op jit(solution)/shard_map/last/pallas_call | solution.py:696
  (113 shorter events, 6.4 us)
Async XLA Ops:
  5.1 2.4 %collective-permute-start = (f32[8,2,72,128]{3,2,1,0:T(8,128)}, f32[8,2,72,128]{3,2,1,0:T(8,128)S(1)}, u32[]{:S(2)}, u32[]{:S(2)}) collective-permute-start(f32[8,2,72,128]{3,2,1,0:T(8,128)} %get-tuple-element.50), channel_id=1, source_target_pairs={{0,1},{1,0},{2,3},{3,2},{4,5},{5,4},{6,7},{7,6},{8,9},{9,8},{10,11... | collective-permute-start | bytes 1769480 | tf_op jit(solution)/shard_map/ppermute | solution.py:567
  8.7 11.2 %collective-permute-start.6 = (f32[1,144,128]{2,1,0:T(8,128)S(1)}, f32[1,144,128]{2,1,0:T(8,128)S(1)}, u32[]{:S(2)}, u32[]{:S(2)}) collective-permute-start(f32[1,144,128]{2,1,0:T(8,128)S(1)} %bitcast.97), channel_id=1, source_target_pairs={{0,12},{2,14},{4,8},{6,10},{8,4},{10,6},{12,0},{14,2},{1,13},{3,15... | collective-permute-start | bytes 221192 | tf_op jit(solution)/shard_map/ppermute | solution.py:595
  13.7 7.7 %collective-permute-start.7 = (f32[1,144,128]{2,1,0:T(8,128)S(1)}, f32[1,144,128]{2,1,0:T(8,128)S(1)}, u32[]{:S(2)}, u32[]{:S(2)}) collective-permute-start(f32[1,144,128]{2,1,0:T(8,128)S(1)} %bitcast.95), channel_id=1, source_target_pairs={{0,14},{2,12},{4,10},{6,8},{8,6},{10,4},{12,2},{14,0},{1,15},{3,13... | collective-permute-start | bytes 221192 | tf_op jit(solution)/shard_map/ppermute | solution.py:595
  14.9 11.6 %collective-permute-start.5 = (f32[1,144,128]{2,1,0:T(8,128)S(1)}, f32[1,144,128]{2,1,0:T(8,128)S(1)}, u32[]{:S(2)}, u32[]{:S(2)}) collective-permute-start(f32[1,144,128]{2,1,0:T(8,128)S(1)} %bitcast.94), channel_id=1, source_target_pairs={{0,10},{2,8},{4,14},{6,12},{8,2},{10,0},{12,6},{14,4},{1,11},{3,9}... | collective-permute-start | bytes 221192 | tf_op jit(solution)/shard_map/ppermute | solution.py:595
  15.7 11.0 %collective-permute-start.4 = (f32[1,144,128]{2,1,0:T(8,128)S(1)}, f32[1,144,128]{2,1,0:T(8,128)S(1)}, u32[]{:S(2)}, u32[]{:S(2)}) collective-permute-start(f32[1,144,128]{2,1,0:T(8,128)S(1)} %bitcast.93), channel_id=1, source_target_pairs={{0,8},{2,10},{4,12},{6,14},{8,0},{10,2},{12,4},{14,6},{1,9},{3,11}... | collective-permute-start | bytes 221192 | tf_op jit(solution)/shard_map/ppermute | solution.py:595
  17.6 9.0 %collective-permute-start.3 = (f32[1,144,128]{2,1,0:T(8,128)S(1)}, f32[1,144,128]{2,1,0:T(8,128)S(1)}, u32[]{:S(2)}, u32[]{:S(2)}) collective-permute-start(f32[1,144,128]{2,1,0:T(8,128)S(1)} %bitcast.91), channel_id=1, source_target_pairs={{0,6},{2,4},{4,2},{6,0},{8,14},{10,12},{12,10},{14,8},{1,7},{3,5},... | collective-permute-start | bytes 221192 | tf_op jit(solution)/shard_map/ppermute | solution.py:595
  20.0 7.0 %collective-permute-start.2 = (f32[1,144,128]{2,1,0:T(8,128)S(1)}, f32[1,144,128]{2,1,0:T(8,128)S(1)}, u32[]{:S(2)}, u32[]{:S(2)}) collective-permute-start(f32[1,144,128]{2,1,0:T(8,128)S(1)} %bitcast.89), channel_id=1, source_target_pairs={{0,4},{2,6},{4,0},{6,2},{8,12},{10,14},{12,8},{14,10},{1,5},{3,7},... | collective-permute-start | bytes 221192 | tf_op jit(solution)/shard_map/ppermute | solution.py:595
  21.5 5.5 %collective-permute-start.1 = (f32[1,144,128]{2,1,0:T(8,128)S(1)}, f32[1,144,128]{2,1,0:T(8,128)S(1)}, u32[]{:S(2)}, u32[]{:S(2)}) collective-permute-start(f32[1,144,128]{2,1,0:T(8,128)S(1)} %bitcast.87), channel_id=1, source_target_pairs={{0,2},{2,0},{4,6},{6,4},{8,10},{10,8},{12,14},{14,12},{1,3},{3,1},... | collective-permute-start | bytes 221192 | tf_op jit(solution)/shard_map/ppermute | solution.py:595
  29.5 9.3 %collective-permute-start.8 = (f32[1,144,128]{2,1,0:T(8,128)S(1)}, f32[1,144,128]{2,1,0:T(8,128)S(1)}, u32[]{:S(2)}, u32[]{:S(2)}) collective-permute-start(f32[1,144,128]{2,1,0:T(8,128)S(1)} %get-tuple-element.53), channel_id=1, source_target_pairs={{0,12},{2,14},{4,8},{6,10},{8,4},{10,6},{12,0},{14,2},{1,13},{3,15... | collective-permute-start | bytes 221192 | tf_op jit(solution)/shard_map/ppermute | solution.py:595
  32.9 7.9 %collective-permute-start.9 = (f32[1,144,128]{2,1,0:T(8,128)S(1)}, f32[1,144,128]{2,1,0:T(8,128)S(1)}, u32[]{:S(2)}, u32[]{:S(2)}) collective-permute-start(f32[1,144,128]{2,1,0:T(8,128)S(1)} %get-tuple-element.54), channel_id=1, source_target_pairs={{0,14},{2,12},{4,10},{6,8},{8,6},{10,4},{12,2},{14,0},{1,15},{3,13... | collective-permute-start | bytes 221192 | tf_op jit(solution)/shard_map/ppermute | solution.py:595
  34.0 11.3 %collective-permute-start.10 = (f32[1,144,128]{2,1,0:T(8,128)S(1)}, f32[1,144,128]{2,1,0:T(8,128)S(1)}, u32[]{:S(2)}, u32[]{:S(2)}) collective-permute-start(f32[1,144,128]{2,1,0:T(8,128)S(1)} %get-tuple-element.55), channel_id=1, source_target_pairs={{0,10},{2,8},{4,14},{6,12},{8,2},{10,0},{12,6},{14,4},{1,11},{3,9}... | collective-permute-start | bytes 221192 | tf_op jit(solution)/shard_map/ppermute | solution.py:595
  36.9 8.4 %collective-permute-start.11 = (f32[1,144,128]{2,1,0:T(8,128)S(1)}, f32[1,144,128]{2,1,0:T(8,128)S(1)}, u32[]{:S(2)}, u32[]{:S(2)}) collective-permute-start(f32[1,144,128]{2,1,0:T(8,128)S(1)} %get-tuple-element.56), channel_id=1, source_target_pairs={{0,8},{2,10},{4,12},{6,14},{8,0},{10,2},{12,4},{14,6},{1,9},{3,11}... | collective-permute-start | bytes 221192 | tf_op jit(solution)/shard_map/ppermute | solution.py:595
  37.1 8.6 %collective-permute-start.12 = (f32[1,144,128]{2,1,0:T(8,128)S(1)}, f32[1,144,128]{2,1,0:T(8,128)S(1)}, u32[]{:S(2)}, u32[]{:S(2)}) collective-permute-start(f32[1,144,128]{2,1,0:T(8,128)S(1)} %get-tuple-element.57), channel_id=1, source_target_pairs={{0,6},{2,4},{4,2},{6,0},{8,14},{10,12},{12,10},{14,8},{1,7},{3,5},... | collective-permute-start | bytes 221192 | tf_op jit(solution)/shard_map/ppermute | solution.py:595
  38.8 7.1 %collective-permute-start.13 = (f32[1,144,128]{2,1,0:T(8,128)}, f32[1,144,128]{2,1,0:T(8,128)S(1)}, u32[]{:S(2)}, u32[]{:S(2)}) collective-permute-start(f32[1,144,128]{2,1,0:T(8,128)} %get-tuple-element.58), channel_id=1, source_target_pairs={{0,4},{2,6},{4,0},{6,2},{8,12},{10,14},{12,8},{14,10},{1,5},{3,7},... | collective-permute-start | bytes 221192 | tf_op jit(solution)/shard_map/ppermute | solution.py:595
  40.8 5.6 %collective-permute-start.14 = (f32[1,144,128]{2,1,0:T(8,128)}, f32[1,144,128]{2,1,0:T(8,128)S(1)}, u32[]{:S(2)}, u32[]{:S(2)}) collective-permute-start(f32[1,144,128]{2,1,0:T(8,128)} %get-tuple-element.59), channel_id=1, source_target_pairs={{0,2},{2,0},{4,6},{6,4},{8,10},{10,8},{12,14},{14,12},{1,3},{3,1},... | collective-permute-start | bytes 221192 | tf_op jit(solution)/shard_map/ppermute | solution.py:595
  45.2 1.3 %collective-permute-start.22 = (f32[2,72,128]{2,1,0:T(8,128)S(1)}, f32[2,72,128]{2,1,0:T(8,128)S(1)}, u32[]{:S(2)}, u32[]{:S(2)}) collective-permute-start(f32[2,72,128]{2,1,0:T(8,128)S(1)} %bitcast.46), channel_id=1, source_target_pairs={{0,1},{1,0},{2,3},{3,2},{4,5},{5,4},{6,7},{7,6},{8,9},{9,8},{10,11... | collective-permute-start | bytes 221192 | tf_op jit(solution)/shard_map/ppermute | solution.py:567
  45.2 1.7 %collective-permute-start.15 = (f32[2,72,128]{2,1,0:T(8,128)S(1)}, f32[2,72,128]{2,1,0:T(8,128)S(1)}, u32[]{:S(2)}, u32[]{:S(2)}) collective-permute-start(f32[2,72,128]{2,1,0:T(8,128)S(1)} %bitcast.52), channel_id=1, source_target_pairs={{0,1},{1,0},{2,3},{3,2},{4,5},{5,4},{6,7},{7,6},{8,9},{9,8},{10,11... | collective-permute-start | bytes 221192 | tf_op jit(solution)/shard_map/ppermute | solution.py:567
  45.8 1.5 %collective-permute-start.16 = (f32[2,72,128]{2,1,0:T(8,128)S(1)}, f32[2,72,128]{2,1,0:T(8,128)}, u32[]{:S(2)}, u32[]{:S(2)}) collective-permute-start(f32[2,72,128]{2,1,0:T(8,128)S(1)} %bitcast.56), channel_id=1, source_target_pairs={{0,1},{1,0},{2,3},{3,2},{4,5},{5,4},{6,7},{7,6},{8,9},{9,8},{10,11... | collective-permute-start | bytes 221192 | tf_op jit(solution)/shard_map/ppermute | solution.py:567
  45.9 1.6 %collective-permute-start.17 = (f32[2,72,128]{2,1,0:T(8,128)S(1)}, f32[2,72,128]{2,1,0:T(8,128)S(1)}, u32[]{:S(2)}, u32[]{:S(2)}) collective-permute-start(f32[2,72,128]{2,1,0:T(8,128)S(1)} %bitcast.60), channel_id=1, source_target_pairs={{0,1},{1,0},{2,3},{3,2},{4,5},{5,4},{6,7},{7,6},{8,9},{9,8},{10,11... | collective-permute-start | bytes 221192 | tf_op jit(solution)/shard_map/ppermute | solution.py:567
  46.4 1.3 %collective-permute-start.18 = (f32[2,72,128]{2,1,0:T(8,128)S(1)}, f32[2,72,128]{2,1,0:T(8,128)S(1)}, u32[]{:S(2)}, u32[]{:S(2)}) collective-permute-start(f32[2,72,128]{2,1,0:T(8,128)S(1)} %bitcast.64), channel_id=1, source_target_pairs={{0,1},{1,0},{2,3},{3,2},{4,5},{5,4},{6,7},{7,6},{8,9},{9,8},{10,11... | collective-permute-start | bytes 221192 | tf_op jit(solution)/shard_map/ppermute | solution.py:567
  46.5 1.3 %collective-permute-start.19 = (f32[2,72,128]{2,1,0:T(8,128)S(1)}, f32[2,72,128]{2,1,0:T(8,128)S(1)}, u32[]{:S(2)}, u32[]{:S(2)}) collective-permute-start(f32[2,72,128]{2,1,0:T(8,128)S(1)} %bitcast.66), channel_id=1, source_target_pairs={{0,1},{1,0},{2,3},{3,2},{4,5},{5,4},{6,7},{7,6},{8,9},{9,8},{10,11... | collective-permute-start | bytes 221192 | tf_op jit(solution)/shard_map/ppermute | solution.py:567
  46.9 1.3 %collective-permute-start.20 = (f32[2,72,128]{2,1,0:T(8,128)S(1)}, f32[2,72,128]{2,1,0:T(8,128)S(1)}, u32[]{:S(2)}, u32[]{:S(2)}) collective-permute-start(f32[2,72,128]{2,1,0:T(8,128)S(1)} %bitcast.70), channel_id=1, source_target_pairs={{0,1},{1,0},{2,3},{3,2},{4,5},{5,4},{6,7},{7,6},{8,9},{9,8},{10,11... | collective-permute-start | bytes 221192 | tf_op jit(solution)/shard_map/ppermute | solution.py:567
  47.2 1.3 %collective-permute-start.21 = (f32[2,72,128]{2,1,0:T(8,128)S(1)}, f32[2,72,128]{2,1,0:T(8,128)S(1)}, u32[]{:S(2)}, u32[]{:S(2)}) collective-permute-start(f32[2,72,128]{2,1,0:T(8,128)S(1)} %bitcast.74), channel_id=1, source_target_pairs={{0,1},{1,0},{2,3},{3,2},{4,5},{5,4},{6,7},{7,6},{8,9},{9,8},{10,11... | collective-permute-start | bytes 221192 | tf_op jit(solution)/shard_map/ppermute | solution.py:567
  49.3 25.1 %copy-start.21 = (f32[64,64]{1,0:T(8,128)S(1)}, f32[64,64]{1,0:T(8,128)}, u32[]{:S(2)}) copy-start(f32[64,64]{1,0:T(8,128)} %pointwise.1) | copy-start | bytes 49156
  49.3 25.1 %copy-start.23 = (f32[1,16,9,64,128]{4,3,2,1,0:T(8,128)S(1)}, f32[1,16,9,64,128]{4,3,2,1,0:T(8,128)}, u32[]{:S(2)}) copy-start(f32[1,16,9,64,128]{4,3,2,1,0:T(8,128)} %param.12) | copy-start | bytes 14155780
  58.6 2.1 %collective-permute-start.23 = (f32[8,2,72,128]{3,2,1,0:T(8,128)S(1)}, f32[8,2,72,128]{3,2,1,0:T(8,128)S(1)}, u32[]{:S(2)}, u32[]{:S(2)}) collective-permute-start(f32[8,2,72,128]{3,2,1,0:T(8,128)S(1)} %get-tuple-element.63), channel_id=1, source_target_pairs={{0,1},{1,0},{2,3},{3,2},{4,5},{5,4},{6,7},{7,6},{8,9},{9,8},{10,11... | collective-permute-start | bytes 1769480 | tf_op jit(solution)/shard_map/ppermute | solution.py:567
  60.8 8.9 %collective-permute-start.29 = (f32[1,144,128]{2,1,0:T(8,128)S(1)}, f32[1,144,128]{2,1,0:T(8,128)S(1)}, u32[]{:S(2)}, u32[]{:S(2)}) collective-permute-start(f32[1,144,128]{2,1,0:T(8,128)S(1)} %bitcast.98), channel_id=1, source_target_pairs={{0,12},{2,14},{4,8},{6,10},{8,4},{10,6},{12,0},{14,2},{1,13},{3,15... | collective-permute-start | bytes 221192 | tf_op jit(solution)/shard_map/ppermute | solution.py:595
  63.4 10.0 %collective-permute-start.30 = (f32[1,144,128]{2,1,0:T(8,128)S(1)}, f32[1,144,128]{2,1,0:T(8,128)S(1)}, u32[]{:S(2)}, u32[]{:S(2)}) collective-permute-start(f32[1,144,128]{2,1,0:T(8,128)S(1)} %bitcast.96), channel_id=1, source_target_pairs={{0,14},{2,12},{4,10},{6,8},{8,6},{10,4},{12,2},{14,0},{1,15},{3,13... | collective-permute-start | bytes 221192 | tf_op jit(solution)/shard_map/ppermute | solution.py:595
  65.1 12.2 %collective-permute-start.28 = (f32[1,144,128]{2,1,0:T(8,128)S(1)}, f32[1,144,128]{2,1,0:T(8,128)S(1)}, u32[]{:S(2)}, u32[]{:S(2)}) collective-permute-start(f32[1,144,128]{2,1,0:T(8,128)S(1)} %bitcast.92), channel_id=1, source_target_pairs={{0,10},{2,8},{4,14},{6,12},{8,2},{10,0},{12,6},{14,4},{1,11},{3,9}... | collective-permute-start | bytes 221192 | tf_op jit(solution)/shard_map/ppermute | solution.py:595
  67.5 10.9 %collective-permute-start.27 = (f32[1,144,128]{2,1,0:T(8,128)S(1)}, f32[1,144,128]{2,1,0:T(8,128)S(1)}, u32[]{:S(2)}, u32[]{:S(2)}) collective-permute-start(f32[1,144,128]{2,1,0:T(8,128)S(1)} %bitcast.90), channel_id=1, source_target_pairs={{0,8},{2,10},{4,12},{6,14},{8,0},{10,2},{12,4},{14,6},{1,9},{3,11}... | collective-permute-start | bytes 221192 | tf_op jit(solution)/shard_map/ppermute | solution.py:595
  68.5 9.9 %collective-permute-start.26 = (f32[1,144,128]{2,1,0:T(8,128)S(1)}, f32[1,144,128]{2,1,0:T(8,128)S(1)}, u32[]{:S(2)}, u32[]{:S(2)}) collective-permute-start(f32[1,144,128]{2,1,0:T(8,128)S(1)} %bitcast.88), channel_id=1, source_target_pairs={{0,6},{2,4},{4,2},{6,0},{8,14},{10,12},{12,10},{14,8},{1,7},{3,5},... | collective-permute-start | bytes 221192 | tf_op jit(solution)/shard_map/ppermute | solution.py:595
  69.7 9.1 %collective-permute-start.25 = (f32[1,144,128]{2,1,0:T(8,128)S(1)}, f32[1,144,128]{2,1,0:T(8,128)S(1)}, u32[]{:S(2)}, u32[]{:S(2)}) collective-permute-start(f32[1,144,128]{2,1,0:T(8,128)S(1)} %bitcast.86), channel_id=1, source_target_pairs={{0,4},{2,6},{4,0},{6,2},{8,12},{10,14},{12,8},{14,10},{1,5},{3,7},... | collective-permute-start | bytes 221192 | tf_op jit(solution)/shard_map/ppermute | solution.py:595
  73.3 5.5 %collective-permute-start.24 = (f32[1,144,128]{2,1,0:T(8,128)S(1)}, f32[1,144,128]{2,1,0:T(8,128)S(1)}, u32[]{:S(2)}, u32[]{:S(2)}) collective-permute-start(f32[1,144,128]{2,1,0:T(8,128)S(1)} %bitcast.85), channel_id=1, source_target_pairs={{0,2},{2,0},{4,6},{6,4},{8,10},{10,8},{12,14},{14,12},{1,3},{3,1},... | collective-permute-start | bytes 221192 | tf_op jit(solution)/shard_map/ppermute | solution.py:595
  82.0 7.4 %collective-permute-start.31 = (f32[1,144,128]{2,1,0:T(8,128)S(1)}, f32[1,144,128]{2,1,0:T(8,128)S(1)}, u32[]{:S(2)}, u32[]{:S(2)}) collective-permute-start(f32[1,144,128]{2,1,0:T(8,128)S(1)} %get-tuple-element.69), channel_id=1, source_target_pairs={{0,2},{2,0},{4,6},{6,4},{8,10},{10,8},{12,14},{14,12},{1,3},{3,1},... | collective-permute-start | bytes 221192 | tf_op jit(solution)/shard_map/ppermute | solution.py:595
  83.3 9.4 %collective-permute-start.32 = (f32[1,144,128]{2,1,0:T(8,128)S(1)}, f32[1,144,128]{2,1,0:T(8,128)S(1)}, u32[]{:S(2)}, u32[]{:S(2)}) collective-permute-start(f32[1,144,128]{2,1,0:T(8,128)S(1)} %get-tuple-element.70), channel_id=1, source_target_pairs={{0,4},{2,6},{4,0},{6,2},{8,12},{10,14},{12,8},{14,10},{1,5},{3,7},... | collective-permute-start | bytes 221192 | tf_op jit(solution)/shard_map/ppermute | solution.py:595
  85.0 15.9 %collective-permute-start.33 = (f32[1,144,128]{2,1,0:T(8,128)S(1)}, f32[1,144,128]{2,1,0:T(8,128)S(1)}, u32[]{:S(2)}, u32[]{:S(2)}) collective-permute-start(f32[1,144,128]{2,1,0:T(8,128)S(1)} %get-tuple-element.71), channel_id=1, source_target_pairs={{0,12},{2,14},{4,8},{6,10},{8,4},{10,6},{12,0},{14,2},{1,13},{3,15... | collective-permute-start | bytes 221192 | tf_op jit(solution)/shard_map/ppermute | solution.py:595
  87.6 13.4 %collective-permute-start.34 = (f32[1,144,128]{2,1,0:T(8,128)S(1)}, f32[1,144,128]{2,1,0:T(8,128)S(1)}, u32[]{:S(2)}, u32[]{:S(2)}) collective-permute-start(f32[1,144,128]{2,1,0:T(8,128)S(1)} %get-tuple-element.72), channel_id=1, source_target_pairs={{0,14},{2,12},{4,10},{6,8},{8,6},{10,4},{12,2},{14,0},{1,15},{3,13... | collective-permute-start | bytes 221192 | tf_op jit(solution)/shard_map/ppermute | solution.py:595
  89.4 11.5 %collective-permute-start.35 = (f32[1,144,128]{2,1,0:T(8,128)S(1)}, f32[1,144,128]{2,1,0:T(8,128)S(1)}, u32[]{:S(2)}, u32[]{:S(2)}) collective-permute-start(f32[1,144,128]{2,1,0:T(8,128)S(1)} %get-tuple-element.73), channel_id=1, source_target_pairs={{0,10},{2,8},{4,14},{6,12},{8,2},{10,0},{12,6},{14,4},{1,11},{3,9}... | collective-permute-start | bytes 221192 | tf_op jit(solution)/shard_map/ppermute | solution.py:595
  89.5 11.5 %collective-permute-start.36 = (f32[1,144,128]{2,1,0:T(8,128)S(1)}, f32[1,144,128]{2,1,0:T(8,128)S(1)}, u32[]{:S(2)}, u32[]{:S(2)}) collective-permute-start(f32[1,144,128]{2,1,0:T(8,128)S(1)} %get-tuple-element.74), channel_id=1, source_target_pairs={{0,8},{2,10},{4,12},{6,14},{8,0},{10,2},{12,4},{14,6},{1,9},{3,11}... | collective-permute-start | bytes 221192 | tf_op jit(solution)/shard_map/ppermute | solution.py:595
  92.7 8.3 %collective-permute-start.37 = (f32[1,144,128]{2,1,0:T(8,128)S(1)}, f32[1,144,128]{2,1,0:T(8,128)S(1)}, u32[]{:S(2)}, u32[]{:S(2)}) collective-permute-start(f32[1,144,128]{2,1,0:T(8,128)S(1)} %get-tuple-element.75), channel_id=1, source_target_pairs={{0,6},{2,4},{4,2},{6,0},{8,14},{10,12},{12,10},{14,8},{1,7},{3,5},... | collective-permute-start | bytes 221192 | tf_op jit(solution)/shard_map/ppermute | solution.py:595
  101.0 1.3 %collective-permute-start.39 = (f32[2,72,128]{2,1,0:T(8,128)S(1)}, f32[2,72,128]{2,1,0:T(8,128)S(1)}, u32[]{:S(2)}, u32[]{:S(2)}) collective-permute-start(f32[2,72,128]{2,1,0:T(8,128)S(1)} %bitcast.50), channel_id=1, source_target_pairs={{0,1},{1,0},{2,3},{3,2},{4,5},{5,4},{6,7},{7,6},{8,9},{9,8},{10,11... | collective-permute-start | bytes 221192 | tf_op jit(solution)/shard_map/ppermute | solution.py:567
  101.1 1.5 %collective-permute-start.38 = (f32[2,72,128]{2,1,0:T(8,128)S(1)}, f32[2,72,128]{2,1,0:T(8,128)S(1)}, u32[]{:S(2)}, u32[]{:S(2)}) collective-permute-start(f32[2,72,128]{2,1,0:T(8,128)S(1)} %bitcast.48), channel_id=1, source_target_pairs={{0,1},{1,0},{2,3},{3,2},{4,5},{5,4},{6,7},{7,6},{8,9},{9,8},{10,11... | collective-permute-start | bytes 221192 | tf_op jit(solution)/shard_map/ppermute | solution.py:567
  101.6 1.3 %collective-permute-start.40 = (f32[2,72,128]{2,1,0:T(8,128)S(1)}, f32[2,72,128]{2,1,0:T(8,128)S(1)}, u32[]{:S(2)}, u32[]{:S(2)}) collective-permute-start(f32[2,72,128]{2,1,0:T(8,128)S(1)} %bitcast.54), channel_id=1, source_target_pairs={{0,1},{1,0},{2,3},{3,2},{4,5},{5,4},{6,7},{7,6},{8,9},{9,8},{10,11... | collective-permute-start | bytes 221192 | tf_op jit(solution)/shard_map/ppermute | solution.py:567
  101.7 1.5 %collective-permute-start.41 = (f32[2,72,128]{2,1,0:T(8,128)S(1)}, f32[2,72,128]{2,1,0:T(8,128)S(1)}, u32[]{:S(2)}, u32[]{:S(2)}) collective-permute-start(f32[2,72,128]{2,1,0:T(8,128)S(1)} %bitcast.58), channel_id=1, source_target_pairs={{0,1},{1,0},{2,3},{3,2},{4,5},{5,4},{6,7},{7,6},{8,9},{9,8},{10,11... | collective-permute-start | bytes 221192 | tf_op jit(solution)/shard_map/ppermute | solution.py:567
  102.1 1.3 %collective-permute-start.42 = (f32[2,72,128]{2,1,0:T(8,128)S(1)}, f32[2,72,128]{2,1,0:T(8,128)S(1)}, u32[]{:S(2)}, u32[]{:S(2)}) collective-permute-start(f32[2,72,128]{2,1,0:T(8,128)S(1)} %bitcast.62), channel_id=1, source_target_pairs={{0,1},{1,0},{2,3},{3,2},{4,5},{5,4},{6,7},{7,6},{8,9},{9,8},{10,11... | collective-permute-start | bytes 221192 | tf_op jit(solution)/shard_map/ppermute | solution.py:567
  102.3 1.3 %collective-permute-start.43 = (f32[2,72,128]{2,1,0:T(8,128)S(1)}, f32[2,72,128]{2,1,0:T(8,128)S(1)}, u32[]{:S(2)}, u32[]{:S(2)}) collective-permute-start(f32[2,72,128]{2,1,0:T(8,128)S(1)} %bitcast.68), channel_id=1, source_target_pairs={{0,1},{1,0},{2,3},{3,2},{4,5},{5,4},{6,7},{7,6},{8,9},{9,8},{10,11... | collective-permute-start | bytes 221192 | tf_op jit(solution)/shard_map/ppermute | solution.py:567
  102.6 1.3 %collective-permute-start.44 = (f32[2,72,128]{2,1,0:T(8,128)S(1)}, f32[2,72,128]{2,1,0:T(8,128)S(1)}, u32[]{:S(2)}, u32[]{:S(2)}) collective-permute-start(f32[2,72,128]{2,1,0:T(8,128)S(1)} %bitcast.72), channel_id=1, source_target_pairs={{0,1},{1,0},{2,3},{3,2},{4,5},{5,4},{6,7},{7,6},{8,9},{9,8},{10,11... | collective-permute-start | bytes 221192 | tf_op jit(solution)/shard_map/ppermute | solution.py:567
  102.8 1.3 %collective-permute-start.45 = (f32[2,72,128]{2,1,0:T(8,128)S(1)}, f32[2,72,128]{2,1,0:T(8,128)S(1)}, u32[]{:S(2)}, u32[]{:S(2)}) collective-permute-start(f32[2,72,128]{2,1,0:T(8,128)S(1)} %bitcast.44), channel_id=1, source_target_pairs={{0,1},{1,0},{2,3},{3,2},{4,5},{5,4},{6,7},{7,6},{8,9},{9,8},{10,11... | collective-permute-start | bytes 221192 | tf_op jit(solution)/shard_map/ppermute | solution.py:567
  (26 other events, 415.1 us)
